TPU v7x, 256 devices: a whole 4x4x8 slice. The times are simulated.
256 devices in a mesh: row: 32 (over y, x, core), col: 8 (over z).
Axes of the slice: x: 4, y: 4, z: 8, core: 2. Of those that a mesh axis runs over, the one named last changes fastest.
Arguments:
- check_field: bfloat16 [2, 152, 131072], P(None, None, ('row', 'col')), may hold values from -6 to 6
- to_equiv: bfloat16 [2, 152, 152], replicated, may hold values from -0.3125 to 0.3125
- upward_ops: bfloat16 [4, 8, 2, 152, 152], replicated, may hold values from -0.125 to 0.125
- downward_ops: bfloat16 [4, 8, 2, 152, 152], replicated, may hold values from -0.3125 to 0.3125
- transfer_ops: bfloat16 [4, 16, 2, 152, 152], replicated, may hold values from -0.078125 to 0.078125
- list_fine: int32 [131072, 16], P(('row', 'col')), may hold values from 0 to 131071, as said below
- list_mid: int32 [16384, 16], P(('row', 'col')), may hold values from 0 to 16383, as said below
- list_low: int32 [2048, 16], P(('row', 'col')), may hold values from 0 to 2047, as said below
- list_top: int32 [32, 16], replicated, may hold values from 0 to 31, as said below
Outputs:
- far_field: float32 [2, 152, 131072], P(None, None, ('row', 'col'))
Inputs may be any that keep to these rules, and one draw needn't show every extreme that they name: `list_fine`: each source lies within 256 of its target box index. `list_mid`: each source lies within 32 of its target box index. `list_low`: each source lies within 4 of its target box index. `list_top`: no box lists itself.
All inputs are finite; a program needn't handle non-finite values.
Results may differ from a plain program's by a relative error of at most 0.014.
Values may be sent and summed in bfloat16 or wider, within the bound.
No kernel may reach another device: no remote copies, remote signals or barrier semaphores. Data moves between devices by JAX's collectives and lax.ppermute only.
A program may use at most 128 MiB of HBM per device.

v0:
```python
import jax
import jax.numpy as jnp
from jax import lax
from jax.sharding import PartitionSpec as P


def with_halo(block, sides, width):
    for axis, dim in sides:
        count = lax.axis_size(axis)
        forward = [(i, i + 1) for i in range(count - 1)]
        backward = [(target, source) for source, target in forward]
        low = lax.ppermute(
            lax.slice_in_dim(block, block.shape[dim] - width, None, axis=dim), axis, forward
        )
        high = lax.ppermute(lax.slice_in_dim(block, 0, width, axis=dim), axis, backward)
        block = jnp.concatenate([low, block, high], axis=dim)
    return block


def realify(operators):
    real_part = operators[..., 0, :, :]
    imag_part = operators[..., 1, :, :]
    upper_rows = jnp.concatenate([real_part, -imag_part], axis=-1)
    lower_rows = jnp.concatenate([imag_part, real_part], axis=-1)
    return jnp.concatenate([upper_rows, lower_rows], axis=-2)


def lift_level(densities, operators):
    stack_width = densities.shape[0]
    parents = densities.shape[1] // 8
    grouped = densities.reshape(stack_width, parents, 8)
    return jnp.einsum("cij,jmc->im", operators, grouped, preferred_element_type=jnp.float32).astype(
        jnp.bfloat16
    )


def spread(expansion, operators):
    stack_width, box_count = expansion.shape
    rounded = expansion.astype(jnp.bfloat16)
    children = jnp.einsum("cij,jm->imc", operators, rounded, preferred_element_type=jnp.float32)
    return children.reshape(stack_width, box_count * operators.shape[0])


def translate(ghosted, operators, sources, ghost_start):
    stack_width, ghost_count = ghosted.shape
    box_count, entry_count = sources.shape
    column_index = sources - ghost_start
    ghost_ids = jnp.arange(ghost_count, dtype=jnp.int32)[:, None]

    def add_entry(entry_slot, running_sum):
        wanted = lax.dynamic_index_in_dim(column_index, entry_slot, 1, keepdims=False)
        selector = (ghost_ids == wanted[None, :]).astype(jnp.bfloat16)
        picked = jnp.dot(ghosted, selector, preferred_element_type=jnp.float32).astype(jnp.bfloat16)
        operator = lax.dynamic_index_in_dim(operators, entry_slot, 0, keepdims=False)
        return running_sum + jnp.dot(operator, picked, preferred_element_type=jnp.float32)

    return lax.fori_loop(
        0, entry_count, add_entry, jnp.zeros((stack_width, box_count), jnp.float32)
    )


def level_step(expansion, densities, down_level, transfer_level, sources, position):
    box_count = densities.shape[1]
    ghosted = with_halo(densities, ((("row", "col"), 1),), box_count)
    start_box = position * box_count
    return spread(expansion, down_level) + translate(
        ghosted, transfer_level, sources, start_box - box_count
    )


def body(
    check_field,
    to_equiv,
    upward_ops,
    downward_ops,
    transfer_ops,
    list_fine,
    list_mid,
    list_low,
    list_top,
):
    stack_width = 2 * check_field.shape[1]
    position = lax.axis_index(("row", "col"))
    row_index = lax.axis_index("row")
    col_index = lax.axis_index("col")
    dense_fine = jnp.dot(
        realify(to_equiv), check_field.reshape(stack_width, -1), preferred_element_type=jnp.float32
    ).astype(jnp.bfloat16)
    dense_mid = lift_level(dense_fine, realify(upward_ops[0]))
    dense_low = lift_level(dense_mid, realify(upward_ops[1]))
    dense_four = lift_level(dense_low, realify(upward_ops[2]))
    upward_top = realify(upward_ops[3])
    own_operator = lax.dynamic_index_in_dim(upward_top, col_index, 0, keepdims=False)
    partial_term = jnp.dot(own_operator, dense_four, preferred_element_type=jnp.float32)
    own_box = lax.psum(partial_term, "col").astype(jnp.bfloat16)
    dense_top = lax.all_gather(own_box, "row", axis=1, tiled=True)
    own_list = lax.dynamic_slice_in_dim(list_top, row_index, 1, 0)
    local_top = translate(dense_top, realify(transfer_ops[3]), own_list, 0)
    down_operator = lax.dynamic_index_in_dim(realify(downward_ops[3]), col_index, 0, keepdims=False)
    local_four = jnp.dot(
        down_operator, local_top.astype(jnp.bfloat16), preferred_element_type=jnp.float32
    )
    local_low = level_step(
        local_four,
        dense_low,
        realify(downward_ops[2]),
        realify(transfer_ops[2]),
        list_low,
        position,
    )
    local_mid = level_step(
        local_low, dense_mid, realify(downward_ops[1]), realify(transfer_ops[1]), list_mid, position
    )
    local_fine = level_step(
        local_mid,
        dense_fine,
        realify(downward_ops[0]),
        realify(transfer_ops[0]),
        list_fine,
        position,
    )
    return local_fine.reshape(2, stack_width // 2, -1)


def solution(mesh):
    in_specs = (
        P(None, None, ("row", "col")),
        P(),
        P(),
        P(),
        P(),
        P(("row", "col"), None),
        P(("row", "col"), None),
        P(("row", "col"), None),
        P(),
    )
    out_specs = P(None, None, ("row", "col"))
    return jax.shard_map(body, mesh=mesh, in_specs=in_specs, out_specs=out_specs, check_vma=False)
```

profile of v0, /device:TPU:2, one launch (start us, length us, event | category | flops | bytes accessed | tf_op | source)
XLA Modules:
  0.0 271.7 jit_solution(8850133849275442751)
XLA Ops:
  0.0 3.9 %slice_bitcast_fusion.10 = (bf16[8,2,152,152]{3,2,1,0:T(8,128)(2,1)S(1)}, bf16[1,8,2,152,152]{4,3,2,1,0:T(8,128)(2,1)S(1)}, bf16[8,2,152,152]{3,2,1,0:T(8,128)(2,1)}, bf16[1,8,2,152,152]{4,3,2,1,0:T(8,128)(2,1)S(1)}) fusion(bf16[4,8,2,152,152]{4,3,2,1,0:T(8,128)(2,1)} %param.19), kind=kLoop, calls=%fused_computation.120 | loop fusion | bytes 5914624 | tf_op jit(solution)/shard_map/squeeze | solution.py:92
  9.4 3.3 %fusion.91 = bf16[304,64]{0,1:T(8,128)(2,1)} fusion(bf16[8,152,152]{2,1,0:T(8,128)(2,1)} %get-tuple-element.648, bf16[8,152,152]{2,1,0:T(8,128)(2,1)} %get-tuple-element.647, bf16[8,152,152]{2,1,0:T(8,128)(2,1)} %fusion.144, bf16[304,64,8]{0,2,1:T(8,128)(2,1)} %bitcast.234), kind=kOutput, calls=%fused_computation.125 | convolution fusion | flops 100568064 | bytes 1459200 | tf_op jit(solution)/shard_map/cij,jmc->im/dot_general | solution.py:32
  12.8 2.3 fusion.97
  15.0 3.8 %collective-permute-start = (bf16[304,8]{0,1:T(8,128)(2,1)}, bf16[304,8]{0,1:T(8,128)(2,1)}, u32[]{:S(2)}, u32[]{:S(2)}) collective-permute-start(bf16[304,8]{0,1:T(8,128)(2,1)} %fusion.97), channel_id=1, source_target_pairs={{0,1},{1,2},{2,3},{3,4},{4,5},{5,6},{6,7},{7,8},{8,9},{9,10},{10,1... | collective-permute-start | bytes 14600 | tf_op jit(solution)/shard_map/ppermute | solution.py:12
  18.9 5.3 %collective-permute-start.1 = (bf16[304,8]{0,1:T(8,128)(2,1)}, bf16[304,8]{0,1:T(8,128)(2,1)}, u32[]{:S(2)}, u32[]{:S(2)}) collective-permute-start(bf16[304,8]{0,1:T(8,128)(2,1)} %fusion.97), channel_id=1, source_target_pairs={{1,0},{2,1},{3,2},{4,3},{5,4},{6,5},{7,6},{8,7},{9,8},{10,9},{11,1... | collective-permute-start | bytes 14600 | tf_op jit(solution)/shard_map/ppermute | solution.py:15
  24.2 1.9 collective-permute-start.2
  26.1 5.8 %collective-permute-start.3 = (bf16[304,64]{0,1:T(8,128)(2,1)}, bf16[304,64]{0,1:T(8,128)(2,1)}, u32[]{:S(2)}, u32[]{:S(2)}) collective-permute-start(bf16[304,64]{0,1:T(8,128)(2,1)} %fusion.91), channel_id=1, source_target_pairs={{1,0},{2,1},{3,2},{4,3},{5,4},{6,5},{7,6},{8,7},{9,8},{10,9},{11,1... | collective-permute-start | bytes 116744 | tf_op jit(solution)/shard_map/ppermute | solution.py:15
  31.8 1.9 collective-permute-start.4
  33.8 1.5 slice_bitcast_fusion.22
  36.5 2.9 %fusion.152 = (bf16[1,16,2,152,152]{4,3,2,1,0:T(8,128)(2,1)}, bf16[1,16,2,152,152]{4,3,2,1,0:T(8,128)(2,1)}, bf16[1,16,2,152,152]{4,3,2,1,0:T(8,128)(2,1)S(1)}, bf16[1,16,2,152,152]{4,3,2,1,0:T(8,128)(2,1)S(1)}) fusion(bf16[4,16,2,152,152]{4,3,2,1,0:T(8,128)(2,1)S(1)} %bitcast.231), kind=kLoop, calls=%fused_computation.205 | loop fusion | bytes 11829248 | tf_op jit(solution)/shard_map/slice | solution.py:118
  39.8 1.7 slice_bitcast_fusion.6
  42.5 4.3 %slice_bitcast_fusion.8 = (bf16[8,2,152,152]{3,2,1,0:T(8,128)(2,1)S(1)}, bf16[1,8,2,152,152]{4,3,2,1,0:T(8,128)(2,1)}, bf16[8,2,152,152]{3,2,1,0:T(8,128)(2,1)S(1)}, bf16[1,8,2,152,152]{4,3,2,1,0:T(8,128)(2,1)}) fusion(bf16[4,8,2,152,152]{4,3,2,1,0:T(8,128)(2,1)} %param.20), kind=kLoop, calls=%fused_computation.118 | loop fusion | bytes 5914624 | tf_op jit(solution)/shard_map/squeeze | solution.py:106
  46.8 1.3 slice_bitcast_fusion.16
  49.4 1.7 slice_bitcast_fusion.4
  52.2 2.0 copy_bitcast_fusion.4
  56.8 1.7 slice_bitcast_fusion.2
  61.6 1.6 slice_bitcast_fusion
  65.1 1.5 fusion.100
  67.9 29.9 %psum.7 = bf16[304,1]{0,1:T(2,128)(2,1)S(1)} all-reduce(f32[304,1]{0,1:T(1,128)S(1)} %convolution_bitcast_fusion.1), channel_id=1, replica_groups=mesh['row'=32,'col'=8] {'col'}, use_global_device_ids=true, to_apply=%region_0.1 | all-reduce | flops 304 | bytes 1824 | tf_op jit(solution)/shard_map/psum | solution.py:95
  97.8 24.3 %all-gather = bf16[32,1,304]{2,1,0:T(2,128)(2,1)S(1)} all-gather(bf16[1,1,304]{2,1,0:T(2,128)(2,1)S(1)} %bitcast.236), channel_id=1, replica_groups=mesh['row'=32,'col'=8] {'row'}, dimensions={0}, use_global_device_ids=true | all-gather | bytes 20064 | tf_op jit(solution)/shard_map/all_gather | solution.py:96
  122.3 5.1 %maximum_maximum_fusion = bf16[16,304,304]{2,1,0:T(8,128)(2,1)} fusion(bf16[16,152,152]{2,1,0:T(8,128)(2,1)} %get-tuple-element.630, bf16[16,152,152]{2,1,0:T(8,128)(2,1)S(1)} %copy-done.13, bf16[16,152,152]{2,1,0:T(8,128)(2,1)} %fusion.148), kind=kLoop, calls=%fused_computation.41 | loop fusion | flops 11829248 | bytes 5175296 | tf_op jit(solution)/shard_map/concatenate | solution.py:25
  127.5 41.2 %while.56 = (s32[]{:T(128)}, f32[304,1]{0,1:T(1,128)S(1)}, bf16[16,304,304]{2,1,0:T(8,128)(2,1)}, s32[1,16]{0,1:T(8,128)S(1)}, bf16[304,32]{1,0:T(8,128)(2,1)S(1)}, /*index=5*/s32[]{:T(128)}, s32[]{:T(128)}) while((s32[]{:T(128)}, f32[304,1]{0,1:T(1,128)S(1)}, bf16[16,304,304]{2,1,0:T(8,128)(2,1)}, s32[1,16]{0,1:T(8,128)S(1)}, ...), condition=%wide.region_2.3_spmd.clone, body=%wide.region_1.2_spmd.clone.sunk | while | flops 204931 | bytes 258407 | solution.py:57
  168.7 1.3 convolution_reduce_fusion.1
  170.1 4.8 %maximum_maximum_fusion.1 = bf16[16,304,304]{2,1,0:T(8,128)(2,1)} fusion(bf16[16,152,152]{2,1,0:T(8,128)(2,1)S(1)} %copy-done.6, bf16[16,152,152]{2,1,0:T(8,128)(2,1)S(1)} %copy-done.5, bf16[16,152,152]{2,1,0:T(8,128)(2,1)} %fusion.149), kind=kLoop, calls=%fused_computation.42 | loop fusion | flops 11829248 | bytes 5175296 | tf_op jit(solution)/shard_map/concatenate | solution.py:25
  175.0 3.7 %maximum_maximum_fusion.2 = bf16[16,304,304]{2,1,0:T(8,128)(2,1)} fusion(bf16[16,152,152]{2,1,0:T(8,128)(2,1)S(1)} %copy-done.8, bf16[16,152,152]{2,1,0:T(8,128)(2,1)S(1)} %copy-done.7, bf16[16,152,152]{2,1,0:T(8,128)(2,1)S(1)} %copy-done.9), kind=kLoop, calls=%fused_computation.43 | loop fusion | flops 11829248 | bytes 5175296 | tf_op jit(solution)/shard_map/concatenate | solution.py:25
  178.7 3.7 %maximum_maximum_fusion.3 = bf16[16,304,304]{2,1,0:T(8,128)(2,1)} fusion(bf16[16,152,152]{2,1,0:T(8,128)(2,1)S(1)} %copy-done.11, bf16[16,152,152]{2,1,0:T(8,128)(2,1)S(1)} %copy-done.10, bf16[16,152,152]{2,1,0:T(8,128)(2,1)S(1)} %copy-done.12), kind=kLoop, calls=%fused_computation.44 | loop fusion | flops 11829248 | bytes 5175296 | tf_op jit(solution)/shard_map/concatenate | solution.py:25
  183.3 4.1 %collective-permute-start.5 = (bf16[304,512]{1,0:T(8,128)(2,1)S(1)}, bf16[304,512]{1,0:T(8,128)(2,1)}, u32[]{:S(2)}, u32[]{:S(2)}) collective-permute-start(bf16[304,512]{1,0:T(8,128)(2,1)S(1)} %convolution_convert_fusion.2), channel_id=1, source_target_pairs={{1,0},{2,1},{3,2},{4,3},{5,4},{6,5},{7,6},{8,7},{9,8},{10,9},{11,1... | collective-permute-start | bytes 933896 | tf_op jit(solution)/shard_map/ppermute | solution.py:15
  188.2 20.4 %while.57 = (s32[]{:T(128)}, f32[304,8]{0,1:T(8,128)S(1)}, bf16[16,304,304]{2,1,0:T(8,128)(2,1)}, s32[8,16]{0,1:T(8,128)S(1)}, bf16[304,24]{0,1:T(8,128)(2,1)S(1)}, /*index=5*/s32[]{:T(128)}, s32[]{:T(128)}) while((s32[]{:T(128)}, f32[304,8]{0,1:T(8,128)S(1)}, bf16[16,304,304]{2,1,0:T(8,128)(2,1)}, s32[8,16]{0,1:T(8,128)S(1)}, ...), condition=%wide.region_4.5_spmd.clone, body=%wide.region_3.4_spmd.clone.sunk | while | flops 1602883 | bytes 268219 | solution.py:57
  189.5 1.2 convolution_add_fusion.6
  210.6 21.9 %while.58 = (s32[]{:T(128)}, f32[304,64]{0,1:T(8,128)S(1)}, bf16[16,304,304]{2,1,0:T(8,128)(2,1)}, s32[64,16]{0,1:T(8,128)S(1)}, bf16[304,192]{1,0:T(8,128)(2,1)S(1)}, /*index=5*/s32[]{:T(128)}, s32[]{:T(128)}) while((s32[]{:T(128)}, f32[304,64]{0,1:T(8,128)S(1)}, bf16[16,304,304]{2,1,0:T(8,128)(2,1)}, s32[64,16]{0,1:T(8,128)S(1)}, ...), condition=%wide.region_6.7_spmd.clone, body=%wide.region_5.6_spmd.clone.sunk | while | flops 19383300 | bytes 507227 | solution.py:57
  210.6 1.3 convolution_add_fusion.7
  212.0 1.3 convolution_add_fusion.7
  213.3 1.3 convolution_add_fusion.7
  214.7 1.3 convolution_add_fusion.7
  216.1 1.3 convolution_add_fusion.7
  217.4 1.3 convolution_add_fusion.7
  218.8 1.3 convolution_add_fusion.7
  220.2 1.3 convolution_add_fusion.7
  221.5 1.3 convolution_add_fusion.7
  222.9 1.3 convolution_add_fusion.7
  224.3 1.3 convolution_add_fusion.7
  225.6 1.3 convolution_add_fusion.7
  227.0 1.3 convolution_add_fusion.7
  228.4 1.3 convolution_add_fusion.7
  229.7 1.3 convolution_add_fusion.7
  231.1 1.3 convolution_add_fusion.7
  232.5 2.0 fusion.82
  236.3 34.4 %while.59 = (s32[]{:T(128)}, f32[304,512]{1,0:T(8,128)S(1)}, bf16[16,304,304]{2,1,0:T(8,128)(2,1)}, s32[512,16]{0,1:T(8,128)S(1)}, bf16[304,1536]{1,0:T(8,128)(2,1)S(1)}, /*index=5*/s32[]{:T(128)}, s32[]{:T(128)}) while((s32[]{:T(128)}, f32[304,512]{1,0:T(8,128)S(1)}, bf16[16,304,304]{2,1,0:T(8,128)(2,1)}, ...), condition=%wide.region_8.9_spmd.clone, body=%wide.region_7.8_spmd.clone.sunk | while | flops 574038016 | bytes 2419291 | solution.py:57
  236.4 2.1 convolution_add_fusion.8
  238.5 2.1 convolution_add_fusion.8
  240.6 2.1 convolution_add_fusion.8
  242.8 2.1 convolution_add_fusion.8
  245.0 2.1 convolution_add_fusion.8
  247.1 2.1 convolution_add_fusion.8
  249.3 2.1 convolution_add_fusion.8
  251.4 2.1 convolution_add_fusion.8
  253.6 2.1 convolution_add_fusion.8
  255.7 2.1 convolution_add_fusion.8
  257.9 2.1 convolution_add_fusion.8
  260.0 2.1 convolution_add_fusion.8
  262.2 2.1 convolution_add_fusion.8
  264.3 2.1 convolution_add_fusion.8
  266.5 2.1 convolution_add_fusion.8
  268.6 2.1 convolution_add_fusion.8
  (255 shorter events, 85.8 us)
Async XLA Ops:
  0.0 8.1 %copy-start = (bf16[2,152,512]{2,1,0:T(8,128)(2,1)S(1)}, bf16[2,152,512]{2,1,0:T(8,128)(2,1)}, u32[]{:S(2)}) copy-start(bf16[2,152,512]{2,1,0:T(8,128)(2,1)} %param.17) | copy-start | bytes 933892
  4.1 2.0 copy-start.31
  8.5 28.0 %slice-start = ((s8[9961472]{0:T(1024)(128)(4,1)}), s8[1572864]{0:T(1024)(128)(4,1)S(1)}, s32[]{:S(2)}) async-start(s8[9961472]{0:T(1024)(128)(4,1)} %bitcast.230), calls=%async_computation | async-start | bytes 3145728
  9.4 3.3 %copy-start.28 = (bf16[8,152,152]{2,1,0:T(8,128)(2,1)S(1)}, bf16[8,152,152]{2,1,0:T(8,128)(2,1)}, u32[]{:S(2)}) copy-start(bf16[8,152,152]{2,1,0:T(8,128)(2,1)} %get-tuple-element.643) | copy-start | bytes 1108996
  9.4 3.3 %copy-start.29 = (bf16[8,152,152]{2,1,0:T(8,128)(2,1)S(1)}, bf16[8,152,152]{2,1,0:T(8,128)(2,1)}, u32[]{:S(2)}) copy-start(bf16[8,152,152]{2,1,0:T(8,128)(2,1)} %get-tuple-element.644) | copy-start | bytes 1108996
  9.4 3.3 %copy-start.30 = (bf16[8,152,152]{2,1,0:T(8,128)(2,1)S(1)}, bf16[8,152,152]{2,1,0:T(8,128)(2,1)}, u32[]{:S(2)}) copy-start(bf16[8,152,152]{2,1,0:T(8,128)(2,1)} %fusion.143) | copy-start | bytes 1108996
  9.4 27.1 %slice-start.1 = ((s8[9961472]{0:T(1024)(128)(4,1)}), s8[4194304]{0:T(1024)(128)(4,1)S(1)}, s32[]{:S(2)}) async-start(s8[9961472]{0:T(1024)(128)(4,1)} %bitcast.230), calls=%async_computation.1 | async-start | bytes 8388608
  12.8 21.0 %copy-start.4 = (bf16[8,2,152,152]{3,2,1,0:T(8,128)(2,1)S(1)}, bf16[8,2,152,152]{3,2,1,0:T(8,128)(2,1)}, u32[]{:S(2)}) copy-start(bf16[8,2,152,152]{3,2,1,0:T(8,128)(2,1)} %get-tuple-element.625) | copy-start | bytes 2217988
  12.8 23.8 %slice-start.2 = ((s8[9961472]{0:T(1024)(128)(4,1)}), s8[4194304]{0:T(1024)(128)(4,1)S(1)}, s32[]{:S(2)}) async-start(s8[9961472]{0:T(1024)(128)(4,1)} %bitcast.230), calls=%async_computation.2 | async-start | bytes 8388608
  15.0 168.2 %collective-permute-start = (bf16[304,8]{0,1:T(8,128)(2,1)}, bf16[304,8]{0,1:T(8,128)(2,1)}, u32[]{:S(2)}, u32[]{:S(2)}) collective-permute-start(bf16[304,8]{0,1:T(8,128)(2,1)} %fusion.97), channel_id=1, source_target_pairs={{0,1},{1,2},{2,3},{3,4},{4,5},{5,6},{6,7},{7,8},{8,9},{9,10},{10,1... | collective-permute-start | bytes 14600 | tf_op jit(solution)/shard_map/ppermute | solution.py:12
  18.9 168.6 %collective-permute-start.1 = (bf16[304,8]{0,1:T(8,128)(2,1)}, bf16[304,8]{0,1:T(8,128)(2,1)}, u32[]{:S(2)}, u32[]{:S(2)}) collective-permute-start(bf16[304,8]{0,1:T(8,128)(2,1)} %fusion.97), channel_id=1, source_target_pairs={{1,0},{2,1},{3,2},{4,3},{5,4},{6,5},{7,6},{8,7},{9,8},{10,9},{11,1... | collective-permute-start | bytes 14600 | tf_op jit(solution)/shard_map/ppermute | solution.py:15
  24.2 185.3 %collective-permute-start.2 = (bf16[304,64]{0,1:T(8,128)(2,1)}, bf16[304,64]{0,1:T(8,128)(2,1)}, u32[]{:S(2)}, u32[]{:S(2)}) collective-permute-start(bf16[304,64]{0,1:T(8,128)(2,1)} %fusion.91), channel_id=1, source_target_pairs={{0,1},{1,2},{2,3},{3,4},{4,5},{5,6},{6,7},{7,8},{8,9},{9,10},{10,1... | collective-permute-start | bytes 116744 | tf_op jit(solution)/shard_map/ppermute | solution.py:12
  26.1 183.4 %collective-permute-start.3 = (bf16[304,64]{0,1:T(8,128)(2,1)}, bf16[304,64]{0,1:T(8,128)(2,1)}, u32[]{:S(2)}, u32[]{:S(2)}) collective-permute-start(bf16[304,64]{0,1:T(8,128)(2,1)} %fusion.91), channel_id=1, source_target_pairs={{1,0},{2,1},{3,2},{4,3},{5,4},{6,5},{7,6},{8,7},{9,8},{10,9},{11,1... | collective-permute-start | bytes 116744 | tf_op jit(solution)/shard_map/ppermute | solution.py:15
  31.8 203.3 %collective-permute-start.4 = (bf16[304,512]{1,0:T(8,128)(2,1)S(1)}, bf16[304,512]{1,0:T(8,128)(2,1)}, u32[]{:S(2)}, u32[]{:S(2)}) collective-permute-start(bf16[304,512]{1,0:T(8,128)(2,1)S(1)} %convolution_convert_fusion.2), channel_id=1, source_target_pairs={{0,1},{1,2},{2,3},{3,4},{4,5},{5,6},{6,7},{7,8},{8,9},{9,10},{10,1... | collective-permute-start | bytes 933896 | tf_op jit(solution)/shard_map/ppermute | solution.py:12
  52.2 4.0 %copy-start.3 = (bf16[1,16,2,152,152]{4,3,2,1,0:T(8,128)(2,1)S(1)}, bf16[1,16,2,152,152]{4,3,2,1,0:T(8,128)(2,1)}, u32[]{:S(2)}) copy-start(bf16[1,16,2,152,152]{4,3,2,1,0:T(8,128)(2,1)} %get-tuple-element.616) | copy-start | bytes 4435972
  54.2 2.3 copy-start.2
  63.2 1.3 copy-start.25
  63.2 1.7 copy-start.26
  63.2 1.9 copy-start.27
  65.1 1.5 copy-start.14
  65.1 1.5 copy-start.15
  65.1 57.1 %copy-start.33 = (s32[32,16]{0,1:T(8,128)S(1)}, s32[32,16]{0,1:T(8,128)}, u32[]{:S(2)}) copy-start(s32[32,16]{0,1:T(8,128)} %param.25) | copy-start | bytes 6148
  66.7 55.7 %copy-start.13 = (bf16[16,152,152]{2,1,0:T(8,128)(2,1)S(1)}, bf16[16,152,152]{2,1,0:T(8,128)(2,1)}, u32[]{:S(2)}) copy-start(bf16[16,152,152]{2,1,0:T(8,128)(2,1)} %get-tuple-element.629) | copy-start | bytes 2217988
  122.3 47.7 %copy-start.6 = (bf16[16,152,152]{2,1,0:T(8,128)(2,1)S(1)}, bf16[16,152,152]{2,1,0:T(8,128)(2,1)}, u32[]{:S(2)}) copy-start(bf16[16,152,152]{2,1,0:T(8,128)(2,1)} %get-tuple-element.632) | copy-start | bytes 2217988
  127.5 42.5 %copy-start.35 = (s32[8,16]{1,0:T(8,128)S(1)}, s32[8,16]{1,0:T(8,128)}, u32[]{:S(2)}) copy-start(s32[8,16]{1,0:T(8,128)} %param.24) | copy-start | bytes 1540
  127.5 42.6 %copy-start.32 = (s32[512,16]{0,1:T(8,128)S(1)}, s32[512,16]{0,1:T(8,128)}, u32[]{:S(2)}) copy-start(s32[512,16]{0,1:T(8,128)} %param.22) | copy-start | bytes 98308
  127.5 42.6 %copy-start.5 = (bf16[16,152,152]{2,1,0:T(8,128)(2,1)S(1)}, bf16[16,152,152]{2,1,0:T(8,128)(2,1)}, u32[]{:S(2)}) copy-start(bf16[16,152,152]{2,1,0:T(8,128)(2,1)} %get-tuple-element.631) | copy-start | bytes 2217988
  170.1 4.9 %copy-start.7 = (bf16[16,152,152]{2,1,0:T(8,128)(2,1)S(1)}, bf16[16,152,152]{2,1,0:T(8,128)(2,1)}, u32[]{:S(2)}) copy-start(bf16[16,152,152]{2,1,0:T(8,128)(2,1)} %get-tuple-element.633) | copy-start | bytes 2217988
  170.1 4.9 %copy-start.8 = (bf16[16,152,152]{2,1,0:T(8,128)(2,1)S(1)}, bf16[16,152,152]{2,1,0:T(8,128)(2,1)}, u32[]{:S(2)}) copy-start(bf16[16,152,152]{2,1,0:T(8,128)(2,1)} %get-tuple-element.634) | copy-start | bytes 2217988
  170.1 4.8 %copy-start.9 = (bf16[16,152,152]{2,1,0:T(8,128)(2,1)S(1)}, bf16[16,152,152]{2,1,0:T(8,128)(2,1)}, u32[]{:S(2)}) copy-start(bf16[16,152,152]{2,1,0:T(8,128)(2,1)} %fusion.150) | copy-start | bytes 2217988
  174.9 3.7 %copy-start.10 = (bf16[16,152,152]{2,1,0:T(8,128)(2,1)S(1)}, bf16[16,152,152]{2,1,0:T(8,128)(2,1)}, u32[]{:S(2)}) copy-start(bf16[16,152,152]{2,1,0:T(8,128)(2,1)} %get-tuple-element.627) | copy-start | bytes 2217988
  174.9 3.7 %copy-start.11 = (bf16[16,152,152]{2,1,0:T(8,128)(2,1)S(1)}, bf16[16,152,152]{2,1,0:T(8,128)(2,1)}, u32[]{:S(2)}) copy-start(bf16[16,152,152]{2,1,0:T(8,128)(2,1)} %get-tuple-element.628) | copy-start | bytes 2217988
  174.9 3.7 %copy-start.12 = (bf16[16,152,152]{2,1,0:T(8,128)(2,1)S(1)}, bf16[16,152,152]{2,1,0:T(8,128)(2,1)}, u32[]{:S(2)}) copy-start(bf16[16,152,152]{2,1,0:T(8,128)(2,1)} %fusion.151) | copy-start | bytes 2217988
  178.7 3.7 %copy-start.21 = (bf16[8,152,152]{2,1,0:T(8,128)(2,1)S(1)}, bf16[8,152,152]{2,1,0:T(8,128)(2,1)}, u32[]{:S(2)}) copy-start(bf16[8,152,152]{2,1,0:T(8,128)(2,1)} %get-tuple-element.635) | copy-start | bytes 1108996
  178.7 3.7 %copy-start.22 = (bf16[8,152,152]{2,1,0:T(8,128)(2,1)S(1)}, bf16[8,152,152]{2,1,0:T(8,128)(2,1)}, u32[]{:S(2)}) copy-start(bf16[8,152,152]{2,1,0:T(8,128)(2,1)} %get-tuple-element.636) | copy-start | bytes 1108996
  178.7 3.7 %copy-start.23 = (bf16[8,152,152]{2,1,0:T(8,128)(2,1)S(1)}, bf16[8,152,152]{2,1,0:T(8,128)(2,1)}, u32[]{:S(2)}) copy-start(bf16[8,152,152]{2,1,0:T(8,128)(2,1)} %get-tuple-element.658) | copy-start | bytes 1108996
  182.4 0.8 copy-start.34
  182.4 26.2 %copy-start.18 = (bf16[8,152,152]{2,1,0:T(8,128)(2,1)S(1)}, bf16[8,152,152]{2,1,0:T(8,128)(2,1)}, u32[]{:S(2)}) copy-start(bf16[8,152,152]{2,1,0:T(8,128)(2,1)} %get-tuple-element.645) | copy-start | bytes 1108996
  182.4 26.2 %copy-start.19 = (bf16[8,152,152]{2,1,0:T(8,128)(2,1)S(1)}, bf16[8,152,152]{2,1,0:T(8,128)(2,1)}, u32[]{:S(2)}) copy-start(bf16[8,152,152]{2,1,0:T(8,128)(2,1)} %get-tuple-element.646) | copy-start | bytes 1108996
  182.4 26.2 %copy-start.20 = (bf16[8,152,152]{2,1,0:T(8,128)(2,1)S(1)}, bf16[8,152,152]{2,1,0:T(8,128)(2,1)}, u32[]{:S(2)}) copy-start(bf16[8,152,152]{2,1,0:T(8,128)(2,1)} %fusion.146) | copy-start | bytes 1108996
  183.3 51.9 %collective-permute-start.5 = (bf16[304,512]{1,0:T(8,128)(2,1)S(1)}, bf16[304,512]{1,0:T(8,128)(2,1)}, u32[]{:S(2)}, u32[]{:S(2)}) collective-permute-start(bf16[304,512]{1,0:T(8,128)(2,1)S(1)} %convolution_convert_fusion.2), channel_id=1, source_target_pairs={{1,0},{2,1},{3,2},{4,3},{5,4},{6,5},{7,6},{8,7},{9,8},{10,9},{11,1... | collective-permute-start | bytes 933896 | tf_op jit(solution)/shard_map/ppermute | solution.py:15
  208.7 23.8 %copy-start.17 = (bf16[8,152,152]{2,1,0:T(8,128)(2,1)S(1)}, bf16[8,152,152]{2,1,0:T(8,128)(2,1)}, u32[]{:S(2)}) copy-start(bf16[8,152,152]{2,1,0:T(8,128)(2,1)} %get-tuple-element.650) | copy-start | bytes 1108996
  209.5 23.0 %copy-start.16 = (bf16[8,152,152]{2,1,0:T(8,128)(2,1)S(1)}, bf16[8,152,152]{2,1,0:T(8,128)(2,1)}, u32[]{:S(2)}) copy-start(bf16[8,152,152]{2,1,0:T(8,128)(2,1)} %get-tuple-element.649) | copy-start | bytes 1108996
  234.4 1.9 copy-start.24
  270.7 1.0 copy-start.1
where the time goes:
time: 275 us; the launch traced here: 272 us
  matrix products  119 us (43%)
  blocking collectives  54.2 us (20%)
  local copies, waits for them, and re-layouts  41.7 us (15%)
  other arithmetic  31.5 us (11%)
  starting transfers between devices  22.8 us (8%)
    dot_general x64, matrix products, add_entry(): jnp.dot(operator, picked, preferred_element_type=jnp.float32)  92.2 us
    psum x1, blocking collectives, body(): own_box = lax.psum(partial_term, 'col').astype(jnp.bfloat16)  29.9 us
    all_gather x1, blocking collectives, body(): dense_top = lax.all_gather(own_box, 'row', axis=1, tiled=True)  24.3 us
    concatenate x4, other arithmetic, realify(): return jnp.concatenate([upper_rows, lower_rows], axis=-2)  17.4 us
    ppermute x3, starting transfers between devices, with_halo(): lax.ppermute(lax.slice_in_dim(block, 0, width, axis=dim), axis, backward)  15.2 us
    squeeze x11, local copies, waits for them, and re-layouts, realify(): imag_part = operators[..., 1, :, :]  14 us
    dot_general x16, matrix products, add_entry(): jnp.dot(ghosted, selector, preferred_element_type=jnp.float32)  13.3 us
    neg x11, other arithmetic, realify(): upper_rows = jnp.concatenate([real_part, -imag_part], axis=-1)  10.4 us
  transfers between devices with their start and end apart: 6, of which 0 were waited for; matrix products, arithmetic and copies ran while one was open for 52% of the time, Pallas kernels for 0%

commit v1 on v0

v1 whole, which is shorter than its diff:
```python
import functools

import jax
import jax.numpy as jnp
from jax import lax
from jax.experimental import pallas as pl
from jax.experimental.pallas import tpu as pltpu
from jax.sharding import PartitionSpec as P

SIZE = 152
HALF = 64
FINE = 512
REACH = 256
ENTRIES = 16
OCTANTS = 8
BF16 = jnp.bfloat16
F32 = jnp.float32


def mm(a, b):
    return jnp.dot(a, b, preferred_element_type=F32)


def iota(shape, dim):
    return lax.broadcasted_iota(jnp.int32, shape, dim)


def combine(by_real, by_imag):
    turned = pltpu.roll(by_imag, HALF, 1)
    return by_real + jnp.where(iota(turned.shape, 1) < HALF, -turned, turned)


def child_columns(level):
    del level
    row = iota((128, 1024), 0)
    col = iota((128, 1024), 1)
    octant, lane = col >> 7, col & 127
    box = (lane & 63) * 8 + octant
    wanted = jnp.where(box < HALF, (lane & HALF) + box, -1)
    return (row == wanted).astype(BF16)


def parent_columns():
    row = iota((128, 1024), 0)
    col = iota((128, 1024), 1)
    octant, lane = col >> 7, col & 127
    box = lane & 63
    wanted = jnp.where((box & 7) == octant, (lane & HALF) + (box >> 3), -1)
    return (row == wanted).astype(BF16)


def up_kernel(col_ref, check, to_equiv, ops_hbm, to_left, to_right, top, ops, own_op, sems):
    copies = [
        pltpu.make_async_copy(ops_hbm.at[level], ops.at[level], sems.at[level])
        for level in range(3)
    ]
    copies.append(pltpu.make_async_copy(ops_hbm.at[3, col_ref[0]], own_op, sems.at[3]))
    for copy in copies:
        copy.start()
    field = jnp.concatenate([check[0], check[1]], axis=1)
    by_real = mm(to_equiv[0], field)
    by_imag = mm(to_equiv[1], field)
    real = (by_real[:, :FINE] - by_imag[:, FINE:]).astype(BF16)
    imag = (by_real[:, FINE:] + by_imag[:, :FINE]).astype(BF16)
    to_left[:, :REACH] = jnp.concatenate([real[:, :REACH], imag[:, :REACH]], axis=0)
    to_right[:, :REACH] = jnp.concatenate([real[:, REACH:], imag[:, REACH:]], axis=0)

    row = iota((FINE, 1024), 0)
    col = iota((FINE, 1024), 1)
    octant, lane = col >> 7, col & 127
    box = (lane & 63) * 8 + octant
    of_real = (row == jnp.where(lane < HALF, box, -1)).astype(BF16)
    of_imag = (row == jnp.where(lane >= HALF, box, -1)).astype(BF16)
    children = (mm(real, of_real) + mm(imag, of_imag)).astype(BF16)
    pick = child_columns(0)
    packed = []
    for level in range(3):
        copies[level].wait()
        by_real = jnp.zeros((SIZE, 128), F32)
        by_imag = jnp.zeros((SIZE, 128), F32)
        for c in range(OCTANTS):
            one = children[:, 128 * c : 128 * (c + 1)]
            by_real += mm(ops[level, c, 0], one)
            by_imag += mm(ops[level, c, 1], one)
        dense = combine(by_real, by_imag).astype(BF16)
        packed.append(dense)
        if level < 2:
            children = mm(dense, pick).astype(BF16)
    both = jnp.concatenate([packed[0].astype(F32), packed[1].astype(F32)], axis=0).astype(BF16)
    to_left[:, REACH:] = both
    to_right[:, REACH:] = both
    copies[3].wait()
    part = combine(mm(own_op[0], packed[2]), mm(own_op[1], packed[2]))
    flat = jnp.transpose(jnp.concatenate([part, jnp.zeros((104, 128), F32)], axis=0))
    top[0:1, :] = flat[0:1, :]
    top[1:2, :] = flat[HALF : HALF + 1, :]


def translate_packed(around, codes, targets, ops_pair):
    by_real = jnp.zeros((SIZE, 128), F32)
    by_imag = jnp.zeros((SIZE, 128), F32)
    for k in range(ENTRIES):
        select = (codes == targets[k : k + 1, :]).astype(BF16)
        picked = mm(around, select).astype(BF16)
        by_real += mm(ops_pair[k, 0], picked)
        by_imag += mm(ops_pair[k, 1], picked)
    return combine(by_real, by_imag)


def near_kernel(
    start_ref, from_left, from_right, to_left, to_right, fine_t, mid_t, low_t, ops_hbm,
    fine_out, mid_out, low_out, around, ops, sems,
):
    copies = [
        pltpu.make_async_copy(ops_hbm.at[level], ops.at[level], sems.at[level])
        for level in range(3)
    ]
    for level in (2, 1, 0):
        copies[level].start()
    position = start_ref[0]
    around[:, 0:REACH] = from_left[:, :REACH]
    around[:, REACH : 2 * REACH] = to_left[:, :REACH]
    around[:, 2 * REACH : 3 * REACH] = to_right[:, :REACH]
    around[:, 3 * REACH :] = from_right[:, :REACH]

    lows = [ref[SIZE:, REACH:].astype(F32) for ref in (to_left, from_left, from_right)]
    low_all = (lows[0] + pltpu.roll(lows[1], 8, 1) + pltpu.roll(lows[2], 16, 1)).astype(BF16)
    row = iota((128, 128), 0)
    lane = row & 63
    place = jnp.where(lane < 8, lane, jnp.where(lane < 16, lane - 16, lane - 8))
    codes = jnp.where(lane < 24, (row >> 6) * 1024 + place, -(1 << 20))
    low_index = low_t[...] - position * 8
    pad = jnp.full((ENTRIES, HALF - 8), -(1 << 19), jnp.int32)
    targets = jnp.concatenate([low_index, pad, low_index + 1024, pad], axis=1)
    copies[2].wait()
    low_out[...] = translate_packed(low_all, codes, targets, ops.at[2])

    mid_all = jnp.concatenate(
        [from_left[:SIZE, REACH:], to_left[:SIZE, REACH:], from_right[:SIZE, REACH:]], axis=1
    )
    row = iota((384, 128), 0)
    codes = ((row >> 6) & 1) * 1024 + (row & 63) + ((row >> 7) - 1) * HALF
    mid_index = mid_t[...] - position * HALF
    targets = jnp.concatenate([mid_index, mid_index + 1024], axis=1)
    copies[1].wait()
    mid_out[...] = translate_packed(mid_all, codes, targets, ops.at[1])

    copies[0].wait()
    row = iota((3 * REACH, REACH), 0)
    for half in range(2):
        start = half * REACH
        window = around[:, start : start + 3 * REACH]
        index = fine_t[:, start : start + REACH] - (position * FINE - REACH + start)
        by_real = jnp.zeros((SIZE, FINE), F32)
        by_imag = jnp.zeros((SIZE, FINE), F32)
        for k in range(ENTRIES):
            select = (row == index[k : k + 1, :]).astype(BF16)
            picked = mm(window, select)
            picked = jnp.concatenate([picked[:SIZE], picked[SIZE:]], axis=1).astype(BF16)
            by_real += mm(ops[0, k, 0], picked)
            by_imag += mm(ops[0, k, 1], picked)
        fine_out[0, :, start : start + REACH] = by_real[:, :REACH] - by_imag[:, REACH:]
        fine_out[1, :, start : start + REACH] = by_real[:, REACH:] + by_imag[:, :REACH]


def down_kernel(
    col_ref, tops, own_list, fine_near, mid_near, low_near, transfer_hbm, down_hbm, out,
    transfer, down, own_op, sems,
):
    copies = [
        pltpu.make_async_copy(down_hbm.at[level], down.at[level], sems.at[level])
        for level in range(3)
    ]
    copies.append(pltpu.make_async_copy(down_hbm.at[3, col_ref[0]], own_op, sems.at[3]))
    copies.append(pltpu.make_async_copy(transfer_hbm.at[3], transfer, sems.at[4]))
    for level in (4, 3, 2, 1, 0):
        copies[level].start()

    gap = jnp.zeros((HALF - tops.shape[1], 256), F32)
    rows = jnp.concatenate([tops[0], gap, tops[1], gap], axis=0)
    dense = jnp.transpose(rows)[:SIZE].astype(BF16)
    row = iota((128, 128), 0)
    lane = iota((128, 128), 1)
    listed = own_list[...]
    pad = jnp.full((1, HALF - ENTRIES), -(1 << 19), jnp.int32)
    wanted = jnp.concatenate([listed, pad, listed + HALF, pad], axis=1)
    picked = mm(dense, (row == wanted).astype(BF16))
    lane = iota((SIZE, 128), 1)
    copies[4].wait()
    by_real = jnp.zeros((SIZE, 128), F32)
    by_imag = jnp.zeros((SIZE, 128), F32)
    for k in range(ENTRIES):
        one = jnp.where((lane & 63) == k, picked, 0.0).astype(BF16)
        by_real += mm(transfer[k, 0], one)
        by_imag += mm(transfer[k, 1], one)
    local = combine(by_real, by_imag)
    for shift in (8, 4, 2, 1):
        local = local + pltpu.roll(local, 128 - shift, 1)
    local = jnp.where((lane & 63) == 0, local, 0.0).astype(BF16)
    copies[3].wait()
    local = combine(mm(own_op[0], local), mm(own_op[1], local)).astype(BF16)
    place = parent_columns()
    for level, near in ((2, low_near), (1, mid_near)):
        parents = mm(local, place).astype(BF16)
        copies[level].wait()
        by_real = jnp.zeros((SIZE, 128), F32)
        by_imag = jnp.zeros((SIZE, 128), F32)
        for c in range(OCTANTS):
            one = parents[:, 128 * c : 128 * (c + 1)]
            by_real += mm(down[level, c, 0], one)
            by_imag += mm(down[level, c, 1], one)
        local = (combine(by_real, by_imag) + near[...]).astype(BF16)
    copies[0].wait()
    row = iota((128, 1024), 0)
    col = iota((128, 1024), 1)
    by_real = jnp.zeros((SIZE, 1024), F32)
    by_imag = jnp.zeros((SIZE, 1024), F32)
    child = col & (FINE - 1)
    source = (col >> 9) * HALF + (child >> 3)
    for c in range(OCTANTS):
        spread = (row == jnp.where((child & 7) == c, source, -1)).astype(BF16)
        parents = mm(local, spread).astype(BF16)
        by_real += mm(down[0, c, 0], parents)
        by_imag += mm(down[0, c, 1], parents)
    out[0] = fine_near[0] + (by_real[:, :FINE] - by_imag[:, FINE:])
    out[1] = fine_near[1] + (by_real[:, FINE:] + by_imag[:, :FINE])


def shape(dims, dtype):
    return jax.ShapeDtypeStruct(dims, dtype)


VMEM = pl.BlockSpec(memory_space=pltpu.VMEM)
SMEM = pl.BlockSpec(memory_space=pltpu.SMEM)
ANY = pl.BlockSpec(memory_space=pl.ANY)
INTERPRET = False


def call(kernel, ins, outs, scratch, flops, limit=40):
    return pl.pallas_call(
        kernel,
        in_specs=ins,
        out_specs=[VMEM] * len(outs),
        out_shape=outs,
        scratch_shapes=scratch,
        compiler_params=pltpu.CompilerParams(vmem_limit_bytes=limit << 20),
        cost_estimate=pl.CostEstimate(flops=flops, bytes_accessed=8 << 20, transcendentals=0),
        interpret=INTERPRET,
    )


def body(
    check_field, to_equiv, upward_ops, downward_ops, transfer_ops, list_fine, list_mid, list_low, list_top
):
    axes = ("row", "col")
    rows, cols = lax.axis_size("row"), lax.axis_size("col")
    count = rows * cols
    position = lax.axis_index(axes).astype(jnp.int32).reshape(1)
    own_col = lax.axis_index("col").astype(jnp.int32).reshape(1)
    octant_ops = (2, SIZE, SIZE)
    to_left, to_right, top = call(
        up_kernel,
        [SMEM, VMEM, VMEM, ANY],
        [shape((2 * SIZE, 384), BF16), shape((2 * SIZE, 384), BF16), shape((2, 256), F32)],
        [
            pltpu.VMEM((3, OCTANTS) + octant_ops, BF16),
            pltpu.VMEM(octant_ops, BF16),
            pltpu.SemaphoreType.DMA((4,)),
        ],
        4 << 30,
    )(own_col, check_field, to_equiv, upward_ops)
    from_left = lax.ppermute(to_right, axes, [(i, (i + 1) % count) for i in range(count)])
    from_right = lax.ppermute(to_left, axes, [(i, (i - 1) % count) for i in range(count)])
    tops = gather_top(top)
    fine, mid, low = call(
        near_kernel,
        [SMEM] + [VMEM] * 7 + [ANY],
        [shape((2, SIZE, FINE), F32), shape((SIZE, 128), F32), shape((SIZE, 128), F32)],
        [
            pltpu.VMEM((2 * SIZE, 1024), BF16),
            pltpu.VMEM((3, ENTRIES) + octant_ops, BF16),
            pltpu.SemaphoreType.DMA((3,)),
        ],
        30 << 30,
    )(position, from_left, from_right, to_left, to_right, list_fine.T, list_mid.T, list_low.T, transfer_ops)
    own_list = lax.dynamic_slice_in_dim(list_top, lax.axis_index("row"), 1, 0)
    (far,) = call(
        down_kernel,
        [SMEM] + [VMEM] * 5 + [ANY, ANY],
        [shape((2, SIZE, FINE), F32)],
        [
            pltpu.VMEM((ENTRIES,) + octant_ops, BF16),
            pltpu.VMEM((3, OCTANTS) + octant_ops, BF16),
            pltpu.VMEM(octant_ops, BF16),
            pltpu.SemaphoreType.DMA((5,)),
        ],
        8 << 30,
    )(own_col, tops, own_list, fine, mid, low, transfer_ops, downward_ops)
    return far


def gather_top(top):
    total = lax.psum(top, "col").astype(BF16)
    return jnp.transpose(lax.all_gather(total, "row", axis=0), (1, 0, 2)).astype(F32)


def solution(mesh):
    split = P(None, None, ("row", "col"))
    lists = P(("row", "col"), None)
    return jax.shard_map(
        body,
        mesh=mesh,
        in_specs=(split, P(), P(), P(), P(), lists, lists, lists, P()),
        out_specs=split,
        check_vma=False,
    )
```

time: 275 us -> 90.5 us (0.33)
  the two profiles are of different devices: /device:TPU:2 before, /device:TPU:1 now
where the time goes in v1:
time: 90.5 us; the launch traced here: 90.3 us
  blocking collectives  41.9 us (46%)
  Pallas kernels  32.6 us (36%)
  local copies, waits for them, and re-layouts  8.37 us (9%)
  starting transfers between devices  7.15 us (8%)
    all_gather x1, blocking collectives, gather_top(): lax.all_gather(total, 'row', axis=0)  29.7 us
    pallas_call x1, Pallas kernels, body(): call(near_kernel, [SMEM] + [VMEM] * 7 + [ANY], [shape((2, SIZE, FINE), F3...  19.5 us
    psum x1, blocking collectives, gather_top(): total = lax.psum(top, 'col').astype(BF16)  12.2 us
    pallas_call x1, Pallas kernels, body(): call(down_kernel, [SMEM] + [VMEM] * 5 + [ANY, ANY], [shape((2, SIZE, FINE...  8.42 us
    unnamed x20, local copies, waits for them, and re-layouts  8.3 us
    pallas_call x1, Pallas kernels, body(): call(up_kernel, [SMEM, VMEM, VMEM, ANY], [shape((2 * SIZE, 384), BF16), s...  4.65 us
    ppermute x1, starting transfers between devices, body(): lax.ppermute(to_left, axes, [(i, (i - 1) % count) for i in range(count)])  4.61 us
    ppermute x1, starting transfers between devices, body(): lax.ppermute(to_right, axes, [(i, (i + 1) % count) for i in range(count)])  2.54 us
  transfers between devices with their start and end apart: 2, of which 0 were waited for; matrix products, arithmetic and copies ran while one was open for 0% of the time, Pallas kernels for 0%

profile of v1, /device:TPU:1, one launch (start us, length us, event | category | flops | bytes accessed | tf_op | source)
XLA Modules:
  0.0 90.3 jit_solution(12250334950240241471)
XLA Ops:
  0.0 0.0 copy-start
  0.0 0.0 copy-start.2
  0.0 2.4 %copy-done.2 = bf16[4,8,2,152,152]{4,3,2,1,0:T(8,128)(2,1)S(1)} copy-done((bf16[4,8,2,152,152]{4,3,2,1,0:T(8,128)(2,1)S(1)}, bf16[4,8,2,152,152]{4,3,2,1,0:T(8,128)(2,1)}, u32[]{:S(2)}) %copy-start.2) | copy-done | bytes 2957336
  2.4 0.0 copy-start.4
  2.4 1.0 %copy-done.4 = bf16[2,152,512]{2,1,0:T(8,128)(2,1)S(1)} copy-done((bf16[2,152,512]{2,1,0:T(8,128)(2,1)S(1)}, bf16[2,152,512]{2,1,0:T(8,128)(2,1)}, u32[]{:S(2)}) %copy-start.4) | copy-done | bytes 311320
  3.4 0.0 copy-start.5
  3.4 0.9 %copy-done.5 = bf16[2,152,152]{2,1,0:T(8,128)(2,1)S(1)} copy-done((bf16[2,152,152]{2,1,0:T(8,128)(2,1)S(1)}, bf16[2,152,152]{2,1,0:T(8,128)(2,1)}, u32[]{:S(2)}) %copy-start.5) | copy-done | bytes 92440
  4.3 0.0 copy-start.8
  4.3 0.0 copy-start.6
  4.3 0.0 copy-start.7
  4.3 4.6 %shard_map.91 = (bf16[304,384]{1,0:T(8,128)(2,1)S(1)}, bf16[304,384]{1,0:T(8,128)(2,1)S(1)}, f32[2,256]{1,0:T(2,128)S(1)}) custom-call(s32[1]{0:T(128)} %bitcast.col_ref, bf16[2,152,512]{2,1,0:T(8,128)(2,1)S(1)} %copy-done.4, bf16[2,152,152]{2,1,0:T(8,128)(2,1)S(1)} %copy-done.5, bf16[4,8,2,152,152]{4,3,2,1,0:T(8,128)(2,1)S(1)} %copy-done.2), custom_call_target="tpu_custom_call" | custom-call | flops 4294967296 | bytes 8388608 | tf_op jit(solution)/shard_map/pallas_call | solution.py:261
  9.0 2.5 %collective-permute-start = (bf16[304,384]{1,0:T(8,128)(2,1)S(1)}, bf16[304,384]{1,0:T(8,128)(2,1)S(1)}, u32[]{:S(2)}, u32[]{:S(2)}) collective-permute-start(bf16[304,384]{1,0:T(8,128)(2,1)S(1)} %get-tuple-element.12.to_right), channel_id=1, source_target_pairs={{0,1},{1,2},{2,3},{3,4},{4,5},{5,6},{6,7},{7,8},{8,9},{9,10},{10,1... | collective-permute-start | bytes 700424 | tf_op jit(solution)/shard_map/ppermute | solution.py:272
  11.5 4.6 %collective-permute-start.1 = (bf16[304,384]{1,0:T(8,128)(2,1)S(1)}, bf16[304,384]{1,0:T(8,128)(2,1)S(1)}, u32[]{:S(2)}, u32[]{:S(2)}) collective-permute-start(bf16[304,384]{1,0:T(8,128)(2,1)S(1)} %get-tuple-element.13.to_left), channel_id=1, source_target_pairs={{0,255},{1,0},{2,1},{3,2},{4,3},{5,4},{6,5},{7,6},{8,7},{9,8},{10,... | collective-permute-start | bytes 700424 | tf_op jit(solution)/shard_map/ppermute | solution.py:273
  16.1 0.0 copy-done.8
  16.1 0.1 copy.17
  16.2 0.0 copy-done
  16.2 0.1 constant_dynamic-slice_fusion
  16.3 0.1 copy.18.own_list
  16.4 12.2 %psum.7 = bf16[2,256]{1,0:T(2,128)(2,1)S(1)} all-reduce(f32[2,256]{1,0:T(2,128)S(1)} %get-tuple-element.11), channel_id=1, replica_groups=mesh['row'=32,'col'=8] {'col'}, use_global_device_ids=true, to_apply=%region_0.0 | all-reduce | flops 512 | bytes 3072 | tf_op jit(solution)/shard_map/psum | solution.py:303
  28.6 29.7 %all-gather.1 = bf16[32,2,256]{2,1,0:T(2,128)(2,1)S(1)} all-gather(bf16[1,2,256]{2,1,0:T(2,128)(2,1)S(1)} %bitcast.13), channel_id=2, replica_groups=mesh['row'=32,'col'=8] {'row'}, dimensions={0}, use_global_device_ids=true | all-gather | bytes 33792 | tf_op jit(solution)/shard_map/all_gather | solution.py:304
  58.3 0.0 collective-permute-done.from_left
  58.3 0.0 collective-permute-done.1.from_right
  58.3 0.0 copy-done.6
  58.3 0.0 copy-done.7
  58.3 0.0 copy-start.1
  58.3 3.8 %copy-done.1 = bf16[4,16,2,152,152]{4,3,2,1,0:T(8,128)(2,1)S(1)} copy-done((bf16[4,16,2,152,152]{4,3,2,1,0:T(8,128)(2,1)S(1)}, bf16[4,16,2,152,152]{4,3,2,1,0:T(8,128)(2,1)}, u32[]{:S(2)}) %copy-start.1) | copy-done | bytes 5914648
  62.1 0.0 copy-start.3
  62.1 19.5 %shard_map.92 = (f32[2,152,512]{2,1,0:T(8,128)S(1)}, f32[152,128]{1,0:T(8,128)S(1)}, f32[152,128]{1,0:T(8,128)S(1)}) custom-call(s32[1]{0:T(128)} %bitcast.3.start_ref, bf16[304,384]{1,0:T(8,128)(2,1)S(1)} %collective-permute-done.from_left, bf16[304,384]{1,0:T(8,128)(2,1)S(1)} %collective-permute-done.1.from_right, ...), custom_call_target="tpu_custom_call" | custom-call | flops 32212254720 | bytes 8388608 | tf_op jit(solution)/shard_map/pallas_call | solution.py:275
  81.7 0.0 copy-done.3
  81.7 8.4 %shard_map.93 = f32[2,152,512]{2,1,0:T(8,128)} custom-call(s32[1]{0:T(128)} %bitcast.col_ref, f32[2,32,256]{2,1,0:T(8,128)S(1)} %convert_bitcast_fusion.tops, s32[1,16]{1,0:T(1,128)S(1)} %copy.18.own_list, f32[2,152,512]{2,1,0:T(8,128)S(1)} %get-tuple-element.14.fine_near, f32[152,128]{1,0:T(8,128)S(1)} %get-tuple-element.15.mid_near, ...), custom_call_target="tpu_custom_call" | custom-call | flops 8589934592 | bytes 8388608 | tf_op jit(solution)/shard_map/pallas_call | solution.py:287
  (1 shorter events, 0.0 us)
Async XLA Ops:
  0.0 16.2 %copy-start = (s32[32,16]{0,1:T(8,128)S(1)}, s32[32,16]{0,1:T(8,128)}, u32[]{:S(2)}) copy-start(s32[32,16]{0,1:T(8,128)} %param.17) | copy-start | bytes 6148
  0.0 2.4 %copy-start.2 = (bf16[4,8,2,152,152]{4,3,2,1,0:T(8,128)(2,1)S(1)}, bf16[4,8,2,152,152]{4,3,2,1,0:T(8,128)(2,1)}, u32[]{:S(2)}) copy-start(bf16[4,8,2,152,152]{4,3,2,1,0:T(8,128)(2,1)} %ops_hbm.2) | copy-start | bytes 8871940
  2.4 1.0 %copy-start.4 = (bf16[2,152,512]{2,1,0:T(8,128)(2,1)S(1)}, bf16[2,152,512]{2,1,0:T(8,128)(2,1)}, u32[]{:S(2)}) copy-start(bf16[2,152,512]{2,1,0:T(8,128)(2,1)} %check.1) | copy-start | bytes 933892
  3.4 0.9 %copy-start.5 = (bf16[2,152,152]{2,1,0:T(8,128)(2,1)S(1)}, bf16[2,152,152]{2,1,0:T(8,128)(2,1)}, u32[]{:S(2)}) copy-start(bf16[2,152,152]{2,1,0:T(8,128)(2,1)} %to_equiv.1) | copy-start | bytes 277252
  4.3 11.8 %copy-start.8 = (s32[8,16]{1,0:T(8,128)S(1)}, s32[8,16]{1,0:T(8,128)}, u32[]{:S(2)}) copy-start(s32[8,16]{1,0:T(8,128)} %param.16) | copy-start | bytes 1540
  4.3 54.0 %copy-start.6 = (s32[512,16]{0,1:T(8,128)S(1)}, s32[512,16]{0,1:T(8,128)}, u32[]{:S(2)}) copy-start(s32[512,16]{0,1:T(8,128)} %param.14) | copy-start | bytes 98308
  4.3 54.0 %copy-start.7 = (s32[64,16]{0,1:T(8,128)S(1)}, s32[64,16]{0,1:T(8,128)}, u32[]{:S(2)}) copy-start(s32[64,16]{0,1:T(8,128)} %param.15) | copy-start | bytes 12292
  9.0 49.3 %collective-permute-start = (bf16[304,384]{1,0:T(8,128)(2,1)S(1)}, bf16[304,384]{1,0:T(8,128)(2,1)S(1)}, u32[]{:S(2)}, u32[]{:S(2)}) collective-permute-start(bf16[304,384]{1,0:T(8,128)(2,1)S(1)} %get-tuple-element.12.to_right), channel_id=1, source_target_pairs={{0,1},{1,2},{2,3},{3,4},{4,5},{5,6},{6,7},{7,8},{8,9},{9,10},{10,1... | collective-permute-start | bytes 700424 | tf_op jit(solution)/shard_map/ppermute | solution.py:272
  11.5 46.8 %collective-permute-start.1 = (bf16[304,384]{1,0:T(8,128)(2,1)S(1)}, bf16[304,384]{1,0:T(8,128)(2,1)S(1)}, u32[]{:S(2)}, u32[]{:S(2)}) collective-permute-start(bf16[304,384]{1,0:T(8,128)(2,1)S(1)} %get-tuple-element.13.to_left), channel_id=1, source_target_pairs={{0,255},{1,0},{2,1},{3,2},{4,3},{5,4},{6,5},{7,6},{8,7},{9,8},{10,... | collective-permute-start | bytes 700424 | tf_op jit(solution)/shard_map/ppermute | solution.py:273
  58.3 3.8 %copy-start.1 = (bf16[4,16,2,152,152]{4,3,2,1,0:T(8,128)(2,1)S(1)}, bf16[4,16,2,152,152]{4,3,2,1,0:T(8,128)(2,1)}, u32[]{:S(2)}) copy-start(bf16[4,16,2,152,152]{4,3,2,1,0:T(8,128)(2,1)} %transfer_hbm.1) | copy-start | bytes 17743876
  62.1 19.5 %copy-start.3 = (bf16[4,8,2,152,152]{4,3,2,1,0:T(8,128)(2,1)S(1)}, bf16[4,8,2,152,152]{4,3,2,1,0:T(8,128)(2,1)}, u32[]{:S(2)}) copy-start(bf16[4,8,2,152,152]{4,3,2,1,0:T(8,128)(2,1)} %down_hbm.1) | copy-start | bytes 8871940

commit v2 on v1

--- a/solution.py
+++ b/solution.py
@@ -92,8 +92,8 @@
     copies[3].wait()
     part = combine(mm(own_op[0], packed[2]), mm(own_op[1], packed[2]))
     flat = jnp.transpose(jnp.concatenate([part, jnp.zeros((104, 128), F32)], axis=0))
-    top[0:1, :] = flat[0:1, :]
-    top[1:2, :] = flat[HALF : HALF + 1, :]
+    top[:, :256] = flat[0:1, :]
+    top[:, 256:] = flat[HALF : HALF + 1, :]
 
 
 def translate_packed(around, codes, targets, ops_pair):
@@ -107,22 +107,18 @@
     return combine(by_real, by_imag)
 
 
-def near_kernel(
-    start_ref, from_left, from_right, to_left, to_right, fine_t, mid_t, low_t, ops_hbm,
-    fine_out, mid_out, low_out, around, ops, sems,
+def small_kernel(
+    start_ref, ride, from_left, from_right, to_left, to_right, mid_t, low_t, ops_hbm,
+    ride_out, mid_out, low_out, ops, sems,
 ):
-    copies = [
-        pltpu.make_async_copy(ops_hbm.at[level], ops.at[level], sems.at[level])
-        for level in range(3)
-    ]
-    for level in (2, 1, 0):
-        copies[level].start()
+    ride_out[...] = ride[...]
+    copies = {
+        level: pltpu.make_async_copy(ops_hbm.at[level], ops.at[level - 1], sems.at[level - 1])
+        for level in (2, 1)
+    }
+    for copy in copies.values():
+        copy.start()
     position = start_ref[0]
-    around[:, 0:REACH] = from_left[:, :REACH]
-    around[:, REACH : 2 * REACH] = to_left[:, :REACH]
-    around[:, 2 * REACH : 3 * REACH] = to_right[:, :REACH]
-    around[:, 3 * REACH :] = from_right[:, :REACH]
-
     lows = [ref[SIZE:, REACH:].astype(F32) for ref in (to_left, from_left, from_right)]
     low_all = (lows[0] + pltpu.roll(lows[1], 8, 1) + pltpu.roll(lows[2], 16, 1)).astype(BF16)
     row = iota((128, 128), 0)
@@ -133,7 +129,7 @@
     pad = jnp.full((ENTRIES, HALF - 8), -(1 << 19), jnp.int32)
     targets = jnp.concatenate([low_index, pad, low_index + 1024, pad], axis=1)
     copies[2].wait()
-    low_out[...] = translate_packed(low_all, codes, targets, ops.at[2])
+    low_out[...] = translate_packed(low_all, codes, targets, ops.at[1])
 
     mid_all = jnp.concatenate(
         [from_left[:SIZE, REACH:], to_left[:SIZE, REACH:], from_right[:SIZE, REACH:]], axis=1
@@ -143,28 +139,35 @@
     mid_index = mid_t[...] - position * HALF
     targets = jnp.concatenate([mid_index, mid_index + 1024], axis=1)
     copies[1].wait()
-    mid_out[...] = translate_packed(mid_all, codes, targets, ops.at[1])
-
-    copies[0].wait()
+    mid_out[...] = translate_packed(mid_all, codes, targets, ops.at[0])
+
+
+def fine_kernel(
+    half, start_ref, ride, before, first, second, fine_t, ops_hbm, ride_out, out, window, ops, sem
+):
+    ride_out[...] = ride[...]
+    copy = pltpu.make_async_copy(ops_hbm.at[0], ops, sem)
+    copy.start()
+    window[:, :REACH] = before[:, :REACH]
+    window[:, REACH : 2 * REACH] = first[:, :REACH]
+    window[:, 2 * REACH :] = second[:, :REACH]
+    index = fine_t[...] - (start_ref[0] * FINE + (half - 1) * REACH)
     row = iota((3 * REACH, REACH), 0)
-    for half in range(2):
-        start = half * REACH
-        window = around[:, start : start + 3 * REACH]
-        index = fine_t[:, start : start + REACH] - (position * FINE - REACH + start)
-        by_real = jnp.zeros((SIZE, FINE), F32)
-        by_imag = jnp.zeros((SIZE, FINE), F32)
-        for k in range(ENTRIES):
-            select = (row == index[k : k + 1, :]).astype(BF16)
-            picked = mm(window, select)
-            picked = jnp.concatenate([picked[:SIZE], picked[SIZE:]], axis=1).astype(BF16)
-            by_real += mm(ops[0, k, 0], picked)
-            by_imag += mm(ops[0, k, 1], picked)
-        fine_out[0, :, start : start + REACH] = by_real[:, :REACH] - by_imag[:, REACH:]
-        fine_out[1, :, start : start + REACH] = by_real[:, REACH:] + by_imag[:, :REACH]
+    by_real = jnp.zeros((SIZE, FINE), F32)
+    by_imag = jnp.zeros((SIZE, FINE), F32)
+    copy.wait()
+    for k in range(ENTRIES):
+        select = (row == index[k : k + 1, :]).astype(BF16)
+        picked = mm(window[...], select)
+        picked = jnp.concatenate([picked[:SIZE], picked[SIZE:]], axis=1).astype(BF16)
+        by_real += mm(ops[k, 0], picked)
+        by_imag += mm(ops[k, 1], picked)
+    out[0] = by_real[:, :REACH] - by_imag[:, REACH:]
+    out[1] = by_real[:, REACH:] + by_imag[:, :REACH]
 
 
 def down_kernel(
-    col_ref, tops, own_list, fine_near, mid_near, low_near, transfer_hbm, down_hbm, out,
+    col_ref, own_ref, tops, own_list, fine_near_a, fine_near_b, mid_near, low_near, transfer_hbm, down_hbm, out,
     transfer, down, own_op, sems,
 ):
     copies = [
@@ -176,12 +179,14 @@
     for level in (4, 3, 2, 1, 0):
         copies[level].start()
 
-    gap = jnp.zeros((HALF - tops.shape[1], 256), F32)
-    rows = jnp.concatenate([tops[0], gap, tops[1], gap], axis=0)
+    gap = jnp.zeros((HALF - tops.shape[0], 256), F32)
+    wide = tops[...].astype(F32)
+    rows = jnp.concatenate([wide[:, :256], gap, wide[:, 256:], gap], axis=0)
     dense = jnp.transpose(rows)[:SIZE].astype(BF16)
     row = iota((128, 128), 0)
     lane = iota((128, 128), 1)
-    listed = own_list[...]
+    listed = own_list[...] ^ own_ref[0]
+    listed = listed ^ ((listed >> 1) & 0b01010)
     pad = jnp.full((1, HALF - ENTRIES), -(1 << 19), jnp.int32)
     wanted = jnp.concatenate([listed, pad, listed + HALF, pad], axis=1)
     picked = mm(dense, (row == wanted).astype(BF16))
@@ -222,8 +227,12 @@
         parents = mm(local, spread).astype(BF16)
         by_real += mm(down[0, c, 0], parents)
         by_imag += mm(down[0, c, 1], parents)
-    out[0] = fine_near[0] + (by_real[:, :FINE] - by_imag[:, FINE:])
-    out[1] = fine_near[1] + (by_real[:, FINE:] + by_imag[:, :FINE])
+    real = by_real[:, :FINE] - by_imag[:, FINE:]
+    imag = by_real[:, FINE:] + by_imag[:, :FINE]
+    out[0, :, :REACH] = fine_near_a[0] + real[:, :REACH]
+    out[0, :, REACH:] = fine_near_b[0] + real[:, REACH:]
+    out[1, :, :REACH] = fine_near_a[1] + imag[:, :REACH]
+    out[1, :, REACH:] = fine_near_b[1] + imag[:, REACH:]
 
 
 def shape(dims, dtype):
@@ -261,32 +270,62 @@
     to_left, to_right, top = call(
         up_kernel,
         [SMEM, VMEM, VMEM, ANY],
-        [shape((2 * SIZE, 384), BF16), shape((2 * SIZE, 384), BF16), shape((2, 256), F32)],
+        [shape((2 * SIZE, 384), BF16), shape((2 * SIZE, 384), BF16), shape((1, 512), F32)],
         [
             pltpu.VMEM((3, OCTANTS) + octant_ops, BF16),
             pltpu.VMEM(octant_ops, BF16),
             pltpu.SemaphoreType.DMA((4,)),
         ],
         4 << 30,
+        60,
     )(own_col, check_field, to_equiv, upward_ops)
     from_left = lax.ppermute(to_right, axes, [(i, (i + 1) % count) for i in range(count)])
     from_right = lax.ppermute(to_left, axes, [(i, (i - 1) % count) for i in range(count)])
-    tops = gather_top(top)
-    fine, mid, low = call(
-        near_kernel,
-        [SMEM] + [VMEM] * 7 + [ANY],
-        [shape((2, SIZE, FINE), F32), shape((SIZE, 128), F32), shape((SIZE, 128), F32)],
-        [
-            pltpu.VMEM((2 * SIZE, 1024), BF16),
-            pltpu.VMEM((3, ENTRIES) + octant_ops, BF16),
-            pltpu.SemaphoreType.DMA((3,)),
-        ],
-        30 << 30,
-    )(position, from_left, from_right, to_left, to_right, list_fine.T, list_mid.T, list_low.T, transfer_ops)
+    def small(ride):
+        return call(
+            small_kernel,
+            [SMEM] + [VMEM] * 7 + [ANY],
+            [shape(ride.shape, BF16), shape((SIZE, 128), F32), shape((SIZE, 128), F32)],
+            [pltpu.VMEM((2, ENTRIES) + octant_ops, BF16), pltpu.SemaphoreType.DMA((2,))],
+            4 << 30,
+        )(position, ride, from_left, from_right, to_left, to_right, list_mid.T, list_low.T, transfer_ops)
+
+    def fine(half, ride):
+        around = (from_left, to_left, to_right) if half == 0 else (to_left, to_right, from_right)
+        return call(
+            functools.partial(fine_kernel, half),
+            [SMEM] + [VMEM] * 5 + [ANY],
+            [shape(ride.shape, BF16), shape((2, SIZE, REACH), F32)],
+            [
+                pltpu.VMEM((2 * SIZE, 3 * REACH), BF16),
+                pltpu.VMEM((ENTRIES,) + octant_ops, BF16),
+                pltpu.SemaphoreType.DMA(()),
+            ],
+            10 << 30,
+        )(position, ride, *around, list_fine.T[:, half * REACH : (half + 1) * REACH], transfer_ops)
+
+    def swap(x, axis, mask):
+        return lax.ppermute(x, axis, [(i, i ^ mask) for i in range(lax.axis_size(axis))])
+
+    total = top
+    for mask in (1, 2, 6):
+        total = total + swap(total, "col", mask)
+    tops = total.astype(BF16)
+    work = [small, functools.partial(fine, 0), functools.partial(fine, 1)]
+    near = []
+    for step, mask in enumerate((1, 2, 6, 8, 24)):
+        other = swap(tops, "row", mask) if mask < rows else None
+        if step < len(work):
+            tops, *parts = work[step](tops)
+            near += parts
+        if other is not None:
+            tops = jnp.concatenate([tops, other], axis=0)
+    mid, low, fine_a, fine_b = near
+    own_row = lax.axis_index("row").astype(jnp.int32).reshape(1)
     own_list = lax.dynamic_slice_in_dim(list_top, lax.axis_index("row"), 1, 0)
     (far,) = call(
         down_kernel,
-        [SMEM] + [VMEM] * 5 + [ANY, ANY],
+        [SMEM, SMEM] + [VMEM] * 6 + [ANY, ANY],
         [shape((2, SIZE, FINE), F32)],
         [
             pltpu.VMEM((ENTRIES,) + octant_ops, BF16),
@@ -295,13 +334,8 @@
             pltpu.SemaphoreType.DMA((5,)),
         ],
         8 << 30,
-    )(own_col, tops, own_list, fine, mid, low, transfer_ops, downward_ops)
+    )(own_col, own_row, tops, own_list, fine_a, fine_b, mid, low, transfer_ops, downward_ops)
     return far
-
-
-def gather_top(top):
-    total = lax.psum(top, "col").astype(BF16)
-    return jnp.transpose(lax.all_gather(total, "row", axis=0), (1, 0, 2)).astype(F32)
 
 
 def solution(mesh):

time: 90.5 us -> 74.1 us (0.82)
  the two profiles are of different devices: /device:TPU:1 before, /device:TPU:2 now
where the time goes in v2:
time: 74.1 us; the launch traced here: 73.3 us
  Pallas kernels  34.1 us (46%)
  starting transfers between devices  20 us (27%)
  waiting for transfers between devices  9.79 us (13%)
  local copies, waits for them, and re-layouts  8.36 us (11%)
    ppermute x8, starting transfers between devices, swap(): lax.ppermute(x, axis, [(i, i ^ mask) for i in range(lax.axis_size(axis))])  16.1 us
    pallas_call x2, Pallas kernels, fine(): call(functools.partial(fine_kernel, half), [SMEM] + [VMEM] * 5 + [ANY], [...  14.2 us
    ppermute x8, waiting for transfers between devices, swap(): lax.ppermute(x, axis, [(i, i ^ mask) for i in range(lax.axis_size(axis))])  9.79 us
    pallas_call x1, Pallas kernels, body(): call(down_kernel, [SMEM, SMEM] + [VMEM] * 6 + [ANY, ANY], [shape((2, SIZE...  8.42 us
    unnamed x20, local copies, waits for them, and re-layouts  8.28 us
    pallas_call x1, Pallas kernels, small(): call(small_kernel, [SMEM] + [VMEM] * 7 + [ANY], [shape(ride.shape, BF16),...  5.93 us
    pallas_call x1, Pallas kernels, body(): call(up_kernel, [SMEM, VMEM, VMEM, ANY], [shape((2 * SIZE, 384), BF16), s...  5.56 us
    ppermute x1, starting transfers between devices, body(): lax.ppermute(to_left, axes, [(i, (i - 1) % count) for i in range(count)])  1.93 us
  transfers between devices with their start and end apart: 10, of which 4 were waited for; matrix products, arithmetic and copies ran while one was open for 0% of the time, Pallas kernels for 27%

profile of v2, /device:TPU:2, one launch (start us, length us, event | category | flops | bytes accessed | tf_op | source)
XLA Modules:
  0.0 73.3 jit_solution(3036805445441423113)
XLA Ops:
  0.0 0.0 copy-start
  0.0 0.0 copy-start.7
  0.0 0.0 copy-start.8
  0.0 0.0 copy-start.6
  0.0 5.6 %shard_map.91 = (bf16[304,384]{1,0:T(8,128)(2,1)}, bf16[304,384]{1,0:T(8,128)(2,1)}, f32[1,512]{1,0:T(1,128)}) custom-call(s32[1]{0:T(128)} %bitcast.col_ref, bf16[2,152,512]{2,1,0:T(8,128)(2,1)} %check.1, bf16[2,152,152]{2,1,0:T(8,128)(2,1)} %to_equiv.1, bf16[4,8,2,152,152]{4,3,2,1,0:T(8,128)(2,1)} %ops_hbm.4), custom_call_target="tpu_custom_call" | custom-call | flops 4294967296 | bytes 8388608 | tf_op jit(solution)/shard_map/pallas_call | solution.py:270
  5.6 2.0 %collective-permute-start = (f32[1,512]{1,0:T(1,128)}, f32[1,512]{1,0:T(1,128)S(1)}, u32[]{:S(2)}, u32[]{:S(2)}) collective-permute-start(f32[1,512]{1,0:T(1,128)} %get-tuple-element.15), channel_id=1, source_target_pairs={{0,1},{1,0},{2,3},{3,2},{4,5},{5,4},{6,7},{7,6},{8,9},{9,8},{10,11... | collective-permute-start | bytes 6152 | tf_op jit(solution)/shard_map/ppermute | solution.py:308
  7.6 1.9 %collective-permute-done = f32[1,512]{1,0:T(1,128)S(1)} collective-permute-done((f32[1,512]{1,0:T(1,128)}, f32[1,512]{1,0:T(1,128)S(1)}, u32[]{:S(2)}, u32[]{:S(2)}) %collective-permute-start) | collective-permute-done | bytes 2080 | tf_op jit(solution)/shard_map/ppermute | solution.py:308
  9.5 0.7 add.16
  10.2 3.3 %collective-permute-start.1 = (f32[1,512]{1,0:T(1,128)S(1)}, f32[1,512]{1,0:T(1,128)S(1)}, u32[]{:S(2)}, u32[]{:S(2)}) collective-permute-start(f32[1,512]{1,0:T(1,128)S(1)} %add.16), channel_id=1, source_target_pairs={{0,2},{1,3},{2,0},{3,1},{4,6},{5,7},{6,4},{7,5},{8,10},{9,11},{10,... | collective-permute-start | bytes 6152 | tf_op jit(solution)/shard_map/ppermute | solution.py:308
  13.4 1.9 %collective-permute-start.3 = (bf16[304,384]{1,0:T(8,128)(2,1)}, bf16[304,384]{1,0:T(8,128)(2,1)S(1)}, u32[]{:S(2)}, u32[]{:S(2)}) collective-permute-start(bf16[304,384]{1,0:T(8,128)(2,1)} %get-tuple-element.16.to_right.second.first), channel_id=1, source_target_pairs={{0,1},{1,2},{2,3},{3,4},{4,5},{5,6},{6,7},{7,8},{8,9},{9,10},{10,1... | collective-permute-start | bytes 700424 | tf_op jit(solution)/shard_map/ppermute | solution.py:282
  15.3 1.9 %collective-permute-start.4 = (bf16[304,384]{1,0:T(8,128)(2,1)}, bf16[304,384]{1,0:T(8,128)(2,1)S(1)}, u32[]{:S(2)}, u32[]{:S(2)}) collective-permute-start(bf16[304,384]{1,0:T(8,128)(2,1)} %get-tuple-element.17.to_left.first.before), channel_id=1, source_target_pairs={{0,255},{1,0},{2,1},{3,2},{4,3},{5,4},{6,5},{7,6},{8,7},{9,8},{10,... | collective-permute-start | bytes 700424 | tf_op jit(solution)/shard_map/ppermute | solution.py:283
  17.3 0.0 collective-permute-done.1
  17.3 3.7 %collective-permute-start.2 = (f32[1,512]{1,0:T(1,128)S(1)}, f32[1,512]{1,0:T(1,128)S(1)}, u32[]{:S(2)}, u32[]{:S(2)}) collective-permute-start(f32[1,512]{1,0:T(1,128)S(1)} %add.17), channel_id=1, source_target_pairs={{0,6},{1,7},{2,4},{3,5},{4,2},{5,3},{6,0},{7,1},{8,14},{9,15},{10,... | collective-permute-start | bytes 6152 | tf_op jit(solution)/shard_map/ppermute | solution.py:308
  21.0 0.0 copy-done.7
  21.0 0.0 copy-done.8
  21.0 0.1 copy.10
  21.1 2.3 %collective-permute-done.2 = f32[1,512]{1,0:T(1,128)S(1)} collective-permute-done((f32[1,512]{1,0:T(1,128)S(1)}, f32[1,512]{1,0:T(1,128)S(1)}, u32[]{:S(2)}, u32[]{:S(2)}) %collective-permute-start.2) | collective-permute-done | bytes 2080 | tf_op jit(solution)/shard_map/ppermute | solution.py:308
  23.4 0.0 collective-permute-start.5
  23.4 0.0 collective-permute-done.3.from_left.before
  23.4 0.0 collective-permute-done.4.from_right.second
  23.4 0.0 copy-done.6
  23.4 0.0 copy-start.1
  23.4 3.8 %copy-done.1 = bf16[4,16,2,152,152]{4,3,2,1,0:T(8,128)(2,1)S(1)} copy-done((bf16[4,16,2,152,152]{4,3,2,1,0:T(8,128)(2,1)S(1)}, bf16[4,16,2,152,152]{4,3,2,1,0:T(8,128)(2,1)}, u32[]{:S(2)}) %copy-start.1) | copy-done | bytes 5914648
  27.3 0.0 copy-start.4
  27.3 0.9 %copy-done.4 = bf16[304,384]{1,0:T(8,128)(2,1)S(1)} copy-done((bf16[304,384]{1,0:T(8,128)(2,1)S(1)}, bf16[304,384]{1,0:T(8,128)(2,1)}, u32[]{:S(2)}) %copy-start.4) | copy-done | bytes 233496
  28.2 0.0 copy-start.5
  28.2 0.9 %copy-done.5 = bf16[304,384]{1,0:T(8,128)(2,1)S(1)} copy-done((bf16[304,384]{1,0:T(8,128)(2,1)S(1)}, bf16[304,384]{1,0:T(8,128)(2,1)}, u32[]{:S(2)}) %copy-start.5) | copy-done | bytes 233496
  29.1 0.0 copy-start.2
  29.1 5.9 %shard_map.92 = (bf16[1,512]{1,0:T(2,128)(2,1)S(1)}, f32[152,128]{1,0:T(8,128)S(1)}, f32[152,128]{1,0:T(8,128)S(1)}) custom-call(s32[1]{0:T(128)} %bitcast.2.start_ref, bf16[1,512]{1,0:T(2,128)(2,1)S(1)} %add_convert_fusion.ride, bf16[304,384]{1,0:T(8,128)(2,1)S(1)} %collective-permute-done.3.from_left.before, ...), custom_call_target="tpu_custom_call" | custom-call | flops 4294967296 | bytes 8388608 | tf_op jit(solution)/shard_map/pallas_call | solution.py:285
  35.1 0.0 collective-permute-done.5
  35.1 3.8 %collective-permute-start.6 = (bf16[2,512]{1,0:T(2,128)(2,1)S(1)}, bf16[2,512]{1,0:T(2,128)(2,1)S(1)}, u32[]{:S(2)}, u32[]{:S(2)}) collective-permute-start(bf16[2,512]{1,0:T(2,128)(2,1)S(1)} %pad_maximum_fusion.4.ride), channel_id=1, source_target_pairs={{0,16},{8,24},{16,0},{24,8},{32,48},{40,56},{48,32},{56,40},{64,80... | collective-permute-start | bytes 6152 | tf_op jit(solution)/shard_map/ppermute | solution.py:308
  38.9 0.0 copy-done.2
  38.9 7.1 %shard_map.93 = (bf16[2,512]{1,0:T(2,128)(2,1)S(1)}, f32[2,152,256]{2,1,0:T(8,128)S(1)}) custom-call(s32[1]{0:T(128)} %bitcast.2.start_ref, bf16[2,512]{1,0:T(2,128)(2,1)S(1)} %pad_maximum_fusion.4.ride, bf16[304,384]{1,0:T(8,128)(2,1)S(1)} %collective-permute-done.3.from_left.before, bf16[304,384]{1,0:T(8,128)(2,1)S(1)} %copy-done.4, ...), custom_call_target="tpu_custom_call" | custom-call | flops 10737418240 | bytes 8388608 | tf_op jit(solution)/shard_map/pallas_call | solution.py:295
  46.0 0.0 collective-permute-done.6
  46.0 0.1 collective-permute-start.7
  46.1 7.1 %shard_map.94 = (bf16[4,512]{1,0:T(4,128)(2,1)S(1)}, f32[2,152,256]{2,1,0:T(8,128)S(1)}) custom-call(s32[1]{0:T(128)} %bitcast.2.start_ref, bf16[4,512]{1,0:T(4,128)(2,1)S(1)} %pad_maximum_fusion.3.ride, bf16[304,384]{1,0:T(8,128)(2,1)S(1)} %copy-done.4, bf16[304,384]{1,0:T(8,128)(2,1)S(1)} %copy-done.5, ...), custom_call_target="tpu_custom_call" | custom-call | flops 10737418240 | bytes 8388608 | tf_op jit(solution)/shard_map/pallas_call | solution.py:295
  53.2 0.0 collective-permute-done.7
  53.2 0.8 %collective-permute-start.8 = (bf16[8,512]{1,0:T(8,128)(2,1)S(1)}, bf16[8,512]{1,0:T(8,128)(2,1)S(1)}, u32[]{:S(2)}, u32[]{:S(2)}) collective-permute-start(bf16[8,512]{1,0:T(8,128)(2,1)S(1)} %pad_maximum_fusion.2), channel_id=1, source_target_pairs={{0,64},{8,72},{16,80},{24,88},{32,96},{40,104},{48,112},{56,120},{... | collective-permute-start | bytes 24584 | tf_op jit(solution)/shard_map/ppermute | solution.py:308
  54.0 2.9 %collective-permute-done.8 = bf16[8,512]{1,0:T(8,128)(2,1)S(1)} collective-permute-done((bf16[8,512]{1,0:T(8,128)(2,1)S(1)}, bf16[8,512]{1,0:T(8,128)(2,1)S(1)}, u32[]{:S(2)}, u32[]{:S(2)}) %collective-permute-start.8) | collective-permute-done | bytes 8224 | tf_op jit(solution)/shard_map/ppermute | solution.py:308
  57.0 2.5 %collective-permute-start.9 = (bf16[16,512]{1,0:T(8,128)(2,1)S(1)}, bf16[16,512]{1,0:T(8,128)(2,1)S(1)}, u32[]{:S(2)}, u32[]{:S(2)}) collective-permute-start(bf16[16,512]{1,0:T(8,128)(2,1)S(1)} %pad_maximum_fusion.1), channel_id=1, source_target_pairs={{0,192},{8,200},{16,208},{24,216},{32,224},{40,232},{48,240},{56,2... | collective-permute-start | bytes 49160 | tf_op jit(solution)/shard_map/ppermute | solution.py:308
  59.5 0.0 copy-done
  59.5 0.1 constant_dynamic-slice_fusion
  59.5 0.1 copy.12.own_list
  59.6 2.6 %collective-permute-done.9 = bf16[16,512]{1,0:T(8,128)(2,1)S(1)} collective-permute-done((bf16[16,512]{1,0:T(8,128)(2,1)S(1)}, bf16[16,512]{1,0:T(8,128)(2,1)S(1)}, u32[]{:S(2)}, u32[]{:S(2)}) %collective-permute-start.9) | collective-permute-done | bytes 16416 | tf_op jit(solution)/shard_map/ppermute | solution.py:308
  62.3 0.0 copy-start.3
  62.3 2.4 %copy-done.3 = bf16[4,8,2,152,152]{4,3,2,1,0:T(8,128)(2,1)S(1)} copy-done((bf16[4,8,2,152,152]{4,3,2,1,0:T(8,128)(2,1)S(1)}, bf16[4,8,2,152,152]{4,3,2,1,0:T(8,128)(2,1)}, u32[]{:S(2)}) %copy-start.3) | copy-done | bytes 2957336
  64.7 8.4 %shard_map.95 = f32[2,152,512]{2,1,0:T(8,128)} custom-call(s32[1]{0:T(128)} %bitcast.col_ref, s32[1]{0:T(128)} %bitcast.1.own_ref, bf16[32,512]{1,0:T(8,128)(2,1)S(1)} %pad_maximum_fusion.tops, s32[1,16]{1,0:T(1,128)S(1)} %copy.12.own_list, f32[2,152,256]{2,1,0:T(8,128)S(1)} %get-tuple-element.21.fine_near_a, ...), custom_call_target="tpu_custom_call" | custom-call | flops 8589934592 | bytes 8388608 | tf_op jit(solution)/shard_map/pallas_call | solution.py:326
  (8 shorter events, 0.1 us)
Async XLA Ops:
  0.0 59.5 %copy-start = (s32[32,16]{0,1:T(8,128)S(1)}, s32[32,16]{0,1:T(8,128)}, u32[]{:S(2)}) copy-start(s32[32,16]{0,1:T(8,128)} %param.17) | copy-start | bytes 6148
  0.0 21.0 %copy-start.7 = (s32[512,16]{0,1:T(8,128)S(1)}, s32[512,16]{0,1:T(8,128)}, u32[]{:S(2)}) copy-start(s32[512,16]{0,1:T(8,128)} %param.14) | copy-start | bytes 98308
  0.0 21.0 %copy-start.8 = (s32[8,16]{1,0:T(8,128)S(1)}, s32[8,16]{1,0:T(8,128)}, u32[]{:S(2)}) copy-start(s32[8,16]{1,0:T(8,128)} %param.16) | copy-start | bytes 1540
  0.0 23.4 %copy-start.6 = (s32[64,16]{0,1:T(8,128)S(1)}, s32[64,16]{0,1:T(8,128)}, u32[]{:S(2)}) copy-start(s32[64,16]{0,1:T(8,128)} %param.15) | copy-start | bytes 12292
  5.6 3.9 %collective-permute-start = (f32[1,512]{1,0:T(1,128)}, f32[1,512]{1,0:T(1,128)S(1)}, u32[]{:S(2)}, u32[]{:S(2)}) collective-permute-start(f32[1,512]{1,0:T(1,128)} %get-tuple-element.15), channel_id=1, source_target_pairs={{0,1},{1,0},{2,3},{3,2},{4,5},{5,4},{6,7},{7,6},{8,9},{9,8},{10,11... | collective-permute-start | bytes 6152 | tf_op jit(solution)/shard_map/ppermute | solution.py:308
  10.2 7.1 %collective-permute-start.1 = (f32[1,512]{1,0:T(1,128)S(1)}, f32[1,512]{1,0:T(1,128)S(1)}, u32[]{:S(2)}, u32[]{:S(2)}) collective-permute-start(f32[1,512]{1,0:T(1,128)S(1)} %add.16), channel_id=1, source_target_pairs={{0,2},{1,3},{2,0},{3,1},{4,6},{5,7},{6,4},{7,5},{8,10},{9,11},{10,... | collective-permute-start | bytes 6152 | tf_op jit(solution)/shard_map/ppermute | solution.py:308
  13.4 10.0 %collective-permute-start.3 = (bf16[304,384]{1,0:T(8,128)(2,1)}, bf16[304,384]{1,0:T(8,128)(2,1)S(1)}, u32[]{:S(2)}, u32[]{:S(2)}) collective-permute-start(bf16[304,384]{1,0:T(8,128)(2,1)} %get-tuple-element.16.to_right.second.first), channel_id=1, source_target_pairs={{0,1},{1,2},{2,3},{3,4},{4,5},{5,6},{6,7},{7,8},{8,9},{9,10},{10,1... | collective-permute-start | bytes 700424 | tf_op jit(solution)/shard_map/ppermute | solution.py:282
  15.3 8.1 %collective-permute-start.4 = (bf16[304,384]{1,0:T(8,128)(2,1)}, bf16[304,384]{1,0:T(8,128)(2,1)S(1)}, u32[]{:S(2)}, u32[]{:S(2)}) collective-permute-start(bf16[304,384]{1,0:T(8,128)(2,1)} %get-tuple-element.17.to_left.first.before), channel_id=1, source_target_pairs={{0,255},{1,0},{2,1},{3,2},{4,3},{5,4},{6,5},{7,6},{8,7},{9,8},{10,... | collective-permute-start | bytes 700424 | tf_op jit(solution)/shard_map/ppermute | solution.py:283
  17.3 6.1 %collective-permute-start.2 = (f32[1,512]{1,0:T(1,128)S(1)}, f32[1,512]{1,0:T(1,128)S(1)}, u32[]{:S(2)}, u32[]{:S(2)}) collective-permute-start(f32[1,512]{1,0:T(1,128)S(1)} %add.17), channel_id=1, source_target_pairs={{0,6},{1,7},{2,4},{3,5},{4,2},{5,3},{6,0},{7,1},{8,14},{9,15},{10,... | collective-permute-start | bytes 6152 | tf_op jit(solution)/shard_map/ppermute | solution.py:308
  23.4 11.7 %collective-permute-start.5 = (bf16[1,512]{1,0:T(2,128)(2,1)S(1)}, bf16[1,512]{1,0:T(2,128)(2,1)S(1)}, u32[]{:S(2)}, u32[]{:S(2)}) collective-permute-start(bf16[1,512]{1,0:T(2,128)(2,1)S(1)} %add_convert_fusion.ride), channel_id=1, source_target_pairs={{0,8},{8,0},{16,24},{24,16},{32,40},{40,32},{48,56},{56,48},{64,72... | collective-permute-start | bytes 3080 | tf_op jit(solution)/shard_map/ppermute | solution.py:308
  23.4 3.8 %copy-start.1 = (bf16[4,16,2,152,152]{4,3,2,1,0:T(8,128)(2,1)S(1)}, bf16[4,16,2,152,152]{4,3,2,1,0:T(8,128)(2,1)}, u32[]{:S(2)}) copy-start(bf16[4,16,2,152,152]{4,3,2,1,0:T(8,128)(2,1)} %transfer_hbm.1) | copy-start | bytes 17743876
  27.3 0.9 %copy-start.4 = (bf16[304,384]{1,0:T(8,128)(2,1)S(1)}, bf16[304,384]{1,0:T(8,128)(2,1)}, u32[]{:S(2)}) copy-start(bf16[304,384]{1,0:T(8,128)(2,1)} %get-tuple-element.17.to_left.first.before) | copy-start | bytes 700420
  28.2 0.9 %copy-start.5 = (bf16[304,384]{1,0:T(8,128)(2,1)S(1)}, bf16[304,384]{1,0:T(8,128)(2,1)}, u32[]{:S(2)}) copy-start(bf16[304,384]{1,0:T(8,128)(2,1)} %get-tuple-element.16.to_right.second.first) | copy-start | bytes 700420
  29.1 9.8 %copy-start.2 = (bf16[4,16,2,152,152]{4,3,2,1,0:T(8,128)(2,1)S(1)}, bf16[4,16,2,152,152]{4,3,2,1,0:T(8,128)(2,1)}, u32[]{:S(2)}) copy-start(bf16[4,16,2,152,152]{4,3,2,1,0:T(8,128)(2,1)} %transfer_hbm.1) | copy-start | bytes 17743876
  35.1 10.9 %collective-permute-start.6 = (bf16[2,512]{1,0:T(2,128)(2,1)S(1)}, bf16[2,512]{1,0:T(2,128)(2,1)S(1)}, u32[]{:S(2)}, u32[]{:S(2)}) collective-permute-start(bf16[2,512]{1,0:T(2,128)(2,1)S(1)} %pad_maximum_fusion.4.ride), channel_id=1, source_target_pairs={{0,16},{8,24},{16,0},{24,8},{32,48},{40,56},{48,32},{56,40},{64,80... | collective-permute-start | bytes 6152 | tf_op jit(solution)/shard_map/ppermute | solution.py:308
  46.0 7.2 %collective-permute-start.7 = (bf16[4,512]{1,0:T(4,128)(2,1)S(1)}, bf16[4,512]{1,0:T(4,128)(2,1)S(1)}, u32[]{:S(2)}, u32[]{:S(2)}) collective-permute-start(bf16[4,512]{1,0:T(4,128)(2,1)S(1)} %pad_maximum_fusion.3.ride), channel_id=1, source_target_pairs={{0,48},{8,56},{16,32},{24,40},{32,16},{40,24},{48,0},{56,8},{64,11... | collective-permute-start | bytes 12296 | tf_op jit(solution)/shard_map/ppermute | solution.py:308
  53.2 3.7 %collective-permute-start.8 = (bf16[8,512]{1,0:T(8,128)(2,1)S(1)}, bf16[8,512]{1,0:T(8,128)(2,1)S(1)}, u32[]{:S(2)}, u32[]{:S(2)}) collective-permute-start(bf16[8,512]{1,0:T(8,128)(2,1)S(1)} %pad_maximum_fusion.2), channel_id=1, source_target_pairs={{0,64},{8,72},{16,80},{24,88},{32,96},{40,104},{48,112},{56,120},{... | collective-permute-start | bytes 24584 | tf_op jit(solution)/shard_map/ppermute | solution.py:308
  57.0 5.3 %collective-permute-start.9 = (bf16[16,512]{1,0:T(8,128)(2,1)S(1)}, bf16[16,512]{1,0:T(8,128)(2,1)S(1)}, u32[]{:S(2)}, u32[]{:S(2)}) collective-permute-start(bf16[16,512]{1,0:T(8,128)(2,1)S(1)} %pad_maximum_fusion.1), channel_id=1, source_target_pairs={{0,192},{8,200},{16,208},{24,216},{32,224},{40,232},{48,240},{56,2... | collective-permute-start | bytes 49160 | tf_op jit(solution)/shard_map/ppermute | solution.py:308
  62.3 2.4 %copy-start.3 = (bf16[4,8,2,152,152]{4,3,2,1,0:T(8,128)(2,1)S(1)}, bf16[4,8,2,152,152]{4,3,2,1,0:T(8,128)(2,1)}, u32[]{:S(2)}) copy-start(bf16[4,8,2,152,152]{4,3,2,1,0:T(8,128)(2,1)} %down_hbm.1) | copy-start | bytes 8871940

commit v3 on v2

v3 whole, which is shorter than its diff:
```python
import functools

import jax
import jax.numpy as jnp
from jax import lax
from jax.experimental import pallas as pl
from jax.experimental.pallas import tpu as pltpu
from jax.sharding import PartitionSpec as P

SIZE = 152
HALF = 64
FINE = 512
REACH = 256
ENTRIES = 16
OCTANTS = 8
BF16 = jnp.bfloat16
F32 = jnp.float32


def mm(a, b):
    return jnp.dot(a, b, preferred_element_type=F32)


def iota(shape, dim):
    return lax.broadcasted_iota(jnp.int32, shape, dim)


def combine(by_real, by_imag):
    turned = pltpu.roll(by_imag, HALF, 1)
    return by_real + jnp.where(iota(turned.shape, 1) < HALF, -turned, turned)


def child_columns():
    row = iota((128, 1024), 0)
    col = iota((128, 1024), 1)
    octant, lane = col >> 7, col & 127
    box = (lane & 63) * 8 + octant
    wanted = jnp.where(box < HALF, (lane & HALF) + box, -1)
    return (row == wanted).astype(BF16)


def parent_columns():
    row = iota((128, 1024), 0)
    col = iota((128, 1024), 1)
    octant, lane = col >> 7, col & 127
    box = lane & 63
    wanted = jnp.where((box & 7) == octant, (lane & HALF) + (box >> 3), -1)
    return (row == wanted).astype(BF16)


def regroup(first, second):
    low = iota(first.shape, 1) < HALF
    return (
        jnp.where(low, first, pltpu.roll(second, HALF, 1)),
        jnp.where(low, pltpu.roll(first, HALF, 1), second),
    )


def apply_each(ops, columns, count):
    by_real = jnp.zeros((SIZE, 128), F32)
    by_imag = jnp.zeros((SIZE, 128), F32)
    for c in range(count):
        one = columns(c)
        by_real += mm(ops[c, 0], one)
        by_imag += mm(ops[c, 1], one)
    return combine(by_real, by_imag)


def tile(array, index):
    return array[:, 128 * index : 128 * (index + 1)]


def up_kernel(
    col_ref, check_hbm, equiv_hbm, ops_hbm, to_left, to_right, top, check, equiv, ops, own_op, sems
):
    first = [
        pltpu.make_async_copy(equiv_hbm, equiv, sems.at[4]),
        pltpu.make_async_copy(check_hbm, check, sems.at[5]),
    ]
    copies = [
        pltpu.make_async_copy(ops_hbm.at[level], ops.at[level], sems.at[level])
        for level in range(3)
    ]
    copies.append(pltpu.make_async_copy(ops_hbm.at[3, col_ref[0]], own_op, sems.at[3]))
    for copy in first + copies:
        copy.start()
    row = iota((FINE, FINE), 0)
    col = iota((FINE, FINE), 1)
    by_octant = (row == (col & 63) * 8 + (col >> 6)).astype(BF16)
    pick = child_columns()
    for copy in first:
        copy.wait()
    field = jnp.concatenate([check[0], check[1]], axis=1)
    by_real = mm(equiv[0], field)
    by_imag = mm(equiv[1], field)
    real = by_real[:, :FINE] - by_imag[:, FINE:]
    imag = by_real[:, FINE:] + by_imag[:, :FINE]
    dense = jnp.concatenate([real, imag], axis=0).astype(BF16)
    to_left[:, :REACH] = dense[:, :REACH]
    to_right[:, :REACH] = dense[:, REACH:]
    ordered = mm(dense, by_octant)
    children = []
    for pair in range(OCTANTS // 2):
        children += regroup(tile(ordered[:SIZE], pair), tile(ordered[SIZE:], pair))
    children = [child.astype(BF16) for child in children]
    packed = []
    for level in range(3):
        copies[level].wait()
        packed.append(apply_each(ops.at[level], lambda c: children[c], OCTANTS).astype(BF16))
        if level < 2:
            spread = mm(packed[level], pick).astype(BF16)
            children = [tile(spread, c) for c in range(OCTANTS)]
    both = jnp.concatenate([packed[0].astype(F32), packed[1].astype(F32)], axis=0).astype(BF16)
    to_left[:, REACH:] = both
    to_right[:, REACH:] = both
    copies[3].wait()
    part = combine(mm(own_op[0], packed[2]), mm(own_op[1], packed[2]))
    flat = jnp.transpose(jnp.concatenate([part, jnp.zeros((104, 128), F32)], axis=0))
    top[:, :256] = flat[0:1, :]
    top[:, 256:] = flat[HALF : HALF + 1, :]


def load_kernel(
    col_ref, ride, transfer_hbm, down_hbm, ride_out, transfer, down, own_op, sems
):
    ride_out[...] = ride[...]
    copies = [
        pltpu.make_async_copy(transfer_hbm.at[3], transfer, sems.at[0]),
        pltpu.make_async_copy(down_hbm.at[3, col_ref[0]], own_op, sems.at[1]),
    ]
    for level in range(3):
        copies.append(
            pltpu.make_async_copy(down_hbm.at[level], down.at[level], sems.at[2 + level])
        )
    for copy in copies:
        copy.start()
    for copy in copies:
        copy.wait()


def translate_packed(around, codes, targets, ops, copy):
    select = jnp.concatenate(
        [(codes == targets[k : k + 1, :]).astype(BF16) for k in range(ENTRIES)], axis=1
    )
    picked = mm(around, select).astype(BF16)
    copy.wait()
    return apply_each(ops, lambda k: tile(picked, k), ENTRIES)


def low_kernel(
    start_ref, ride, from_left, from_right, own, low_t, ops_hbm, ride_out, out, ops, sem
):
    ride_out[...] = ride[...]
    copy = pltpu.make_async_copy(ops_hbm.at[2], ops, sem)
    copy.start()
    lows = [ref[:, REACH:].astype(F32)[SIZE:] for ref in (own, from_left, from_right)]
    around = (lows[0] + pltpu.roll(lows[1], 8, 1) + pltpu.roll(lows[2], 16, 1)).astype(BF16)
    row = iota((128, 128), 0)
    lane = row & 63
    place = jnp.where(lane < 8, lane, jnp.where(lane < 16, lane - 16, lane - 8))
    codes = jnp.where(lane < 24, (row >> 6) * 1024 + place, -(1 << 20))
    index = low_t[...] - start_ref[0] * 8
    pad = jnp.full((ENTRIES, HALF - 8), -(1 << 19), jnp.int32)
    targets = jnp.concatenate([index, pad, index + 1024, pad], axis=1)
    out[...] = translate_packed(around, codes, targets, ops, copy)


def mid_kernel(
    start_ref, ride, from_left, from_right, own, mid_t, ops_hbm, ride_out, out, ops, sem
):
    ride_out[...] = ride[...]
    copy = pltpu.make_async_copy(ops_hbm.at[1], ops, sem)
    copy.start()
    mids = [ref[:, REACH:].astype(F32)[:SIZE] for ref in (from_left, own, from_right)]
    around = jnp.concatenate(mids, axis=1).astype(BF16)
    row = iota((384, 128), 0)
    codes = ((row >> 6) & 1) * 1024 + (row & 63) + ((row >> 7) - 1) * HALF
    index = mid_t[...] - start_ref[0] * HALF
    targets = jnp.concatenate([index, index + 1024], axis=1)
    out[...] = translate_packed(around, codes, targets, ops, copy)


def fine_kernel(
    half, start_ref, ride, before, first, second, fine_t, ops_hbm, ride_out, out, window, picked, ops, sem
):
    ride_out[...] = ride[...]
    copy = pltpu.make_async_copy(ops_hbm.at[0], ops, sem)
    copy.start()
    window[:, :REACH] = before[:, :REACH]
    window[:, REACH : 2 * REACH] = first[:, :REACH]
    window[:, 2 * REACH :] = second[:, :REACH]
    index = fine_t[:, half * REACH : (half + 1) * REACH] - (start_ref[0] * FINE + (half - 1) * REACH)
    row = iota((3 * REACH, REACH), 0)
    for k in range(ENTRIES):
        select = (row == index[k : k + 1, :]).astype(BF16)
        both = mm(window[...], select)
        picked[k, :, :REACH] = both[:SIZE].astype(BF16)
        picked[k, :, REACH:] = both[SIZE:].astype(BF16)
    copy.wait()
    by_real = jnp.zeros((SIZE, FINE), F32)
    by_imag = jnp.zeros((SIZE, FINE), F32)
    for k in range(ENTRIES):
        by_real += mm(ops[k, 0], picked[k])
        by_imag += mm(ops[k, 1], picked[k])
    out[0] = by_real[:, :REACH] - by_imag[:, REACH:]
    out[1] = by_real[:, REACH:] + by_imag[:, :REACH]


def down_kernel(
    own_ref, tops, own_list, fine_near_a, fine_near_b, mid_near, low_near, transfer, down, own_op, out
):
    gap = jnp.zeros((HALF - tops.shape[0], 256), F32)
    wide = tops[...].astype(F32)
    rows = jnp.concatenate([wide[:, :256], gap, wide[:, 256:], gap], axis=0)
    dense = jnp.transpose(rows)[:SIZE].astype(BF16)
    listed = own_list[...] ^ own_ref[0]
    listed = listed ^ ((listed >> 1) & 0b01010)
    pad = jnp.full((1, HALF - ENTRIES), -(1 << 19), jnp.int32)
    wanted = jnp.concatenate([listed, pad, listed + HALF, pad], axis=1)
    picked = mm(dense, (iota((128, 128), 0) == wanted).astype(BF16))
    entry = iota((SIZE, 128), 1) & 63
    local = apply_each(transfer, lambda k: jnp.where(entry == k, picked, 0.0).astype(BF16), ENTRIES)
    for shift in (8, 4, 2, 1):
        local = local + pltpu.roll(local, 128 - shift, 1)
    local = jnp.where(entry == 0, local, 0.0).astype(BF16)
    local = combine(mm(own_op[0], local), mm(own_op[1], local)).astype(BF16)
    place = parent_columns()
    for level, near in ((2, low_near), (1, mid_near)):
        parents = mm(local, place).astype(BF16)
        local = apply_each(down.at[level], lambda c: tile(parents, c), OCTANTS) + near[...]
        local = local.astype(BF16)
    real, imag = [], []
    for pair in range(OCTANTS // 2):
        terms = [
            combine(mm(down[0, c, 0], local), mm(down[0, c, 1], local))
            for c in (2 * pair, 2 * pair + 1)
        ]
        one_real, one_imag = regroup(*terms)
        real.append(one_real)
        imag.append(one_imag)
    both = jnp.concatenate([jnp.concatenate(real, axis=1), jnp.concatenate(imag, axis=1)], axis=0)
    high = both.astype(BF16)
    low = (both - high.astype(F32)).astype(BF16)
    row = iota((FINE, FINE), 0)
    col = iota((FINE, FINE), 1)
    place = (row == (col & 7) * HALF + (col >> 3)).astype(BF16)
    far = mm(high, place) + mm(low, place)
    out[0, :, :REACH] = fine_near_a[0] + far[:SIZE, :REACH]
    out[0, :, REACH:] = fine_near_b[0] + far[:SIZE, REACH:]
    out[1, :, :REACH] = fine_near_a[1] + far[SIZE:, :REACH]
    out[1, :, REACH:] = fine_near_b[1] + far[SIZE:, REACH:]


def shape(dims, dtype):
    return jax.ShapeDtypeStruct(dims, dtype)


VMEM = pl.BlockSpec(memory_space=pltpu.VMEM)
SMEM = pl.BlockSpec(memory_space=pltpu.SMEM)
HBM = pl.BlockSpec(memory_space=pltpu.HBM)
INTERPRET = False


def in_hbm(x):
    return x if INTERPRET else pltpu.with_memory_space_constraint(x, pltpu.HBM)


def on_chip(dims, dtype):
    return shape(dims, dtype) if INTERPRET else pltpu.VMEM(dims, dtype)


def call(kernel, ins, outs, scratch, flops, limit=40):
    return pl.pallas_call(
        kernel,
        in_specs=ins,
        out_specs=[VMEM] * len(outs),
        out_shape=outs,
        scratch_shapes=scratch,
        compiler_params=pltpu.CompilerParams(vmem_limit_bytes=limit << 20),
        cost_estimate=pl.CostEstimate(flops=flops, bytes_accessed=8 << 20, transcendentals=0),
        interpret=INTERPRET,
    )


def body(
    check_field, to_equiv, upward_ops, downward_ops, transfer_ops, list_fine, list_mid, list_low, list_top
):
    axes = ("row", "col")
    rows, cols = lax.axis_size("row"), lax.axis_size("col")
    count = rows * cols
    position = lax.axis_index(axes).astype(jnp.int32).reshape(1)
    own_col = lax.axis_index("col").astype(jnp.int32).reshape(1)
    own_row = lax.axis_index("row").astype(jnp.int32).reshape(1)
    check_field, to_equiv, upward_ops, downward_ops, transfer_ops = [
        in_hbm(x) for x in (check_field, to_equiv, upward_ops, downward_ops, transfer_ops)
    ]
    octant_ops = (2, SIZE, SIZE)
    to_left, to_right, top = call(
        up_kernel,
        [SMEM, HBM, HBM, HBM],
        [shape((2 * SIZE, 384), BF16), shape((2 * SIZE, 384), BF16), shape((1, 512), F32)],
        [
            pltpu.VMEM((2, SIZE, FINE), BF16),
            pltpu.VMEM(octant_ops, BF16),
            pltpu.VMEM((3, OCTANTS) + octant_ops, BF16),
            pltpu.VMEM(octant_ops, BF16),
            pltpu.SemaphoreType.DMA((6,)),
        ],
        4 << 30,
    )(own_col, check_field, to_equiv, upward_ops)
    from_left = lax.ppermute(to_right, axes, [(i, (i + 1) % count) for i in range(count)])
    from_right = lax.ppermute(to_left, axes, [(i, (i - 1) % count) for i in range(count)])

    def load(ride):
        return call(
            load_kernel,
            [SMEM, VMEM, HBM, HBM],
            [
                shape(ride.shape, ride.dtype),
                on_chip((ENTRIES,) + octant_ops, BF16),
                on_chip((3, OCTANTS) + octant_ops, BF16),
                on_chip(octant_ops, BF16),
            ],
            [pltpu.SemaphoreType.DMA((5,))],
            4 << 30,
        )(own_col, ride, transfer_ops, downward_ops)

    def small(kernel, listed, ride):
        return call(
            kernel,
            [SMEM] + [VMEM] * 5 + [HBM],
            [shape(ride.shape, ride.dtype), shape((SIZE, 128), F32)],
            [pltpu.VMEM((ENTRIES,) + octant_ops, BF16), pltpu.SemaphoreType.DMA(())],
            4 << 30,
        )(position, ride, from_left, from_right, to_left, listed.T, transfer_ops)

    def fine(half, ride):
        around = (from_left, to_left, to_right) if half == 0 else (to_left, to_right, from_right)
        return call(
            functools.partial(fine_kernel, half),
            [SMEM] + [VMEM] * 5 + [HBM],
            [shape(ride.shape, ride.dtype), shape((2, SIZE, REACH), F32)],
            [
                pltpu.VMEM((2 * SIZE, 3 * REACH), BF16),
                pltpu.VMEM((ENTRIES, SIZE, FINE), BF16),
                pltpu.VMEM((ENTRIES,) + octant_ops, BF16),
                pltpu.SemaphoreType.DMA(()),
            ],
            6 << 30,
        )(position, ride, *around, list_fine.T, transfer_ops)

    def swap(x, axis, mask):
        return lax.ppermute(x, axis, [(i, i ^ mask) for i in range(lax.axis_size(axis))])

    work = {
        1: load,
        2: functools.partial(fine, 0),
        3: functools.partial(fine, 1),
        4: functools.partial(small, mid_kernel, list_mid),
        5: functools.partial(small, low_kernel, list_low),
    }
    done = {}
    total = top
    for step, mask in enumerate((1, 2, 6, 1, 2, 6, 8, 24)):
        axis = "col" if step < 3 else "row"
        other = swap(total, axis, mask) if axis == "col" or mask < rows else None
        if step in work:
            total, *done[step] = work[step](total)
        if axis == "col":
            total = total + other
        elif other is not None:
            total = jnp.concatenate([total, other], axis=0)
        if step == 2:
            total = total.astype(BF16)
    own_list = lax.dynamic_slice_in_dim(list_top, lax.axis_index("row"), 1, 0)
    (far,) = call(
        down_kernel,
        [SMEM] + [VMEM] * 9,
        [shape((2, SIZE, FINE), F32)],
        [],
        8 << 30,
    )(own_row, total, own_list, *done[2], *done[3], *done[4], *done[5], *done[1])
    return far


def solution(mesh):
    split = P(None, None, ("row", "col"))
    lists = P(("row", "col"), None)
    return jax.shard_map(
        body,
        mesh=mesh,
        in_specs=(split, P(), P(), P(), P(), lists, lists, lists, P()),
        out_specs=split,
        check_vma=False,
    )
```

time: 74.1 us -> 57.9 us (0.78)
  the two profiles are of different devices: /device:TPU:2 before, /device:TPU:24 now
where the time goes in v3:
time: 57.9 us; the launch traced here: 57.6 us
  Pallas kernels  28 us (48%)
  starting transfers between devices  15.9 us (27%)
  waiting for transfers between devices  9.06 us (16%)
  local copies, waits for them, and re-layouts  4.25 us (7%)
    pallas_call x2, Pallas kernels, fine(): call(functools.partial(fine_kernel, half), [SMEM] + [VMEM] * 5 + [HBM], [...  10.4 us
    ppermute x8, starting transfers between devices, swap(): lax.ppermute(x, axis, [(i, i ^ mask) for i in range(lax.axis_size(axis))])  9.46 us
    ppermute x8, waiting for transfers between devices, swap(): lax.ppermute(x, axis, [(i, i ^ mask) for i in range(lax.axis_size(axis))])  9.05 us
    ppermute x1, starting transfers between devices, body(): lax.ppermute(to_left, axes, [(i, (i - 1) % count) for i in range(count)])  6.37 us
    pallas_call x2, Pallas kernels, small(): call(kernel, [SMEM] + [VMEM] * 5 + [HBM], [shape(ride.shape, ride.dtype),...  5.36 us
    pallas_call x1, Pallas kernels, body(): call(down_kernel, [SMEM] + [VMEM] * 9, [shape((2, SIZE, FINE), F32)], [],...  4.99 us
    pallas_call x1, Pallas kernels, body(): call(up_kernel, [SMEM, HBM, HBM, HBM], [shape((2 * SIZE, 384), BF16), sha...  4.37 us
    unnamed x26, local copies, waits for them, and re-layouts  4.18 us
  transfers between devices with their start and end apart: 10, of which 3 were waited for; matrix products, arithmetic and copies ran while one was open for 0% of the time, Pallas kernels for 32%

profile of v3, /device:TPU:24, one launch (start us, length us, event | category | flops | bytes accessed | tf_op | source)
XLA Modules:
  0.0 57.6 jit_solution(1607922017511380153)
XLA Ops:
  0.0 0.0 copy-start
  0.0 0.0 copy-start.11
  0.0 4.4 %shard_map.91 = (bf16[304,384]{1,0:T(8,128)(2,1)S(1)}, bf16[304,384]{1,0:T(8,128)(2,1)S(1)}, f32[1,512]{1,0:T(1,128)S(1)}) custom-call(s32[1]{0:T(128)} %bitcast.2.col_ref, bf16[2,152,512]{2,1,0:T(8,128)(2,1)} %check_hbm.1, bf16[2,152,152]{2,1,0:T(8,128)(2,1)} %equiv_hbm.1, bf16[4,8,2,152,152]{4,3,2,1,0:T(8,128)(2,1)} %ops_hbm.5), custom_call_target="tpu_custom_call" | custom-call | flops 4294967296 | bytes 8388608 | tf_op jit(solution)/shard_map/pallas_call | solution.py:298
  4.4 2.0 %collective-permute-start = (f32[1,512]{1,0:T(1,128)S(1)}, f32[1,512]{1,0:T(1,128)S(1)}, u32[]{:S(2)}, u32[]{:S(2)}) collective-permute-start(f32[1,512]{1,0:T(1,128)S(1)} %get-tuple-element.20), channel_id=1, source_target_pairs={{0,1},{1,0},{2,3},{3,2},{4,5},{5,4},{6,7},{7,6},{8,9},{9,8},{10,11... | collective-permute-start | bytes 6152 | tf_op jit(solution)/shard_map/ppermute | solution.py:353
  6.4 0.1 collective-permute-start.2
  6.5 6.4 %collective-permute-start.4 = (bf16[304,384]{1,0:T(8,128)(2,1)S(1)}, bf16[304,384]{1,0:T(8,128)(2,1)S(1)}, u32[]{:S(2)}, u32[]{:S(2)}) collective-permute-start(bf16[304,384]{1,0:T(8,128)(2,1)S(1)} %get-tuple-element.23.first.before.own), channel_id=1, source_target_pairs={{0,255},{1,0},{2,1},{3,2},{4,3},{5,4},{6,5},{7,6},{8,7},{9,8},{10,... | collective-permute-start | bytes 700424 | tf_op jit(solution)/shard_map/ppermute | solution.py:312
  12.9 0.0 copy-done.11
  12.9 0.1 copy.10
  12.9 0.0 collective-permute-done
  13.0 0.0 copy-start.1
  13.0 0.1 collective-permute-start.1
  13.1 2.9 %shard_map.92 = (f32[1,512]{1,0:T(1,128)S(1)}, bf16[16,2,152,152]{3,2,1,0:T(8,128)(2,1)S(1)}, bf16[3,8,2,152,152]{4,3,2,1,0:T(8,128)(2,1)S(1)}, bf16[2,152,152]{2,1,0:T(8,128)(2,1)S(1)}) custom-call(s32[1]{0:T(128)} %bitcast.2.col_ref, f32[1,512]{1,0:T(1,128)S(1)} %add.16.ride, bf16[4,16,2,152,152]{4,3,2,1,0:T(8,128)(2,1)} %ops_hbm.9, ...), custom_call_target="tpu_custom_call" | custom-call | flops 4294967296 | bytes 8388608 | tf_op jit(solution)/shard_map/pallas_call | solution.py:315
  16.0 0.0 copy-start.3
  16.0 0.0 copy-start.5
  16.0 1.6 %collective-permute-done.1 = f32[1,512]{1,0:T(1,128)S(1)} collective-permute-done((f32[1,512]{1,0:T(1,128)S(1)}, f32[1,512]{1,0:T(1,128)S(1)}, u32[]{:S(2)}, u32[]{:S(2)}) %collective-permute-start.1) | collective-permute-done | bytes 2080 | tf_op jit(solution)/shard_map/ppermute | solution.py:353
  17.5 2.1 %collective-permute-start.3 = (f32[1,512]{1,0:T(1,128)S(1)}, f32[1,512]{1,0:T(1,128)S(1)}, u32[]{:S(2)}, u32[]{:S(2)}) collective-permute-start(f32[1,512]{1,0:T(1,128)S(1)} %add.17.ride), channel_id=1, source_target_pairs={{0,6},{1,7},{2,4},{3,5},{4,2},{5,3},{6,0},{7,1},{8,14},{9,15},{10,... | collective-permute-start | bytes 6152 | tf_op jit(solution)/shard_map/ppermute | solution.py:353
  19.7 0.0 collective-permute-done.2.before.from_left
  19.7 0.0 copy-done.1
  19.7 5.2 %shard_map.93 = (f32[1,512]{1,0:T(1,128)S(1)}, f32[2,152,256]{2,1,0:T(8,128)S(1)}) custom-call(s32[1]{0:T(128)} %bitcast.1.start_ref, f32[1,512]{1,0:T(1,128)S(1)} %add.17.ride, bf16[304,384]{1,0:T(8,128)(2,1)S(1)} %collective-permute-done.2.before.from_left, bf16[304,384]{1,0:T(8,128)(2,1)S(1)} %get-tuple-element.23.first.before.own, ...), custom_call_target="tpu_custom_call" | custom-call | flops 6442450944 | bytes 8388608 | tf_op jit(solution)/shard_map/pallas_call | solution.py:339
  24.9 0.0 copy-done.3
  24.9 0.0 copy-done.5
  24.9 0.0 copy-start.7
  24.9 0.0 collective-permute-done.3
  25.0 0.0 copy-start.2
  25.0 0.1 collective-permute-start.5
  25.1 0.0 collective-permute-done.4.second.from_right
  25.1 5.2 %shard_map.94 = (bf16[1,512]{1,0:T(2,128)(2,1)S(1)}, f32[2,152,256]{2,1,0:T(8,128)S(1)}) custom-call(s32[1]{0:T(128)} %bitcast.1.start_ref, bf16[1,512]{1,0:T(2,128)(2,1)S(1)} %add_convert_fusion.ride, bf16[304,384]{1,0:T(8,128)(2,1)S(1)} %get-tuple-element.23.first.before.own, bf16[304,384]{1,0:T(8,128)(2,1)S(1)} %get-tuple-element.22.second.first, ...), custom_call_target="tpu_custom_call" | custom-call | flops 6442450944 | bytes 8388608 | tf_op jit(solution)/shard_map/pallas_call | solution.py:339
  30.3 0.0 copy-done.7
  30.3 0.0 copy-start.9
  30.3 0.0 collective-permute-done.5
  30.3 1.8 %collective-permute-start.6 = (bf16[2,512]{1,0:T(2,128)(2,1)S(1)}, bf16[2,512]{1,0:T(2,128)(2,1)S(1)}, u32[]{:S(2)}, u32[]{:S(2)}) collective-permute-start(bf16[2,512]{1,0:T(2,128)(2,1)S(1)} %pad_maximum_fusion.4.ride), channel_id=1, source_target_pairs={{0,16},{8,24},{16,0},{24,8},{32,48},{40,56},{48,32},{56,40},{64,80... | collective-permute-start | bytes 6152 | tf_op jit(solution)/shard_map/ppermute | solution.py:353
  32.1 0.0 copy-done.2
  32.1 2.7 %shard_map.95 = (bf16[2,512]{1,0:T(2,128)(2,1)S(1)}, f32[152,128]{1,0:T(8,128)S(1)}) custom-call(s32[1]{0:T(128)} %bitcast.1.start_ref, bf16[2,512]{1,0:T(2,128)(2,1)S(1)} %pad_maximum_fusion.4.ride, bf16[304,384]{1,0:T(8,128)(2,1)S(1)} %collective-permute-done.2.before.from_left, bf16[304,384]{1,0:T(8,128)(2,1)S(1)} %collective-permute-done.4.second.from_right, ...), custom_call_target="tpu_custom_call" | custom-call | flops 4294967296 | bytes 8388608 | tf_op jit(solution)/shard_map/pallas_call | solution.py:329
  34.8 0.0 copy-done.9
  34.8 0.0 collective-permute-done.6
  34.8 2.2 %collective-permute-start.7 = (bf16[4,512]{1,0:T(4,128)(2,1)S(1)}, bf16[4,512]{1,0:T(4,128)(2,1)S(1)}, u32[]{:S(2)}, u32[]{:S(2)}) collective-permute-start(bf16[4,512]{1,0:T(4,128)(2,1)S(1)} %pad_maximum_fusion.3.ride), channel_id=1, source_target_pairs={{0,48},{8,56},{16,32},{24,40},{32,16},{40,24},{48,0},{56,8},{64,11... | collective-permute-start | bytes 12296 | tf_op jit(solution)/shard_map/ppermute | solution.py:353
  37.1 0.0 copy-start.6
  37.1 2.7 %shard_map.96 = (bf16[4,512]{1,0:T(4,128)(2,1)S(1)}, f32[152,128]{1,0:T(8,128)S(1)}) custom-call(s32[1]{0:T(128)} %bitcast.1.start_ref, bf16[4,512]{1,0:T(4,128)(2,1)S(1)} %pad_maximum_fusion.3.ride, bf16[304,384]{1,0:T(8,128)(2,1)S(1)} %collective-permute-done.2.before.from_left, bf16[304,384]{1,0:T(8,128)(2,1)S(1)} %collective-permute-done.4.second.from_right, ...), custom_call_target="tpu_custom_call" | custom-call | flops 4294967296 | bytes 8388608 | tf_op jit(solution)/shard_map/pallas_call | solution.py:329
  39.8 0.0 collective-permute-done.7
  39.8 0.8 %collective-permute-start.8 = (bf16[8,512]{1,0:T(8,128)(2,1)S(1)}, bf16[8,512]{1,0:T(8,128)(2,1)S(1)}, u32[]{:S(2)}, u32[]{:S(2)}) collective-permute-start(bf16[8,512]{1,0:T(8,128)(2,1)S(1)} %pad_maximum_fusion.2), channel_id=1, source_target_pairs={{0,64},{8,72},{16,80},{24,88},{32,96},{40,104},{48,112},{56,120},{... | collective-permute-start | bytes 24584 | tf_op jit(solution)/shard_map/ppermute | solution.py:353
  40.6 2.9 %collective-permute-done.8 = bf16[8,512]{1,0:T(8,128)(2,1)S(1)} collective-permute-done((bf16[8,512]{1,0:T(8,128)(2,1)S(1)}, bf16[8,512]{1,0:T(8,128)(2,1)S(1)}, u32[]{:S(2)}, u32[]{:S(2)}) %collective-permute-start.8) | collective-permute-done | bytes 8224 | tf_op jit(solution)/shard_map/ppermute | solution.py:353
  43.5 0.3 collective-permute-start.9
  43.9 0.0 copy-done
  43.9 0.1 constant_dynamic-slice_fusion
  43.9 0.1 copy.12.own_list
  44.0 4.6 %collective-permute-done.9 = bf16[16,512]{1,0:T(8,128)(2,1)S(1)} collective-permute-done((bf16[16,512]{1,0:T(8,128)(2,1)S(1)}, bf16[16,512]{1,0:T(8,128)(2,1)S(1)}, u32[]{:S(2)}, u32[]{:S(2)}) %collective-permute-start.9) | collective-permute-done | bytes 16416 | tf_op jit(solution)/shard_map/ppermute | solution.py:353
  48.6 0.0 copy-done.6
  48.6 0.0 copy-start.4
  48.6 2.0 %copy-done.4 = bf16[3,8,2,152,152]{4,3,2,1,0:T(8,128)(2,1)S(1)} copy-done((bf16[3,8,2,152,152]{4,3,2,1,0:T(8,128)(2,1)S(1)}, bf16[3,8,2,152,152]{4,3,2,1,0:T(8,128)(2,1)}, u32[]{:S(2)}) %copy-start.4) | copy-done | bytes 2218008
  50.7 0.0 copy-start.8
  50.7 1.0 %copy-done.8 = f32[2,152,256]{2,1,0:T(8,128)S(1)} copy-done((f32[2,152,256]{2,1,0:T(8,128)S(1)}, f32[2,152,256]{2,1,0:T(8,128)}, u32[]{:S(2)}) %copy-start.8) | copy-done | bytes 311320
  51.6 0.0 copy-start.10
  51.6 1.0 %copy-done.10 = f32[2,152,256]{2,1,0:T(8,128)S(1)} copy-done((f32[2,152,256]{2,1,0:T(8,128)S(1)}, f32[2,152,256]{2,1,0:T(8,128)}, u32[]{:S(2)}) %copy-start.10) | copy-done | bytes 311320
  52.6 5.0 %shard_map.97 = f32[2,152,512]{2,1,0:T(8,128)} custom-call(s32[1]{0:T(128)} %bitcast.own_ref, bf16[32,512]{1,0:T(8,128)(2,1)S(1)} %pad_maximum_fusion.tops, s32[1,16]{1,0:T(1,128)S(1)} %copy.12.own_list, f32[2,152,256]{2,1,0:T(8,128)S(1)} %copy-done.8, f32[2,152,256]{2,1,0:T(8,128)S(1)} %copy-done.10, f32[152,128]{1,0:T(8,128)S(1)} %get-tuple-element.30.mid_near, ...), custom_call_target="tpu_custom_call" | custom-call | flops 8589934592 | bytes 8388608 | tf_op jit(solution)/shard_map/pallas_call | solution.py:376
  (8 shorter events, 0.1 us)
Async XLA Ops:
  0.0 43.9 %copy-start = (s32[32,16]{0,1:T(8,128)S(1)}, s32[32,16]{0,1:T(8,128)}, u32[]{:S(2)}) copy-start(s32[32,16]{0,1:T(8,128)} %param.17) | copy-start | bytes 6148
  0.0 12.9 %copy-start.11 = (s32[8,16]{1,0:T(8,128)S(1)}, s32[8,16]{1,0:T(8,128)}, u32[]{:S(2)}) copy-start(s32[8,16]{1,0:T(8,128)} %param.16) | copy-start | bytes 1540
  4.4 8.6 %collective-permute-start = (f32[1,512]{1,0:T(1,128)S(1)}, f32[1,512]{1,0:T(1,128)S(1)}, u32[]{:S(2)}, u32[]{:S(2)}) collective-permute-start(f32[1,512]{1,0:T(1,128)S(1)} %get-tuple-element.20), channel_id=1, source_target_pairs={{0,1},{1,0},{2,3},{3,2},{4,5},{5,4},{6,7},{7,6},{8,9},{9,8},{10,11... | collective-permute-start | bytes 6152 | tf_op jit(solution)/shard_map/ppermute | solution.py:353
  6.4 13.3 %collective-permute-start.2 = (bf16[304,384]{1,0:T(8,128)(2,1)S(1)}, bf16[304,384]{1,0:T(8,128)(2,1)S(1)}, u32[]{:S(2)}, u32[]{:S(2)}) collective-permute-start(bf16[304,384]{1,0:T(8,128)(2,1)S(1)} %get-tuple-element.22.second.first), channel_id=1, source_target_pairs={{0,1},{1,2},{2,3},{3,4},{4,5},{5,6},{6,7},{7,8},{8,9},{9,10},{10,1... | collective-permute-start | bytes 700424 | tf_op jit(solution)/shard_map/ppermute | solution.py:311
  6.5 18.6 %collective-permute-start.4 = (bf16[304,384]{1,0:T(8,128)(2,1)S(1)}, bf16[304,384]{1,0:T(8,128)(2,1)S(1)}, u32[]{:S(2)}, u32[]{:S(2)}) collective-permute-start(bf16[304,384]{1,0:T(8,128)(2,1)S(1)} %get-tuple-element.23.first.before.own), channel_id=1, source_target_pairs={{0,255},{1,0},{2,1},{3,2},{4,3},{5,4},{6,5},{7,6},{8,7},{9,8},{10,... | collective-permute-start | bytes 700424 | tf_op jit(solution)/shard_map/ppermute | solution.py:312
  13.0 6.7 %copy-start.1 = (s32[512,16]{0,1:T(8,128)S(1)}, s32[512,16]{0,1:T(8,128)}, u32[]{:S(2)}) copy-start(s32[512,16]{0,1:T(8,128)} %param.14) | copy-start | bytes 98308
  13.0 4.6 %collective-permute-start.1 = (f32[1,512]{1,0:T(1,128)S(1)}, f32[1,512]{1,0:T(1,128)S(1)}, u32[]{:S(2)}, u32[]{:S(2)}) collective-permute-start(f32[1,512]{1,0:T(1,128)S(1)} %add.16.ride), channel_id=1, source_target_pairs={{0,2},{1,3},{2,0},{3,1},{4,6},{5,7},{6,4},{7,5},{8,10},{9,11},{10,... | collective-permute-start | bytes 6152 | tf_op jit(solution)/shard_map/ppermute | solution.py:353
  16.0 8.9 %copy-start.3 = (bf16[3,8,2,152,152]{4,3,2,1,0:T(8,128)(2,1)}, bf16[3,8,2,152,152]{4,3,2,1,0:T(8,128)(2,1)S(1)}, u32[]{:S(2)}) copy-start(bf16[3,8,2,152,152]{4,3,2,1,0:T(8,128)(2,1)S(1)} %get-tuple-element.33.down) | copy-start | bytes 6653956
  16.0 8.9 %copy-start.5 = (bf16[2,152,152]{2,1,0:T(8,128)(2,1)}, bf16[2,152,152]{2,1,0:T(8,128)(2,1)S(1)}, u32[]{:S(2)}) copy-start(bf16[2,152,152]{2,1,0:T(8,128)(2,1)S(1)} %get-tuple-element.34.own_op) | copy-start | bytes 277252
  17.5 7.4 %collective-permute-start.3 = (f32[1,512]{1,0:T(1,128)S(1)}, f32[1,512]{1,0:T(1,128)S(1)}, u32[]{:S(2)}, u32[]{:S(2)}) collective-permute-start(f32[1,512]{1,0:T(1,128)S(1)} %add.17.ride), channel_id=1, source_target_pairs={{0,6},{1,7},{2,4},{3,5},{4,2},{5,3},{6,0},{7,1},{8,14},{9,15},{10,... | collective-permute-start | bytes 6152 | tf_op jit(solution)/shard_map/ppermute | solution.py:353
  24.9 5.4 %copy-start.7 = (f32[2,152,256]{2,1,0:T(8,128)}, f32[2,152,256]{2,1,0:T(8,128)S(1)}, u32[]{:S(2)}) copy-start(f32[2,152,256]{2,1,0:T(8,128)S(1)} %get-tuple-element.28.fine_near_a) | copy-start | bytes 933892
  25.0 7.1 %copy-start.2 = (s32[64,16]{0,1:T(8,128)S(1)}, s32[64,16]{0,1:T(8,128)}, u32[]{:S(2)}) copy-start(s32[64,16]{0,1:T(8,128)} %param.15) | copy-start | bytes 12292
  25.0 5.4 %collective-permute-start.5 = (bf16[1,512]{1,0:T(2,128)(2,1)S(1)}, bf16[1,512]{1,0:T(2,128)(2,1)S(1)}, u32[]{:S(2)}, u32[]{:S(2)}) collective-permute-start(bf16[1,512]{1,0:T(2,128)(2,1)S(1)} %add_convert_fusion.ride), channel_id=1, source_target_pairs={{0,8},{8,0},{16,24},{24,16},{32,40},{40,32},{48,56},{56,48},{64,72... | collective-permute-start | bytes 3080 | tf_op jit(solution)/shard_map/ppermute | solution.py:353
  30.3 4.5 %copy-start.9 = (f32[2,152,256]{2,1,0:T(8,128)}, f32[2,152,256]{2,1,0:T(8,128)S(1)}, u32[]{:S(2)}) copy-start(f32[2,152,256]{2,1,0:T(8,128)S(1)} %get-tuple-element.29.fine_near_b) | copy-start | bytes 933892
  30.3 4.4 %collective-permute-start.6 = (bf16[2,512]{1,0:T(2,128)(2,1)S(1)}, bf16[2,512]{1,0:T(2,128)(2,1)S(1)}, u32[]{:S(2)}, u32[]{:S(2)}) collective-permute-start(bf16[2,512]{1,0:T(2,128)(2,1)S(1)} %pad_maximum_fusion.4.ride), channel_id=1, source_target_pairs={{0,16},{8,24},{16,0},{24,8},{32,48},{40,56},{48,32},{56,40},{64,80... | collective-permute-start | bytes 6152 | tf_op jit(solution)/shard_map/ppermute | solution.py:353
  34.8 5.0 %collective-permute-start.7 = (bf16[4,512]{1,0:T(4,128)(2,1)S(1)}, bf16[4,512]{1,0:T(4,128)(2,1)S(1)}, u32[]{:S(2)}, u32[]{:S(2)}) collective-permute-start(bf16[4,512]{1,0:T(4,128)(2,1)S(1)} %pad_maximum_fusion.3.ride), channel_id=1, source_target_pairs={{0,48},{8,56},{16,32},{24,40},{32,16},{40,24},{48,0},{56,8},{64,11... | collective-permute-start | bytes 12296 | tf_op jit(solution)/shard_map/ppermute | solution.py:353
  37.1 11.5 %copy-start.6 = (bf16[2,152,152]{2,1,0:T(8,128)(2,1)S(1)}, bf16[2,152,152]{2,1,0:T(8,128)(2,1)}, u32[]{:S(2)}) copy-start(bf16[2,152,152]{2,1,0:T(8,128)(2,1)} %copy-done.5) | copy-start | bytes 277252
  39.8 3.7 %collective-permute-start.8 = (bf16[8,512]{1,0:T(8,128)(2,1)S(1)}, bf16[8,512]{1,0:T(8,128)(2,1)S(1)}, u32[]{:S(2)}, u32[]{:S(2)}) collective-permute-start(bf16[8,512]{1,0:T(8,128)(2,1)S(1)} %pad_maximum_fusion.2), channel_id=1, source_target_pairs={{0,64},{8,72},{16,80},{24,88},{32,96},{40,104},{48,112},{56,120},{... | collective-permute-start | bytes 24584 | tf_op jit(solution)/shard_map/ppermute | solution.py:353
  43.5 5.0 %collective-permute-start.9 = (bf16[16,512]{1,0:T(8,128)(2,1)S(1)}, bf16[16,512]{1,0:T(8,128)(2,1)S(1)}, u32[]{:S(2)}, u32[]{:S(2)}) collective-permute-start(bf16[16,512]{1,0:T(8,128)(2,1)S(1)} %pad_maximum_fusion.1), channel_id=1, source_target_pairs={{0,192},{8,200},{16,208},{24,216},{32,224},{40,232},{48,240},{56,2... | collective-permute-start | bytes 49160 | tf_op jit(solution)/shard_map/ppermute | solution.py:353
  48.6 2.1 %copy-start.4 = (bf16[3,8,2,152,152]{4,3,2,1,0:T(8,128)(2,1)S(1)}, bf16[3,8,2,152,152]{4,3,2,1,0:T(8,128)(2,1)}, u32[]{:S(2)}) copy-start(bf16[3,8,2,152,152]{4,3,2,1,0:T(8,128)(2,1)} %copy-done.3) | copy-start | bytes 6653956
  50.7 1.0 %copy-start.8 = (f32[2,152,256]{2,1,0:T(8,128)S(1)}, f32[2,152,256]{2,1,0:T(8,128)}, u32[]{:S(2)}) copy-start(f32[2,152,256]{2,1,0:T(8,128)} %copy-done.7) | copy-start | bytes 933892
  51.6 1.0 %copy-start.10 = (f32[2,152,256]{2,1,0:T(8,128)S(1)}, f32[2,152,256]{2,1,0:T(8,128)}, u32[]{:S(2)}) copy-start(f32[2,152,256]{2,1,0:T(8,128)} %copy-done.9) | copy-start | bytes 933892

commit v4 on v3

v4 whole, which is shorter than its diff:
```python
import functools

import jax
import jax.numpy as jnp
from jax import lax
from jax.experimental import pallas as pl
from jax.experimental.pallas import tpu as pltpu
from jax.sharding import PartitionSpec as P

SIZE = 152
HALF = 64
FINE = 512
REACH = 256
ENTRIES = 16
GROUP = 8
OCTANTS = 8
BF16 = jnp.bfloat16
F32 = jnp.float32


def mm(a, b):
    return jnp.dot(a, b, preferred_element_type=F32)


def iota(shape, dim):
    return lax.broadcasted_iota(jnp.int32, shape, dim)


def combine(by_real, by_imag):
    turned = pltpu.roll(by_imag, HALF, 1)
    return by_real + jnp.where(iota(turned.shape, 1) < HALF, -turned, turned)


def child_columns():
    row = iota((128, 1024), 0)
    col = iota((128, 1024), 1)
    octant, lane = col >> 7, col & 127
    box = (lane & 63) * 8 + octant
    wanted = jnp.where(box < HALF, (lane & HALF) + box, -1)
    return (row == wanted).astype(BF16)


def parent_columns():
    row = iota((128, 1024), 0)
    col = iota((128, 1024), 1)
    octant, lane = col >> 7, col & 127
    box = lane & 63
    wanted = jnp.where((box & 7) == octant, (lane & HALF) + (box >> 3), -1)
    return (row == wanted).astype(BF16)


def regroup(first, second):
    low = iota(first.shape, 1) < HALF
    return (
        jnp.where(low, first, pltpu.roll(second, HALF, 1)),
        jnp.where(low, pltpu.roll(first, HALF, 1), second),
    )


def apply_each(ops, columns, count):
    by_real = jnp.zeros((SIZE, 128), F32)
    by_imag = jnp.zeros((SIZE, 128), F32)
    for c in range(count):
        one = columns(c)
        by_real += mm(ops[c, 0], one)
        by_imag += mm(ops[c, 1], one)
    return combine(by_real, by_imag)


def tile(array, index):
    return array[:, 128 * index : 128 * (index + 1)]


def up_kernel(
    check_hbm, equiv_hbm, ops_hbm, to_left, to_right, top, check, equiv, ops, own_op, sems
):
    first = [
        pltpu.make_async_copy(equiv_hbm, equiv, sems.at[4]),
        pltpu.make_async_copy(check_hbm, check, sems.at[5]),
    ]
    copies = [
        pltpu.make_async_copy(ops_hbm.at[level], ops.at[level], sems.at[level])
        for level in range(3)
    ]
    copies.append(pltpu.make_async_copy(ops_hbm.at[3, lax.axis_index("col")], own_op, sems.at[3]))
    for copy in first + copies:
        copy.start()
    row = iota((FINE, FINE), 0)
    col = iota((FINE, FINE), 1)
    by_octant = (row == (col & 63) * 8 + (col >> 6)).astype(BF16)
    pick = child_columns()
    for copy in first:
        copy.wait()
    field = jnp.concatenate([check[0], check[1]], axis=1)
    by_real = mm(equiv[0], field)
    by_imag = mm(equiv[1], field)
    real = by_real[:, :FINE] - by_imag[:, FINE:]
    imag = by_real[:, FINE:] + by_imag[:, :FINE]
    dense = jnp.concatenate([real, imag], axis=0).astype(BF16)
    to_left[:, :REACH] = dense[:, :REACH]
    to_right[:, :REACH] = dense[:, REACH:]
    ordered = mm(dense, by_octant)
    children = []
    for pair in range(OCTANTS // 2):
        children += regroup(tile(ordered[:SIZE], pair), tile(ordered[SIZE:], pair))
    children = [child.astype(BF16) for child in children]
    packed = []
    for level in range(3):
        copies[level].wait()
        packed.append(apply_each(ops.at[level], lambda c: children[c], OCTANTS).astype(BF16))
        if level < 2:
            spread = mm(packed[level], pick).astype(BF16)
            children = [tile(spread, c) for c in range(OCTANTS)]
    both = jnp.concatenate([packed[0].astype(F32), packed[1].astype(F32)], axis=0).astype(BF16)
    to_left[:, REACH:] = both
    to_right[:, REACH:] = both
    copies[3].wait()
    part = combine(mm(own_op[0], packed[2]), mm(own_op[1], packed[2]))
    flat = jnp.transpose(jnp.concatenate([part, jnp.zeros((104, 128), F32)], axis=0))
    top[:, :256] = flat[0:1, :]
    top[:, 256:] = flat[HALF : HALF + 1, :]


def load_kernel(ride, transfer_hbm, ride_out, transfer, sem):
    ride_out[...] = ride[...]
    copy = pltpu.make_async_copy(transfer_hbm.at[3], transfer, sem)
    copy.start()
    copy.wait()


def device_position():
    return lax.axis_index("row") * lax.axis_size("col") + lax.axis_index("col")


def translate_packed(around, codes, targets, ops, copies):
    select = jnp.concatenate(
        [(codes == targets[k : k + 1, :]).astype(BF16) for k in range(ENTRIES)], axis=1
    )
    picked = mm(around, select).astype(BF16)
    by_real = jnp.zeros((SIZE, 128), F32)
    by_imag = jnp.zeros((SIZE, 128), F32)
    for k in range(ENTRIES):
        if k % GROUP == 0:
            copies[k // GROUP].wait()
        by_real += mm(ops[k, 0], tile(picked, k))
        by_imag += mm(ops[k, 1], tile(picked, k))
    return combine(by_real, by_imag)


def start_copies(ops_hbm, level, ops, sems):
    copies = []
    for group in range(ENTRIES // GROUP):
        part = pl.ds(group * GROUP, GROUP)
        copies.append(pltpu.make_async_copy(ops_hbm.at[level, part], ops.at[part], sems.at[group]))
        copies[group].start()
    return copies


def low_kernel(ride, from_left, from_right, own, low_list, ops_hbm, ride_out, out, ops, sems):
    ride_out[...] = ride[...]
    copies = start_copies(ops_hbm, 2, ops, sems)
    lows = [ref[:, REACH:].astype(F32)[SIZE:] for ref in (own, from_left, from_right)]
    around = (lows[0] + pltpu.roll(lows[1], 8, 1) + pltpu.roll(lows[2], 16, 1)).astype(BF16)
    row = iota((128, 128), 0)
    lane = row & 63
    place = jnp.where(lane < 8, lane, jnp.where(lane < 16, lane - 16, lane - 8))
    codes = jnp.where(lane < 24, (row >> 6) * 1024 + place, -(1 << 20)).astype(F32)
    index = (low_list[...] - device_position() * 8).astype(F32)
    listed = jnp.transpose(jnp.concatenate([index, jnp.zeros((8, 112), F32)], axis=1))[:ENTRIES]
    pad = jnp.full((ENTRIES, HALF - 8), -(1 << 19), F32)
    targets = jnp.concatenate([listed, pad, listed + 1024, pad], axis=1)
    out[...] = translate_packed(around, codes, targets, ops, copies)


def mid_kernel(ride, from_left, from_right, own, mid_t, ops_hbm, ride_out, out, ops, sems):
    ride_out[...] = ride[...]
    copies = start_copies(ops_hbm, 1, ops, sems)
    mids = [ref[:, REACH:].astype(F32)[:SIZE] for ref in (from_left, own, from_right)]
    around = jnp.concatenate(mids, axis=1).astype(BF16)
    row = iota((384, 128), 0)
    codes = ((row >> 6) & 1) * 1024 + (row & 63) + ((row >> 7) - 1) * HALF
    index = mid_t[...] - device_position() * HALF
    targets = jnp.concatenate([index, index + 1024], axis=1)
    out[...] = translate_packed(around, codes, targets, ops, copies)


def fine_kernel(part, ride, before, first, second, fine_t, ops_hbm, *refs):
    half, group = part
    earlier, (ride_out, out, window, picked, ops, sem) = refs[:-6], refs[-6:]
    ride_out[...] = ride[...]
    begin = group * GROUP
    copy = pltpu.make_async_copy(ops_hbm.at[0, pl.ds(begin, GROUP)], ops, sem)
    copy.start()
    window[:, :REACH] = before[:, :REACH]
    window[:, REACH : 2 * REACH] = first[:, :REACH]
    window[:, 2 * REACH :] = second[:, :REACH]
    index = fine_t[begin : begin + GROUP, half * REACH : (half + 1) * REACH]
    index = index - (device_position() * FINE + (half - 1) * REACH)
    row = iota((3 * REACH, REACH), 0)
    for k in range(GROUP):
        select = (row == index[k : k + 1, :]).astype(BF16)
        both = mm(window[...], select)
        picked[k, :, :REACH] = both[:SIZE].astype(BF16)
        picked[k, :, REACH:] = both[SIZE:].astype(BF16)
    copy.wait()
    by_real = jnp.zeros((SIZE, FINE), F32)
    by_imag = jnp.zeros((SIZE, FINE), F32)
    for k in range(GROUP):
        by_real += mm(ops[k, 0], picked[k])
        by_imag += mm(ops[k, 1], picked[k])
    real = by_real[:, :REACH] - by_imag[:, REACH:]
    imag = by_real[:, REACH:] + by_imag[:, :REACH]
    if earlier:
        real += earlier[0][0]
        imag += earlier[0][1]
    out[0] = real
    out[1] = imag


def down_kernel(
    tops, others, top_list, fine_a_hbm, fine_b_hbm, mid_near, low_near, transfer, down_hbm,
    out_hbm, out, near, down, own_op, sems,
):
    copies = [
        pltpu.make_async_copy(down_hbm.at[level], down.at[level], sems.at[level])
        for level in range(3)
    ]
    copies.append(pltpu.make_async_copy(down_hbm.at[3, lax.axis_index("col")], own_op, sems.at[3]))
    near_copies = [
        pltpu.make_async_copy(hbm, near.at[half], sems.at[4 + half])
        for half, hbm in enumerate((fine_a_hbm, fine_b_hbm))
    ]
    for copy in [copies[3], copies[2], copies[1], copies[0]] + near_copies:
        copy.start()
    wide = jnp.concatenate([tops[...].astype(F32), others[...].astype(F32)], axis=0)
    gap = jnp.zeros((HALF - wide.shape[0], 256), F32)
    rows = jnp.concatenate([wide[:, :256], gap, wide[:, 256:], gap], axis=0)
    dense = jnp.transpose(rows)[:SIZE].astype(BF16)
    own_row = lax.axis_index("row")
    place = top_list[...] ^ own_row
    place = place ^ ((place >> 1) & 0b01010)
    mine = iota(place.shape, 1) == own_row
    listed = jnp.sum(jnp.where(mine, place.astype(F32), 0.0), axis=1, keepdims=True)
    pad = jnp.full((HALF - ENTRIES, 1), -1.0, F32)
    wanted = jnp.concatenate([listed, pad, listed + HALF, pad], axis=0)
    select = (iota((128, 128), 1).astype(F32) == wanted).astype(BF16)
    picked = lax.dot_general(dense, select, (((1,), (1,)), ((), ())), preferred_element_type=F32)
    entry = iota((SIZE, 128), 1) & 63
    local = apply_each(transfer, lambda k: jnp.where(entry == k, picked, 0.0).astype(BF16), ENTRIES)
    for shift in (8, 4, 2, 1):
        local = local + pltpu.roll(local, 128 - shift, 1)
    local = jnp.where(entry == 0, local, 0.0).astype(BF16)
    copies[3].wait()
    local = combine(mm(own_op[0], local), mm(own_op[1], local)).astype(BF16)
    place = parent_columns()
    for level, at_level in ((2, low_near), (1, mid_near)):
        parents = mm(local, place).astype(BF16)
        copies[level].wait()
        local = apply_each(down.at[level], lambda c: tile(parents, c), OCTANTS) + at_level[...]
        local = local.astype(BF16)
    copies[0].wait()
    real, imag = [], []
    for pair in range(OCTANTS // 2):
        terms = [
            combine(mm(down[0, c, 0], local), mm(down[0, c, 1], local))
            for c in (2 * pair, 2 * pair + 1)
        ]
        one_real, one_imag = regroup(*terms)
        real.append(one_real)
        imag.append(one_imag)
    row = iota((FINE, FINE), 0)
    col = iota((FINE, FINE), 1)
    place = (row == (col & 7) * HALF + (col >> 3)).astype(BF16)
    for copy in near_copies:
        copy.wait()
    out_copies = []
    for part, terms in enumerate((real, imag)):
        term = jnp.concatenate(terms, axis=1)
        high = term.astype(BF16)
        low = (term - high.astype(F32)).astype(BF16)
        far = mm(high, place) + mm(low, place)
        out[part, :, :REACH] = near[0, part] + far[:, :REACH]
        out[part, :, REACH:] = near[1, part] + far[:, REACH:]
        out_copies.append(pltpu.make_async_copy(out.at[part], out_hbm.at[part], sems.at[6 + part]))
        out_copies[part].start()
    for copy in out_copies:
        copy.wait()


def shape(dims, dtype):
    return jax.ShapeDtypeStruct(dims, dtype)


VMEM = pl.BlockSpec(memory_space=pltpu.VMEM)
SMEM = pl.BlockSpec(memory_space=pltpu.SMEM)
HBM = pl.BlockSpec(memory_space=pltpu.HBM)
INTERPRET = False


def in_hbm(x):
    return x if INTERPRET else pltpu.with_memory_space_constraint(x, pltpu.HBM)


def on_chip(dims, dtype):
    return shape(dims, dtype) if INTERPRET else pltpu.VMEM(dims, dtype)


def call(kernel, ins, outs, scratch, flops, limit=16, place=VMEM):
    return pl.pallas_call(
        kernel,
        in_specs=ins,
        out_specs=[place] * len(outs),
        out_shape=outs,
        scratch_shapes=scratch,
        compiler_params=pltpu.CompilerParams(vmem_limit_bytes=limit << 20),
        cost_estimate=pl.CostEstimate(flops=flops, bytes_accessed=8 << 20, transcendentals=0),
        interpret=INTERPRET,
    )


def body(
    check_field, to_equiv, upward_ops, downward_ops, transfer_ops, list_fine, list_mid, list_low, list_top
):
    axes = ("row", "col")
    rows, cols = lax.axis_size("row"), lax.axis_size("col")
    count = rows * cols
    check_field, to_equiv, upward_ops, downward_ops, transfer_ops = [
        in_hbm(x) for x in (check_field, to_equiv, upward_ops, downward_ops, transfer_ops)
    ]
    octant_ops = (2, SIZE, SIZE)
    to_left, to_right, top = call(
        up_kernel,
        [HBM, HBM, HBM],
        [shape((2 * SIZE, 384), BF16), shape((2 * SIZE, 384), BF16), shape((1, 512), F32)],
        [
            pltpu.VMEM((2, SIZE, FINE), BF16),
            pltpu.VMEM(octant_ops, BF16),
            pltpu.VMEM((3, OCTANTS) + octant_ops, BF16),
            pltpu.VMEM(octant_ops, BF16),
            pltpu.SemaphoreType.DMA((6,)),
        ],
        4 << 30,
    )(check_field, to_equiv, upward_ops)
    from_left = lax.ppermute(to_right, axes, [(i, (i + 1) % count) for i in range(count)])
    from_right = lax.ppermute(to_left, axes, [(i, (i - 1) % count) for i in range(count)])

    def load(ride):
        return call(
            load_kernel,
            [VMEM, HBM],
            [shape(ride.shape, ride.dtype), on_chip((ENTRIES,) + octant_ops, BF16)],
            [pltpu.SemaphoreType.DMA(())],
            2 << 30,
        )(ride, transfer_ops)

    def small(kernel, listed, ride):
        return call(
            kernel,
            [VMEM] * 5 + [HBM],
            [shape(ride.shape, ride.dtype), shape((SIZE, 128), F32)],
            [pltpu.VMEM((ENTRIES,) + octant_ops, BF16), pltpu.SemaphoreType.DMA((2,))],
            3 << 30,
        )(ride, from_left, from_right, to_left, listed, transfer_ops)

    def fine(half, group, earlier, ride):
        around = (from_left, to_left, to_right) if half == 0 else (to_left, to_right, from_right)
        return call(
            functools.partial(fine_kernel, (half, group)),
            [VMEM] * 5 + [HBM] + [VMEM] * len(earlier),
            [shape(ride.shape, ride.dtype), shape((2, SIZE, REACH), F32)],
            [
                pltpu.VMEM((2 * SIZE, 3 * REACH), BF16),
                pltpu.VMEM((GROUP, SIZE, FINE), BF16),
                pltpu.VMEM((GROUP,) + octant_ops, BF16),
                pltpu.SemaphoreType.DMA(()),
            ],
            4 << 30,
        )(ride, *around, list_fine.T, transfer_ops, *earlier)

    def swap(x, axis, mask):
        return lax.ppermute(x, axis, [(i, i ^ mask) for i in range(lax.axis_size(axis))])

    work = {
        1: lambda ride: fine(0, 0, [], ride),
        2: lambda ride: fine(0, 1, done[1], ride),
        3: lambda ride: fine(1, 0, [], ride),
        4: lambda ride: fine(1, 1, done[3], ride),
        5: functools.partial(small, mid_kernel, list_mid.T),
        6: functools.partial(small, low_kernel, list_low),
        7: load,
    }
    done = {}
    total = top
    for step, mask in enumerate((1, 2, 6, 1, 2, 6, 8, 24)):
        axis = "col" if step < 3 else "row"
        other = swap(total, axis, mask) if axis == "col" or mask < rows else None
        if step in work:
            total, *done[step] = work[step](total)
        if axis == "col":
            total = total + other
        elif step < 7:
            total = total if other is None else jnp.concatenate([total, other], axis=0)
        if step == 2:
            total = total.astype(BF16)
    other = total if other is None else other
    (far,) = call(
        down_kernel,
        [VMEM] * 3 + [HBM] * 2 + [VMEM] * 3 + [HBM],
        [shape((2, SIZE, FINE), F32)],
        [
            pltpu.VMEM((2, SIZE, FINE), F32),
            pltpu.VMEM((2, 2, SIZE, REACH), F32),
            pltpu.VMEM((3, OCTANTS) + octant_ops, BF16),
            pltpu.VMEM(octant_ops, BF16),
            pltpu.SemaphoreType.DMA((8,)),
        ],
        8 << 30,
        place=HBM,
    )(
        total, other, list_top.T, in_hbm(done[2][0]), in_hbm(done[4][0]), *done[5], *done[6], *done[7],
        downward_ops,
    )
    return far


def solution(mesh):
    split = P(None, None, ("row", "col"))
    lists = P(("row", "col"), None)
    return jax.shard_map(
        body,
        mesh=mesh,
        in_specs=(split, P(), P(), P(), P(), lists, lists, lists, P()),
        out_specs=split,
        check_vma=False,
    )
```

time: 57.9 us -> 54.3 us (0.938)
  the two profiles are of different devices: /device:TPU:24 before, /device:TPU:2 now
where the time goes in v4:
time: 54.3 us; the launch traced here: 54 us
  Pallas kernels  28.8 us (53%)
  starting transfers between devices  18.4 us (34%)
  waiting for transfers between devices  5.6 us (10%)
  local copies, waits for them, and re-layouts  0.73 us (1%)
    ppermute x8, starting transfers between devices, swap(): lax.ppermute(x, axis, [(i, i ^ mask) for i in range(lax.axis_size(axis))])  13.5 us
    pallas_call x4, Pallas kernels, fine(): call(functools.partial(fine_kernel, (half, group)), [VMEM] * 5 + [HBM] +...  12.6 us
    pallas_call x1, Pallas kernels, body(): call(down_kernel, [VMEM] * 3 + [HBM] * 2 + [VMEM] * 3 + [HBM], [shape((2,...  5.44 us
    ppermute x8, waiting for transfers between devices, swap(): lax.ppermute(x, axis, [(i, i ^ mask) for i in range(lax.axis_size(axis))])  5.09 us
    pallas_call x2, Pallas kernels, small(): call(kernel, [VMEM] * 5 + [HBM], [shape(ride.shape, ride.dtype), shape((S...  4.74 us
    pallas_call x1, Pallas kernels, body(): call(up_kernel, [HBM, HBM, HBM], [shape((2 * SIZE, 384), BF16), shape((2...  4.35 us
    ppermute x1, starting transfers between devices, body(): lax.ppermute(to_left, axes, [(i, (i - 1) % count) for i in range(count)])  2.9 us
    ppermute x1, starting transfers between devices, body(): lax.ppermute(to_right, axes, [(i, (i + 1) % count) for i in range(count)])  1.99 us
  transfers between devices with their start and end apart: 10, of which 5 were waited for; matrix products, arithmetic and copies ran while one was open for 0% of the time, Pallas kernels for 35%

profile of v4, /device:TPU:2, one launch (start us, length us, event | category | flops | bytes accessed | tf_op | source)
XLA Modules:
  0.0 54.0 jit_solution(5796953513845851476)
XLA Ops:
  0.0 0.0 copy-start
  0.0 4.3 %shard_map.91 = (bf16[304,384]{1,0:T(8,128)(2,1)S(1)}, bf16[304,384]{1,0:T(8,128)(2,1)S(1)}, f32[1,512]{1,0:T(1,128)S(1)}) custom-call(bf16[2,152,512]{2,1,0:T(8,128)(2,1)} %check_hbm.1, bf16[2,152,152]{2,1,0:T(8,128)(2,1)} %equiv_hbm.1, bf16[4,8,2,152,152]{4,3,2,1,0:T(8,128)(2,1)} %ops_hbm.7), custom_call_target="tpu_custom_call" | custom-call | flops 4294967296 | bytes 8388608 | tf_op jit(solution)/shard_map/pallas_call | solution.py:331
  4.4 2.0 %collective-permute-start.1 = (bf16[304,384]{1,0:T(8,128)(2,1)S(1)}, bf16[304,384]{1,0:T(8,128)(2,1)S(1)}, u32[]{:S(2)}, u32[]{:S(2)}) collective-permute-start(bf16[304,384]{1,0:T(8,128)(2,1)S(1)} %get-tuple-element.23.second.first), channel_id=1, source_target_pairs={{0,1},{1,2},{2,3},{3,4},{4,5},{5,6},{6,7},{7,8},{8,9},{9,10},{10,1... | collective-permute-start | bytes 700424 | tf_op jit(solution)/shard_map/ppermute | solution.py:344
  6.4 1.9 %collective-permute-start = (f32[1,512]{1,0:T(1,128)S(1)}, f32[1,512]{1,0:T(1,128)S(1)}, u32[]{:S(2)}, u32[]{:S(2)}) collective-permute-start(f32[1,512]{1,0:T(1,128)S(1)} %get-tuple-element.22), channel_id=1, source_target_pairs={{0,1},{1,0},{2,3},{3,2},{4,5},{5,4},{6,7},{7,6},{8,9},{9,8},{10,11... | collective-permute-start | bytes 6152 | tf_op jit(solution)/shard_map/ppermute | solution.py:381
  8.3 2.9 %collective-permute-start.4 = (bf16[304,384]{1,0:T(8,128)(2,1)S(1)}, bf16[304,384]{1,0:T(8,128)(2,1)S(1)}, u32[]{:S(2)}, u32[]{:S(2)}) collective-permute-start(bf16[304,384]{1,0:T(8,128)(2,1)S(1)} %get-tuple-element.24.first.before.own), channel_id=1, source_target_pairs={{0,255},{1,0},{2,1},{3,2},{4,3},{5,4},{6,5},{7,6},{8,7},{9,8},{10,... | collective-permute-start | bytes 700424 | tf_op jit(solution)/shard_map/ppermute | solution.py:345
  11.2 0.2 collective-permute-done
  11.4 3.3 %collective-permute-start.2 = (f32[1,512]{1,0:T(1,128)S(1)}, f32[1,512]{1,0:T(1,128)S(1)}, u32[]{:S(2)}, u32[]{:S(2)}) collective-permute-start(f32[1,512]{1,0:T(1,128)S(1)} %add.9.ride), channel_id=1, source_target_pairs={{0,2},{1,3},{2,0},{3,1},{4,6},{5,7},{6,4},{7,5},{8,10},{9,11},{10,... | collective-permute-start | bytes 6152 | tf_op jit(solution)/shard_map/ppermute | solution.py:381
  14.6 0.5 collective-permute-done.1.before.from_left
  15.1 0.0 copy-done
  15.1 3.1 %shard_map.92 = (f32[1,512]{1,0:T(1,128)S(1)}, f32[2,152,256]{2,1,0:T(8,128)S(1)}) custom-call(f32[1,512]{1,0:T(1,128)S(1)} %add.9.ride, bf16[304,384]{1,0:T(8,128)(2,1)S(1)} %collective-permute-done.1.before.from_left, bf16[304,384]{1,0:T(8,128)(2,1)S(1)} %get-tuple-element.24.first.before.own, bf16[304,384]{1,0:T(8,128)(2,1)S(1)} %get-tuple-element.23.second.first, ...), custom_call_target="tpu_custom_call" | custom-call | flops 4294967296 | bytes 8388608 | tf_op jit(solution)/shard_map/pallas_call | solution.py:367
  18.3 0.0 collective-permute-done.2
  18.3 3.2 %collective-permute-start.3 = (f32[1,512]{1,0:T(1,128)S(1)}, f32[1,512]{1,0:T(1,128)S(1)}, u32[]{:S(2)}, u32[]{:S(2)}) collective-permute-start(f32[1,512]{1,0:T(1,128)S(1)} %add.10.ride), channel_id=1, source_target_pairs={{0,6},{1,7},{2,4},{3,5},{4,2},{5,3},{6,0},{7,1},{8,14},{9,15},{10,... | collective-permute-start | bytes 6152 | tf_op jit(solution)/shard_map/ppermute | solution.py:381
  21.5 3.2 %shard_map.93 = (f32[1,512]{1,0:T(1,128)S(1)}, f32[2,152,256]{2,1,0:T(8,128)S(1)}) custom-call(f32[1,512]{1,0:T(1,128)S(1)} %add.10.ride, bf16[304,384]{1,0:T(8,128)(2,1)S(1)} %collective-permute-done.1.before.from_left, bf16[304,384]{1,0:T(8,128)(2,1)S(1)} %get-tuple-element.24.first.before.own, bf16[304,384]{1,0:T(8,128)(2,1)S(1)} %get-tuple-element.23.second.first, ...), custom_call_target="tpu_custom_call" | custom-call | flops 4294967296 | bytes 8388608 | tf_op jit(solution)/shard_map/pallas_call | solution.py:367
  24.6 0.0 copy-start.4
  24.7 0.7 %copy-done.4 = f32[2,152,256]{2,1,0:T(8,128)} copy-done((f32[2,152,256]{2,1,0:T(8,128)}, f32[2,152,256]{2,1,0:T(8,128)S(1)}, u32[]{:S(2)}) %copy-start.4) | copy-done | bytes 311320
  25.4 0.0 collective-permute-done.3
  25.4 0.1 collective-permute-start.5
  25.5 0.0 collective-permute-done.4.second.from_right
  25.5 3.1 %shard_map.94 = (bf16[1,512]{1,0:T(2,128)(2,1)S(1)}, f32[2,152,256]{2,1,0:T(8,128)S(1)}) custom-call(bf16[1,512]{1,0:T(2,128)(2,1)S(1)} %add_convert_fusion.ride, bf16[304,384]{1,0:T(8,128)(2,1)S(1)} %get-tuple-element.24.first.before.own, bf16[304,384]{1,0:T(8,128)(2,1)S(1)} %get-tuple-element.23.second.first, ...), custom_call_target="tpu_custom_call" | custom-call | flops 4294967296 | bytes 8388608 | tf_op jit(solution)/shard_map/pallas_call | solution.py:367
  28.6 0.0 collective-permute-done.5
  28.7 4.1 %collective-permute-start.6 = (bf16[2,512]{1,0:T(2,128)(2,1)S(1)}, bf16[2,512]{1,0:T(2,128)(2,1)S(1)}, u32[]{:S(2)}, u32[]{:S(2)}) collective-permute-start(bf16[2,512]{1,0:T(2,128)(2,1)S(1)} %pad_maximum_fusion.2.ride), channel_id=1, source_target_pairs={{0,16},{8,24},{16,0},{24,8},{32,48},{40,56},{48,32},{56,40},{64,80... | collective-permute-start | bytes 6152 | tf_op jit(solution)/shard_map/ppermute | solution.py:381
  32.8 0.0 copy-start.1
  32.8 3.2 %shard_map.95 = (bf16[2,512]{1,0:T(2,128)(2,1)S(1)}, f32[2,152,256]{2,1,0:T(8,128)S(1)}) custom-call(bf16[2,512]{1,0:T(2,128)(2,1)S(1)} %pad_maximum_fusion.2.ride, bf16[304,384]{1,0:T(8,128)(2,1)S(1)} %get-tuple-element.24.first.before.own, bf16[304,384]{1,0:T(8,128)(2,1)S(1)} %get-tuple-element.23.second.first, ...), custom_call_target="tpu_custom_call" | custom-call | flops 4294967296 | bytes 8388608 | tf_op jit(solution)/shard_map/pallas_call | solution.py:367
  35.9 0.0 copy-start.5
  35.9 0.0 collective-permute-done.6
  36.0 0.1 collective-permute-start.7
  36.1 0.0 copy-done.1
  36.1 0.0 copy-start.3
  36.1 2.3 %shard_map.96 = (bf16[4,512]{1,0:T(4,128)(2,1)S(1)}, f32[152,128]{1,0:T(8,128)S(1)}) custom-call(bf16[4,512]{1,0:T(4,128)(2,1)S(1)} %pad_maximum_fusion.1.ride, bf16[304,384]{1,0:T(8,128)(2,1)S(1)} %collective-permute-done.1.before.from_left, bf16[304,384]{1,0:T(8,128)(2,1)S(1)} %collective-permute-done.4.second.from_right, ...), custom_call_target="tpu_custom_call" | custom-call | flops 3221225472 | bytes 8388608 | tf_op jit(solution)/shard_map/pallas_call | solution.py:357
  38.4 0.0 copy-done.5
  38.4 1.2 %collective-permute-done.7 = bf16[4,512]{1,0:T(4,128)(2,1)S(1)} collective-permute-done((bf16[4,512]{1,0:T(4,128)(2,1)S(1)}, bf16[4,512]{1,0:T(4,128)(2,1)S(1)}, u32[]{:S(2)}, u32[]{:S(2)}) %collective-permute-start.7) | collective-permute-done | bytes 4128 | tf_op jit(solution)/shard_map/ppermute | solution.py:381
  39.7 0.1 collective-permute-start.8
  39.8 0.0 copy-done.3
  39.8 2.4 %shard_map.97 = (bf16[8,512]{1,0:T(8,128)(2,1)S(1)}, f32[152,128]{1,0:T(8,128)S(1)}) custom-call(bf16[8,512]{1,0:T(8,128)(2,1)S(1)} %pad_maximum_fusion.ride, bf16[304,384]{1,0:T(8,128)(2,1)S(1)} %collective-permute-done.1.before.from_left, bf16[304,384]{1,0:T(8,128)(2,1)S(1)} %collective-permute-done.4.second.from_right, ...), custom_call_target="tpu_custom_call" | custom-call | flops 3221225472 | bytes 8388608 | tf_op jit(solution)/shard_map/pallas_call | solution.py:357
  42.2 1.2 %collective-permute-done.8 = bf16[8,512]{1,0:T(8,128)(2,1)S(1)} collective-permute-done((bf16[8,512]{1,0:T(8,128)(2,1)S(1)}, bf16[8,512]{1,0:T(8,128)(2,1)S(1)}, u32[]{:S(2)}, u32[]{:S(2)}) %collective-permute-start.8) | collective-permute-done | bytes 8224 | tf_op jit(solution)/shard_map/ppermute | solution.py:381
  43.4 0.0 copy-start.2
  43.4 0.7 %collective-permute-start.9 = (bf16[16,512]{1,0:T(8,128)(2,1)S(1)}, bf16[16,512]{1,0:T(8,128)(2,1)S(1)}, u32[]{:S(2)}, u32[]{:S(2)}) collective-permute-start(bf16[16,512]{1,0:T(8,128)(2,1)S(1)} %constant_dynamic-update-slice_fusion.ride), channel_id=1, source_target_pairs={{0,192},{8,200},{16,208},{24,216},{32,224},{40,232},{48,240},{56,2... | collective-permute-start | bytes 49160 | tf_op jit(solution)/shard_map/ppermute | solution.py:381
  44.1 1.7 %shard_map.98 = (bf16[16,512]{1,0:T(8,128)(2,1)S(1)}, bf16[16,2,152,152]{3,2,1,0:T(8,128)(2,1)S(1)}) custom-call(bf16[16,512]{1,0:T(8,128)(2,1)S(1)} %constant_dynamic-update-slice_fusion.ride, bf16[4,16,2,152,152]{4,3,2,1,0:T(8,128)(2,1)} %transfer_hbm.1), custom_call_target="tpu_custom_call" | custom-call | flops 2147483648 | bytes 8388608 | tf_op jit(solution)/shard_map/pallas_call | solution.py:348
  45.9 2.5 %collective-permute-done.9.others = bf16[16,512]{1,0:T(8,128)(2,1)S(1)} collective-permute-done((bf16[16,512]{1,0:T(8,128)(2,1)S(1)}, bf16[16,512]{1,0:T(8,128)(2,1)S(1)}, u32[]{:S(2)}, u32[]{:S(2)}) %collective-permute-start.9) | collective-permute-done | bytes 16416 | tf_op jit(solution)/shard_map/ppermute | solution.py:381
  48.4 0.0 copy-done.2
  48.4 5.4 %shard_map.99 = f32[2,152,512]{2,1,0:T(8,128)} custom-call(bf16[16,512]{1,0:T(8,128)(2,1)S(1)} %get-tuple-element.33.tops, bf16[16,512]{1,0:T(8,128)(2,1)S(1)} %collective-permute-done.9.others, s32[16,32]{1,0:T(8,128)S(1)} %bitcast.8, f32[2,152,256]{2,1,0:T(8,128)} %copy-done.4, f32[2,152,256]{2,1,0:T(8,128)} %copy-done.5, ...), custom_call_target="tpu_custom_call" | custom-call | flops 8589934592 | bytes 8388608 | tf_op jit(solution)/shard_map/pallas_call | solution.py:406
  (8 shorter events, 0.1 us)
Async XLA Ops:
  0.0 15.1 %copy-start = (s32[512,16]{0,1:T(8,128)S(1)}, s32[512,16]{0,1:T(8,128)}, u32[]{:S(2)}) copy-start(s32[512,16]{0,1:T(8,128)} %param.14) | copy-start | bytes 98308
  4.4 10.8 %collective-permute-start.1 = (bf16[304,384]{1,0:T(8,128)(2,1)S(1)}, bf16[304,384]{1,0:T(8,128)(2,1)S(1)}, u32[]{:S(2)}, u32[]{:S(2)}) collective-permute-start(bf16[304,384]{1,0:T(8,128)(2,1)S(1)} %get-tuple-element.23.second.first), channel_id=1, source_target_pairs={{0,1},{1,2},{2,3},{3,4},{4,5},{5,6},{6,7},{7,8},{8,9},{9,10},{10,1... | collective-permute-start | bytes 700424 | tf_op jit(solution)/shard_map/ppermute | solution.py:344
  6.4 5.0 %collective-permute-start = (f32[1,512]{1,0:T(1,128)S(1)}, f32[1,512]{1,0:T(1,128)S(1)}, u32[]{:S(2)}, u32[]{:S(2)}) collective-permute-start(f32[1,512]{1,0:T(1,128)S(1)} %get-tuple-element.22), channel_id=1, source_target_pairs={{0,1},{1,0},{2,3},{3,2},{4,5},{5,4},{6,7},{7,6},{8,9},{9,8},{10,11... | collective-permute-start | bytes 6152 | tf_op jit(solution)/shard_map/ppermute | solution.py:381
  8.3 17.2 %collective-permute-start.4 = (bf16[304,384]{1,0:T(8,128)(2,1)S(1)}, bf16[304,384]{1,0:T(8,128)(2,1)S(1)}, u32[]{:S(2)}, u32[]{:S(2)}) collective-permute-start(bf16[304,384]{1,0:T(8,128)(2,1)S(1)} %get-tuple-element.24.first.before.own), channel_id=1, source_target_pairs={{0,255},{1,0},{2,1},{3,2},{4,3},{5,4},{6,5},{7,6},{8,7},{9,8},{10,... | collective-permute-start | bytes 700424 | tf_op jit(solution)/shard_map/ppermute | solution.py:345
  11.4 6.9 %collective-permute-start.2 = (f32[1,512]{1,0:T(1,128)S(1)}, f32[1,512]{1,0:T(1,128)S(1)}, u32[]{:S(2)}, u32[]{:S(2)}) collective-permute-start(f32[1,512]{1,0:T(1,128)S(1)} %add.9.ride), channel_id=1, source_target_pairs={{0,2},{1,3},{2,0},{3,1},{4,6},{5,7},{6,4},{7,5},{8,10},{9,11},{10,... | collective-permute-start | bytes 6152 | tf_op jit(solution)/shard_map/ppermute | solution.py:381
  18.3 7.1 %collective-permute-start.3 = (f32[1,512]{1,0:T(1,128)S(1)}, f32[1,512]{1,0:T(1,128)S(1)}, u32[]{:S(2)}, u32[]{:S(2)}) collective-permute-start(f32[1,512]{1,0:T(1,128)S(1)} %add.10.ride), channel_id=1, source_target_pairs={{0,6},{1,7},{2,4},{3,5},{4,2},{5,3},{6,0},{7,1},{8,14},{9,15},{10,... | collective-permute-start | bytes 6152 | tf_op jit(solution)/shard_map/ppermute | solution.py:381
  24.6 0.7 %copy-start.4 = (f32[2,152,256]{2,1,0:T(8,128)}, f32[2,152,256]{2,1,0:T(8,128)S(1)}, u32[]{:S(2)}) copy-start(f32[2,152,256]{2,1,0:T(8,128)S(1)} %get-tuple-element.34.fine_a_hbm) | copy-start | bytes 933892
  25.4 3.3 %collective-permute-start.5 = (bf16[1,512]{1,0:T(2,128)(2,1)S(1)}, bf16[1,512]{1,0:T(2,128)(2,1)S(1)}, u32[]{:S(2)}, u32[]{:S(2)}) collective-permute-start(bf16[1,512]{1,0:T(2,128)(2,1)S(1)} %add_convert_fusion.ride), channel_id=1, source_target_pairs={{0,8},{8,0},{16,24},{24,16},{32,40},{40,32},{48,56},{56,48},{64,72... | collective-permute-start | bytes 3080 | tf_op jit(solution)/shard_map/ppermute | solution.py:381
  28.7 7.3 %collective-permute-start.6 = (bf16[2,512]{1,0:T(2,128)(2,1)S(1)}, bf16[2,512]{1,0:T(2,128)(2,1)S(1)}, u32[]{:S(2)}, u32[]{:S(2)}) collective-permute-start(bf16[2,512]{1,0:T(2,128)(2,1)S(1)} %pad_maximum_fusion.2.ride), channel_id=1, source_target_pairs={{0,16},{8,24},{16,0},{24,8},{32,48},{40,56},{48,32},{56,40},{64,80... | collective-permute-start | bytes 6152 | tf_op jit(solution)/shard_map/ppermute | solution.py:381
  32.8 3.3 %copy-start.1 = (s32[64,16]{0,1:T(8,128)S(1)}, s32[64,16]{0,1:T(8,128)}, u32[]{:S(2)}) copy-start(s32[64,16]{0,1:T(8,128)} %param.15) | copy-start | bytes 12292
  35.9 2.5 %copy-start.5 = (f32[2,152,256]{2,1,0:T(8,128)}, f32[2,152,256]{2,1,0:T(8,128)S(1)}, u32[]{:S(2)}) copy-start(f32[2,152,256]{2,1,0:T(8,128)S(1)} %get-tuple-element.35.fine_b_hbm) | copy-start | bytes 933892
  36.0 3.7 %collective-permute-start.7 = (bf16[4,512]{1,0:T(4,128)(2,1)S(1)}, bf16[4,512]{1,0:T(4,128)(2,1)S(1)}, u32[]{:S(2)}, u32[]{:S(2)}) collective-permute-start(bf16[4,512]{1,0:T(4,128)(2,1)S(1)} %pad_maximum_fusion.1.ride), channel_id=1, source_target_pairs={{0,48},{8,56},{16,32},{24,40},{32,16},{40,24},{48,0},{56,8},{64,11... | collective-permute-start | bytes 12296 | tf_op jit(solution)/shard_map/ppermute | solution.py:381
  36.1 3.7 %copy-start.3 = (s32[8,16]{1,0:T(8,128)S(1)}, s32[8,16]{1,0:T(8,128)}, u32[]{:S(2)}) copy-start(s32[8,16]{1,0:T(8,128)} %low_list.1) | copy-start | bytes 1540
  39.7 3.7 %collective-permute-start.8 = (bf16[8,512]{1,0:T(8,128)(2,1)S(1)}, bf16[8,512]{1,0:T(8,128)(2,1)S(1)}, u32[]{:S(2)}, u32[]{:S(2)}) collective-permute-start(bf16[8,512]{1,0:T(8,128)(2,1)S(1)} %pad_maximum_fusion.ride), channel_id=1, source_target_pairs={{0,64},{8,72},{16,80},{24,88},{32,96},{40,104},{48,112},{56,120},{... | collective-permute-start | bytes 24584 | tf_op jit(solution)/shard_map/ppermute | solution.py:381
  43.4 5.0 %copy-start.2 = (s32[32,16]{0,1:T(8,128)S(1)}, s32[32,16]{0,1:T(8,128)}, u32[]{:S(2)}) copy-start(s32[32,16]{0,1:T(8,128)} %param.17) | copy-start | bytes 6148
  43.4 4.9 %collective-permute-start.9 = (bf16[16,512]{1,0:T(8,128)(2,1)S(1)}, bf16[16,512]{1,0:T(8,128)(2,1)S(1)}, u32[]{:S(2)}, u32[]{:S(2)}) collective-permute-start(bf16[16,512]{1,0:T(8,128)(2,1)S(1)} %constant_dynamic-update-slice_fusion.ride), channel_id=1, source_target_pairs={{0,192},{8,200},{16,208},{24,216},{32,224},{40,232},{48,240},{56,2... | collective-permute-start | bytes 49160 | tf_op jit(solution)/shard_map/ppermute | solution.py:381

commit v5 on v4

--- a/solution.py
+++ b/solution.py
@@ -71,8 +71,28 @@
     return array[:, 128 * index : 128 * (index + 1)]
 
 
+def pass_on(ride, ride_out):
+    def step(i, carry):
+        part = pl.ds(pl.multiple_of(i * 256, 256), 256)
+        ride_out[:, part] = ride[:, part]
+        return carry
+
+    lax.fori_loop(0, 2, step, 0)
+
+
+def fill_places(places, row_to_col):
+    def step(i, carry):
+        begin = pl.multiple_of(i * 256, 256)
+        row = iota((256, FINE), 0) + begin
+        col = iota((256, FINE), 1)
+        places[pl.ds(begin, 256), :] = (row == row_to_col(col)).astype(BF16)
+        return carry
+
+    lax.fori_loop(0, 2, step, 0)
+
+
 def up_kernel(
-    check_hbm, equiv_hbm, ops_hbm, to_left, to_right, top, check, equiv, ops, own_op, sems
+    check_hbm, equiv_hbm, ops_hbm, to_left, to_right, top, check, equiv, ops, own_op, by_octant, sems
 ):
     first = [
         pltpu.make_async_copy(equiv_hbm, equiv, sems.at[4]),
@@ -85,9 +105,7 @@
     copies.append(pltpu.make_async_copy(ops_hbm.at[3, lax.axis_index("col")], own_op, sems.at[3]))
     for copy in first + copies:
         copy.start()
-    row = iota((FINE, FINE), 0)
-    col = iota((FINE, FINE), 1)
-    by_octant = (row == (col & 63) * 8 + (col >> 6)).astype(BF16)
+    fill_places(by_octant, lambda col: (col & 63) * 8 + (col >> 6))
     pick = child_columns()
     for copy in first:
         copy.wait()
@@ -99,7 +117,7 @@
     dense = jnp.concatenate([real, imag], axis=0).astype(BF16)
     to_left[:, :REACH] = dense[:, :REACH]
     to_right[:, :REACH] = dense[:, REACH:]
-    ordered = mm(dense, by_octant)
+    ordered = mm(dense, by_octant[...])
     children = []
     for pair in range(OCTANTS // 2):
         children += regroup(tile(ordered[:SIZE], pair), tile(ordered[SIZE:], pair))
@@ -122,9 +140,9 @@
 
 
 def load_kernel(ride, transfer_hbm, ride_out, transfer, sem):
-    ride_out[...] = ride[...]
     copy = pltpu.make_async_copy(transfer_hbm.at[3], transfer, sem)
     copy.start()
+    ride_out[...] = ride[...]
     copy.wait()
 
 
@@ -157,8 +175,8 @@
 
 
 def low_kernel(ride, from_left, from_right, own, low_list, ops_hbm, ride_out, out, ops, sems):
-    ride_out[...] = ride[...]
     copies = start_copies(ops_hbm, 2, ops, sems)
+    pass_on(ride, ride_out)
     lows = [ref[:, REACH:].astype(F32)[SIZE:] for ref in (own, from_left, from_right)]
     around = (lows[0] + pltpu.roll(lows[1], 8, 1) + pltpu.roll(lows[2], 16, 1)).astype(BF16)
     row = iota((128, 128), 0)
@@ -173,8 +191,8 @@
 
 
 def mid_kernel(ride, from_left, from_right, own, mid_t, ops_hbm, ride_out, out, ops, sems):
-    ride_out[...] = ride[...]
     copies = start_copies(ops_hbm, 1, ops, sems)
+    pass_on(ride, ride_out)
     mids = [ref[:, REACH:].astype(F32)[:SIZE] for ref in (from_left, own, from_right)]
     around = jnp.concatenate(mids, axis=1).astype(BF16)
     row = iota((384, 128), 0)
@@ -187,10 +205,10 @@
 def fine_kernel(part, ride, before, first, second, fine_t, ops_hbm, *refs):
     half, group = part
     earlier, (ride_out, out, window, picked, ops, sem) = refs[:-6], refs[-6:]
-    ride_out[...] = ride[...]
     begin = group * GROUP
     copy = pltpu.make_async_copy(ops_hbm.at[0, pl.ds(begin, GROUP)], ops, sem)
     copy.start()
+    pass_on(ride, ride_out)
     window[:, :REACH] = before[:, :REACH]
     window[:, REACH : 2 * REACH] = first[:, :REACH]
     window[:, 2 * REACH :] = second[:, :REACH]
@@ -219,7 +237,7 @@
 
 def down_kernel(
     tops, others, top_list, fine_a_hbm, fine_b_hbm, mid_near, low_near, transfer, down_hbm,
-    out_hbm, out, near, down, own_op, sems,
+    out_hbm, out, near, down, own_op, places, sems,
 ):
     copies = [
         pltpu.make_async_copy(down_hbm.at[level], down.at[level], sems.at[level])
@@ -232,6 +250,7 @@
     ]
     for copy in [copies[3], copies[2], copies[1], copies[0]] + near_copies:
         copy.start()
+    fill_places(places, lambda col: (col & 7) * HALF + (col >> 3))
     wide = jnp.concatenate([tops[...].astype(F32), others[...].astype(F32)], axis=0)
     gap = jnp.zeros((HALF - wide.shape[0], 256), F32)
     rows = jnp.concatenate([wide[:, :256], gap, wide[:, 256:], gap], axis=0)
@@ -268,9 +287,6 @@
         one_real, one_imag = regroup(*terms)
         real.append(one_real)
         imag.append(one_imag)
-    row = iota((FINE, FINE), 0)
-    col = iota((FINE, FINE), 1)
-    place = (row == (col & 7) * HALF + (col >> 3)).astype(BF16)
     for copy in near_copies:
         copy.wait()
     out_copies = []
@@ -278,7 +294,7 @@
         term = jnp.concatenate(terms, axis=1)
         high = term.astype(BF16)
         low = (term - high.astype(F32)).astype(BF16)
-        far = mm(high, place) + mm(low, place)
+        far = mm(high, places[...]) + mm(low, places[...])
         out[part, :, :REACH] = near[0, part] + far[:, :REACH]
         out[part, :, REACH:] = near[1, part] + far[:, REACH:]
         out_copies.append(pltpu.make_async_copy(out.at[part], out_hbm.at[part], sems.at[6 + part]))
@@ -303,6 +319,10 @@
 
 def on_chip(dims, dtype):
     return shape(dims, dtype) if INTERPRET else pltpu.VMEM(dims, dtype)
+
+
+def off_chip(dims, dtype):
+    return shape(dims, dtype) if INTERPRET else pltpu.HBM(dims, dtype)
 
 
 def call(kernel, ins, outs, scratch, flops, limit=16, place=VMEM):
@@ -337,6 +357,7 @@
             pltpu.VMEM(octant_ops, BF16),
             pltpu.VMEM((3, OCTANTS) + octant_ops, BF16),
             pltpu.VMEM(octant_ops, BF16),
+            pltpu.VMEM((FINE, FINE), BF16),
             pltpu.SemaphoreType.DMA((6,)),
         ],
         4 << 30,
@@ -350,7 +371,7 @@
             [VMEM, HBM],
             [shape(ride.shape, ride.dtype), on_chip((ENTRIES,) + octant_ops, BF16)],
             [pltpu.SemaphoreType.DMA(())],
-            2 << 30,
+            8 << 30,
         )(ride, transfer_ops)
 
     def small(kernel, listed, ride):
@@ -367,7 +388,7 @@
         return call(
             functools.partial(fine_kernel, (half, group)),
             [VMEM] * 5 + [HBM] + [VMEM] * len(earlier),
-            [shape(ride.shape, ride.dtype), shape((2, SIZE, REACH), F32)],
+            [shape(ride.shape, ride.dtype), (off_chip if group else shape)((2, SIZE, REACH), F32)],
             [
                 pltpu.VMEM((2 * SIZE, 3 * REACH), BF16),
                 pltpu.VMEM((GROUP, SIZE, FINE), BF16),
@@ -381,13 +402,13 @@
         return lax.ppermute(x, axis, [(i, i ^ mask) for i in range(lax.axis_size(axis))])
 
     work = {
-        1: lambda ride: fine(0, 0, [], ride),
-        2: lambda ride: fine(0, 1, done[1], ride),
-        3: lambda ride: fine(1, 0, [], ride),
-        4: lambda ride: fine(1, 1, done[3], ride),
-        5: functools.partial(small, mid_kernel, list_mid.T),
-        6: functools.partial(small, low_kernel, list_low),
-        7: load,
+        1: load,
+        2: lambda ride: fine(0, 0, [], ride),
+        3: lambda ride: fine(0, 1, done[2], ride),
+        4: lambda ride: fine(1, 0, [], ride),
+        5: lambda ride: fine(1, 1, done[4], ride),
+        6: functools.partial(small, mid_kernel, list_mid.T),
+        7: functools.partial(small, low_kernel, list_low),
     }
     done = {}
     total = top
@@ -412,12 +433,13 @@
             pltpu.VMEM((2, 2, SIZE, REACH), F32),
             pltpu.VMEM((3, OCTANTS) + octant_ops, BF16),
             pltpu.VMEM(octant_ops, BF16),
+            pltpu.VMEM((FINE, FINE), BF16),
             pltpu.SemaphoreType.DMA((8,)),
         ],
         8 << 30,
         place=HBM,
     )(
-        total, other, list_top.T, in_hbm(done[2][0]), in_hbm(done[4][0]), *done[5], *done[6], *done[7],
+        total, other, list_top.T, in_hbm(done[3][0]), in_hbm(done[5][0]), *done[6], *done[7], *done[1],
         downward_ops,
     )
     return far

time: 54.3 us -> 50.3 us (0.926); the launches traced: 54 us -> 49.3 us
  Pallas kernels: 28.8 us -> 26.1 us
  starting transfers between devices: 18.4 us -> 16.1 us
  waiting for transfers between devices: 5.6 us -> 6.75 us
  local copies, waits for them, and re-layouts: 0.73 us -> 0.02 us
    pallas_call x4, Pallas kernels: 12.6 us -> 9.98 us  [fine(): call(functools.partial(fine_kernel, (half, group)), [VMEM] * 5 + [HBM] +...]
    ppermute x1, starting transfers between devices: 1.99 us -> 0.09 us  [body(): lax.ppermute(to_right, axes, [(i, (i + 1) % count) for i in range(count)])]
    ppermute x8, waiting for transfers between devices: 5.09 us -> 6.75 us  [swap(): lax.ppermute(x, axis, [(i, i ^ mask) for i in range(lax.axis_size(axis))])]
    ppermute x8, starting transfers between devices: 13.5 us -> 12 us  [swap(): lax.ppermute(x, axis, [(i, i ^ mask) for i in range(lax.axis_size(axis))])]
    ppermute x1, starting transfers between devices: 2.9 us -> 3.98 us  [body(): lax.ppermute(to_left, axes, [(i, (i - 1) % count) for i in range(count)])]
    unnamed x13 -> x9, local copies, waits for them, and re-layouts: 0.73 us -> 0.02 us
  transfers between devices with their start and end apart: 10 -> 10, of which waited for: 5 -> 5; matrix products, arithmetic and copies ran while one was open for 0% -> 0% of each run, Pallas kernels for 35% -> 33%
where the time goes in v5:
time: 50.3 us; the launch traced here: 49.3 us
  Pallas kernels  26.1 us (52%)
  starting transfers between devices  16.1 us (32%)
  waiting for transfers between devices  6.75 us (13%)
    ppermute x8, starting transfers between devices, swap(): lax.ppermute(x, axis, [(i, i ^ mask) for i in range(lax.axis_size(axis))])  12 us
    pallas_call x4, Pallas kernels, fine(): call(functools.partial(fine_kernel, (half, group)), [VMEM] * 5 + [HBM] +...  9.98 us
    ppermute x8, waiting for transfers between devices, swap(): lax.ppermute(x, axis, [(i, i ^ mask) for i in range(lax.axis_size(axis))])  6.75 us
    pallas_call x1, Pallas kernels, body(): call(down_kernel, [VMEM] * 3 + [HBM] * 2 + [VMEM] * 3 + [HBM], [shape((2,...  5.44 us
    pallas_call x2, Pallas kernels, small(): call(kernel, [VMEM] * 5 + [HBM], [shape(ride.shape, ride.dtype), shape((S...  4.65 us
    pallas_call x1, Pallas kernels, body(): call(up_kernel, [HBM, HBM, HBM], [shape((2 * SIZE, 384), BF16), shape((2...  4.33 us
    ppermute x1, starting transfers between devices, body(): lax.ppermute(to_left, axes, [(i, (i - 1) % count) for i in range(count)])  3.98 us
    pallas_call x1, Pallas kernels, load(): call(load_kernel, [VMEM, HBM], [shape(ride.shape, ride.dtype), on_chip((E...  1.71 us
  transfers between devices with their start and end apart: 10, of which 5 were waited for; matrix products, arithmetic and copies ran while one was open for 0% of the time, Pallas kernels for 33%

profile of v5, /device:TPU:2, one launch (start us, length us, event | category | flops | bytes accessed | tf_op | source)
XLA Modules:
  0.0 49.3 jit_solution(5174462846664048261)
XLA Ops:
  0.0 4.3 %shard_map.91 = (bf16[304,384]{1,0:T(8,128)(2,1)S(1)}, bf16[304,384]{1,0:T(8,128)(2,1)S(1)}, f32[1,512]{1,0:T(1,128)S(1)}) custom-call(bf16[2,152,512]{2,1,0:T(8,128)(2,1)} %check_hbm.1, bf16[2,152,152]{2,1,0:T(8,128)(2,1)} %equiv_hbm.1, bf16[4,8,2,152,152]{4,3,2,1,0:T(8,128)(2,1)} %ops_hbm.7), custom_call_target="tpu_custom_call" | custom-call | flops 4294967296 | bytes 8388608 | tf_op jit(solution)/shard_map/pallas_call | solution.py:351
  4.3 2.0 %collective-permute-start = (f32[1,512]{1,0:T(1,128)S(1)}, f32[1,512]{1,0:T(1,128)S(1)}, u32[]{:S(2)}, u32[]{:S(2)}) collective-permute-start(f32[1,512]{1,0:T(1,128)S(1)} %get-tuple-element.22), channel_id=1, source_target_pairs={{0,1},{1,0},{2,3},{3,2},{4,5},{5,4},{6,7},{7,6},{8,9},{9,8},{10,11... | collective-permute-start | bytes 6152 | tf_op jit(solution)/shard_map/ppermute | solution.py:402
  6.4 0.1 collective-permute-start.2
  6.5 4.0 %collective-permute-start.5 = (bf16[304,384]{1,0:T(8,128)(2,1)S(1)}, bf16[304,384]{1,0:T(8,128)(2,1)S(1)}, u32[]{:S(2)}, u32[]{:S(2)}) collective-permute-start(bf16[304,384]{1,0:T(8,128)(2,1)S(1)} %get-tuple-element.25.first.before.own), channel_id=1, source_target_pairs={{0,255},{1,0},{2,1},{3,2},{4,3},{5,4},{6,5},{7,6},{8,7},{9,8},{10,... | collective-permute-start | bytes 700424 | tf_op jit(solution)/shard_map/ppermute | solution.py:366
  10.4 0.0 collective-permute-done
  10.4 0.0 copy-start
  10.5 1.3 %collective-permute-start.1 = (f32[1,512]{1,0:T(1,128)S(1)}, f32[1,512]{1,0:T(1,128)S(1)}, u32[]{:S(2)}, u32[]{:S(2)}) collective-permute-start(f32[1,512]{1,0:T(1,128)S(1)} %add.9.ride), channel_id=1, source_target_pairs={{0,2},{1,3},{2,0},{3,1},{4,6},{5,7},{6,4},{7,5},{8,10},{9,11},{10,... | collective-permute-start | bytes 6152 | tf_op jit(solution)/shard_map/ppermute | solution.py:402
  11.8 1.7 %shard_map.92 = (f32[1,512]{1,0:T(1,128)S(1)}, bf16[16,2,152,152]{3,2,1,0:T(8,128)(2,1)S(1)}) custom-call(f32[1,512]{1,0:T(1,128)S(1)} %add.9.ride, bf16[4,16,2,152,152]{4,3,2,1,0:T(8,128)(2,1)} %ops_hbm.13), custom_call_target="tpu_custom_call" | custom-call | flops 8589934592 | bytes 8388608 | tf_op jit(solution)/shard_map/pallas_call | solution.py:369
  13.5 3.0 %collective-permute-done.1 = f32[1,512]{1,0:T(1,128)S(1)} collective-permute-done((f32[1,512]{1,0:T(1,128)S(1)}, f32[1,512]{1,0:T(1,128)S(1)}, u32[]{:S(2)}, u32[]{:S(2)}) %collective-permute-start.1) | collective-permute-done | bytes 2080 | tf_op jit(solution)/shard_map/ppermute | solution.py:402
  16.5 2.9 %collective-permute-start.3 = (f32[1,512]{1,0:T(1,128)S(1)}, f32[1,512]{1,0:T(1,128)S(1)}, u32[]{:S(2)}, u32[]{:S(2)}) collective-permute-start(f32[1,512]{1,0:T(1,128)S(1)} %add.10.ride), channel_id=1, source_target_pairs={{0,6},{1,7},{2,4},{3,5},{4,2},{5,3},{6,0},{7,1},{8,14},{9,15},{10,... | collective-permute-start | bytes 6152 | tf_op jit(solution)/shard_map/ppermute | solution.py:402
  19.4 0.0 collective-permute-done.2.before.from_left
  19.4 0.0 copy-done
  19.4 2.1 %shard_map.93 = (f32[1,512]{1,0:T(1,128)S(1)}, f32[2,152,256]{2,1,0:T(8,128)S(1)}) custom-call(f32[1,512]{1,0:T(1,128)S(1)} %add.10.ride, bf16[304,384]{1,0:T(8,128)(2,1)S(1)} %collective-permute-done.2.before.from_left, bf16[304,384]{1,0:T(8,128)(2,1)S(1)} %get-tuple-element.25.first.before.own, bf16[304,384]{1,0:T(8,128)(2,1)S(1)} %get-tuple-element.24.second.first, ...), custom_call_target="tpu_custom_call" | custom-call | flops 4294967296 | bytes 8388608 | tf_op jit(solution)/shard_map/pallas_call | solution.py:388
  21.5 0.7 %collective-permute-done.3 = f32[1,512]{1,0:T(1,128)S(1)} collective-permute-done((f32[1,512]{1,0:T(1,128)S(1)}, f32[1,512]{1,0:T(1,128)S(1)}, u32[]{:S(2)}, u32[]{:S(2)}) %collective-permute-start.3) | collective-permute-done | bytes 2080 | tf_op jit(solution)/shard_map/ppermute | solution.py:402
  22.2 0.0 collective-permute-start.4
  22.2 2.9 %shard_map.94 = (bf16[1,512]{1,0:T(2,128)(2,1)S(1)}, f32[2,152,256]{2,1,0:T(8,128)}) custom-call(bf16[1,512]{1,0:T(2,128)(2,1)S(1)} %add_convert_fusion.ride, bf16[304,384]{1,0:T(8,128)(2,1)S(1)} %collective-permute-done.2.before.from_left, bf16[304,384]{1,0:T(8,128)(2,1)S(1)} %get-tuple-element.25.first.before.own, ...), custom_call_target="tpu_custom_call" | custom-call | flops 4294967296 | bytes 8388608 | tf_op jit(solution)/shard_map/pallas_call | solution.py:388
  25.1 0.0 collective-permute-done.4
  25.1 3.8 %collective-permute-start.6 = (bf16[2,512]{1,0:T(2,128)(2,1)S(1)}, bf16[2,512]{1,0:T(2,128)(2,1)S(1)}, u32[]{:S(2)}, u32[]{:S(2)}) collective-permute-start(bf16[2,512]{1,0:T(2,128)(2,1)S(1)} %pad_maximum_fusion.2.ride), channel_id=1, source_target_pairs={{0,16},{8,24},{16,0},{24,8},{32,48},{40,56},{48,32},{56,40},{64,80... | collective-permute-start | bytes 6152 | tf_op jit(solution)/shard_map/ppermute | solution.py:402
  28.9 0.0 collective-permute-done.5.second.from_right
  28.9 2.1 %shard_map.95 = (bf16[2,512]{1,0:T(2,128)(2,1)S(1)}, f32[2,152,256]{2,1,0:T(8,128)S(1)}) custom-call(bf16[2,512]{1,0:T(2,128)(2,1)S(1)} %pad_maximum_fusion.2.ride, bf16[304,384]{1,0:T(8,128)(2,1)S(1)} %get-tuple-element.25.first.before.own, bf16[304,384]{1,0:T(8,128)(2,1)S(1)} %get-tuple-element.24.second.first, ...), custom_call_target="tpu_custom_call" | custom-call | flops 4294967296 | bytes 8388608 | tf_op jit(solution)/shard_map/pallas_call | solution.py:388
  31.1 0.0 collective-permute-done.6
  31.1 0.3 collective-permute-start.7
  31.4 0.0 copy-start.1
  31.4 2.9 %shard_map.96 = (bf16[4,512]{1,0:T(4,128)(2,1)S(1)}, f32[2,152,256]{2,1,0:T(8,128)}) custom-call(bf16[4,512]{1,0:T(4,128)(2,1)S(1)} %pad_maximum_fusion.1.ride, bf16[304,384]{1,0:T(8,128)(2,1)S(1)} %get-tuple-element.25.first.before.own, bf16[304,384]{1,0:T(8,128)(2,1)S(1)} %get-tuple-element.24.second.first, ...), custom_call_target="tpu_custom_call" | custom-call | flops 4294967296 | bytes 8388608 | tf_op jit(solution)/shard_map/pallas_call | solution.py:388
  34.3 0.7 %collective-permute-done.7 = bf16[4,512]{1,0:T(4,128)(2,1)S(1)} collective-permute-done((bf16[4,512]{1,0:T(4,128)(2,1)S(1)}, bf16[4,512]{1,0:T(4,128)(2,1)S(1)}, u32[]{:S(2)}, u32[]{:S(2)}) %collective-permute-start.7) | collective-permute-done | bytes 4128 | tf_op jit(solution)/shard_map/ppermute | solution.py:402
  35.0 0.2 collective-permute-start.8
  35.2 0.0 copy-done.1
  35.2 0.0 copy-start.3
  35.2 2.3 %shard_map.97 = (bf16[8,512]{1,0:T(8,128)(2,1)S(1)}, f32[152,128]{1,0:T(8,128)S(1)}) custom-call(bf16[8,512]{1,0:T(8,128)(2,1)S(1)} %pad_maximum_fusion.ride, bf16[304,384]{1,0:T(8,128)(2,1)S(1)} %collective-permute-done.2.before.from_left, bf16[304,384]{1,0:T(8,128)(2,1)S(1)} %collective-permute-done.5.second.from_right, ...), custom_call_target="tpu_custom_call" | custom-call | flops 3221225472 | bytes 8388608 | tf_op jit(solution)/shard_map/pallas_call | solution.py:378
  37.5 1.2 %collective-permute-done.8 = bf16[8,512]{1,0:T(8,128)(2,1)S(1)} collective-permute-done((bf16[8,512]{1,0:T(8,128)(2,1)S(1)}, bf16[8,512]{1,0:T(8,128)(2,1)S(1)}, u32[]{:S(2)}, u32[]{:S(2)}) %collective-permute-start.8) | collective-permute-done | bytes 8224 | tf_op jit(solution)/shard_map/ppermute | solution.py:402
  38.7 0.0 copy-start.2
  38.7 1.5 %collective-permute-start.9 = (bf16[16,512]{1,0:T(8,128)(2,1)S(1)}, bf16[16,512]{1,0:T(8,128)(2,1)S(1)}, u32[]{:S(2)}, u32[]{:S(2)}) collective-permute-start(bf16[16,512]{1,0:T(8,128)(2,1)S(1)} %constant_dynamic-update-slice_fusion.ride), channel_id=1, source_target_pairs={{0,192},{8,200},{16,208},{24,216},{32,224},{40,232},{48,240},{56,2... | collective-permute-start | bytes 49160 | tf_op jit(solution)/shard_map/ppermute | solution.py:402
  40.3 0.0 copy-done.3
  40.3 2.3 %shard_map.98 = (bf16[16,512]{1,0:T(8,128)(2,1)S(1)}, f32[152,128]{1,0:T(8,128)S(1)}) custom-call(bf16[16,512]{1,0:T(8,128)(2,1)S(1)} %constant_dynamic-update-slice_fusion.ride, bf16[304,384]{1,0:T(8,128)(2,1)S(1)} %collective-permute-done.2.before.from_left, bf16[304,384]{1,0:T(8,128)(2,1)S(1)} %collective-permute-done.5.second.from_right, ...), custom_call_target="tpu_custom_call" | custom-call | flops 3221225472 | bytes 8388608 | tf_op jit(solution)/shard_map/pallas_call | solution.py:378
  42.6 1.1 %collective-permute-done.9.others = bf16[16,512]{1,0:T(8,128)(2,1)S(1)} collective-permute-done((bf16[16,512]{1,0:T(8,128)(2,1)S(1)}, bf16[16,512]{1,0:T(8,128)(2,1)S(1)}, u32[]{:S(2)}, u32[]{:S(2)}) %collective-permute-start.9) | collective-permute-done | bytes 16416 | tf_op jit(solution)/shard_map/ppermute | solution.py:402
  43.7 0.0 copy-done.2
  43.7 5.4 %shard_map.99 = f32[2,152,512]{2,1,0:T(8,128)} custom-call(bf16[16,512]{1,0:T(8,128)(2,1)S(1)} %get-tuple-element.33.tops, bf16[16,512]{1,0:T(8,128)(2,1)S(1)} %collective-permute-done.9.others, s32[16,32]{1,0:T(8,128)S(1)} %bitcast.8, f32[2,152,256]{2,1,0:T(8,128)} %get-tuple-element.34.fine_a_hbm, f32[2,152,256]{2,1,0:T(8,128)} %get-tuple-element.35.fine_b_hbm, ...), custom_call_target="tpu_custom_call" | custom-call | flops 8589934592 | bytes 8388608 | tf_op jit(solution)/shard_map/pallas_call | solution.py:427
  (8 shorter events, 0.0 us)
Async XLA Ops:
  4.3 6.1 %collective-permute-start = (f32[1,512]{1,0:T(1,128)S(1)}, f32[1,512]{1,0:T(1,128)S(1)}, u32[]{:S(2)}, u32[]{:S(2)}) collective-permute-start(f32[1,512]{1,0:T(1,128)S(1)} %get-tuple-element.22), channel_id=1, source_target_pairs={{0,1},{1,0},{2,3},{3,2},{4,5},{5,4},{6,7},{7,6},{8,9},{9,8},{10,11... | collective-permute-start | bytes 6152 | tf_op jit(solution)/shard_map/ppermute | solution.py:402
  6.4 13.1 %collective-permute-start.2 = (bf16[304,384]{1,0:T(8,128)(2,1)S(1)}, bf16[304,384]{1,0:T(8,128)(2,1)S(1)}, u32[]{:S(2)}, u32[]{:S(2)}) collective-permute-start(bf16[304,384]{1,0:T(8,128)(2,1)S(1)} %get-tuple-element.24.second.first), channel_id=1, source_target_pairs={{0,1},{1,2},{2,3},{3,4},{4,5},{5,6},{6,7},{7,8},{8,9},{9,10},{10,1... | collective-permute-start | bytes 700424 | tf_op jit(solution)/shard_map/ppermute | solution.py:365
  6.5 22.5 %collective-permute-start.5 = (bf16[304,384]{1,0:T(8,128)(2,1)S(1)}, bf16[304,384]{1,0:T(8,128)(2,1)S(1)}, u32[]{:S(2)}, u32[]{:S(2)}) collective-permute-start(bf16[304,384]{1,0:T(8,128)(2,1)S(1)} %get-tuple-element.25.first.before.own), channel_id=1, source_target_pairs={{0,255},{1,0},{2,1},{3,2},{4,3},{5,4},{6,5},{7,6},{8,7},{9,8},{10,... | collective-permute-start | bytes 700424 | tf_op jit(solution)/shard_map/ppermute | solution.py:366
  10.4 9.0 %copy-start = (s32[512,16]{0,1:T(8,128)S(1)}, s32[512,16]{0,1:T(8,128)}, u32[]{:S(2)}) copy-start(s32[512,16]{0,1:T(8,128)} %param.14) | copy-start | bytes 98308
  10.5 6.1 %collective-permute-start.1 = (f32[1,512]{1,0:T(1,128)S(1)}, f32[1,512]{1,0:T(1,128)S(1)}, u32[]{:S(2)}, u32[]{:S(2)}) collective-permute-start(f32[1,512]{1,0:T(1,128)S(1)} %add.9.ride), channel_id=1, source_target_pairs={{0,2},{1,3},{2,0},{3,1},{4,6},{5,7},{6,4},{7,5},{8,10},{9,11},{10,... | collective-permute-start | bytes 6152 | tf_op jit(solution)/shard_map/ppermute | solution.py:402
  16.5 5.7 %collective-permute-start.3 = (f32[1,512]{1,0:T(1,128)S(1)}, f32[1,512]{1,0:T(1,128)S(1)}, u32[]{:S(2)}, u32[]{:S(2)}) collective-permute-start(f32[1,512]{1,0:T(1,128)S(1)} %add.10.ride), channel_id=1, source_target_pairs={{0,6},{1,7},{2,4},{3,5},{4,2},{5,3},{6,0},{7,1},{8,14},{9,15},{10,... | collective-permute-start | bytes 6152 | tf_op jit(solution)/shard_map/ppermute | solution.py:402
  22.2 2.9 %collective-permute-start.4 = (bf16[1,512]{1,0:T(2,128)(2,1)S(1)}, bf16[1,512]{1,0:T(2,128)(2,1)S(1)}, u32[]{:S(2)}, u32[]{:S(2)}) collective-permute-start(bf16[1,512]{1,0:T(2,128)(2,1)S(1)} %add_convert_fusion.ride), channel_id=1, source_target_pairs={{0,8},{8,0},{16,24},{24,16},{32,40},{40,32},{48,56},{56,48},{64,72... | collective-permute-start | bytes 3080 | tf_op jit(solution)/shard_map/ppermute | solution.py:402
  25.1 5.9 %collective-permute-start.6 = (bf16[2,512]{1,0:T(2,128)(2,1)S(1)}, bf16[2,512]{1,0:T(2,128)(2,1)S(1)}, u32[]{:S(2)}, u32[]{:S(2)}) collective-permute-start(bf16[2,512]{1,0:T(2,128)(2,1)S(1)} %pad_maximum_fusion.2.ride), channel_id=1, source_target_pairs={{0,16},{8,24},{16,0},{24,8},{32,48},{40,56},{48,32},{56,40},{64,80... | collective-permute-start | bytes 6152 | tf_op jit(solution)/shard_map/ppermute | solution.py:402
  31.1 3.9 %collective-permute-start.7 = (bf16[4,512]{1,0:T(4,128)(2,1)S(1)}, bf16[4,512]{1,0:T(4,128)(2,1)S(1)}, u32[]{:S(2)}, u32[]{:S(2)}) collective-permute-start(bf16[4,512]{1,0:T(4,128)(2,1)S(1)} %pad_maximum_fusion.1.ride), channel_id=1, source_target_pairs={{0,48},{8,56},{16,32},{24,40},{32,16},{40,24},{48,0},{56,8},{64,11... | collective-permute-start | bytes 12296 | tf_op jit(solution)/shard_map/ppermute | solution.py:402
  31.4 3.8 %copy-start.1 = (s32[64,16]{0,1:T(8,128)S(1)}, s32[64,16]{0,1:T(8,128)}, u32[]{:S(2)}) copy-start(s32[64,16]{0,1:T(8,128)} %param.15) | copy-start | bytes 12292
  35.0 3.7 %collective-permute-start.8 = (bf16[8,512]{1,0:T(8,128)(2,1)S(1)}, bf16[8,512]{1,0:T(8,128)(2,1)S(1)}, u32[]{:S(2)}, u32[]{:S(2)}) collective-permute-start(bf16[8,512]{1,0:T(8,128)(2,1)S(1)} %pad_maximum_fusion.ride), channel_id=1, source_target_pairs={{0,64},{8,72},{16,80},{24,88},{32,96},{40,104},{48,112},{56,120},{... | collective-permute-start | bytes 24584 | tf_op jit(solution)/shard_map/ppermute | solution.py:402
  35.2 5.1 %copy-start.3 = (s32[8,16]{1,0:T(8,128)S(1)}, s32[8,16]{1,0:T(8,128)}, u32[]{:S(2)}) copy-start(s32[8,16]{1,0:T(8,128)} %low_list.1) | copy-start | bytes 1540
  38.7 5.0 %copy-start.2 = (s32[32,16]{0,1:T(8,128)S(1)}, s32[32,16]{0,1:T(8,128)}, u32[]{:S(2)}) copy-start(s32[32,16]{0,1:T(8,128)} %param.17) | copy-start | bytes 6148
  38.7 4.9 %collective-permute-start.9 = (bf16[16,512]{1,0:T(8,128)(2,1)S(1)}, bf16[16,512]{1,0:T(8,128)(2,1)S(1)}, u32[]{:S(2)}, u32[]{:S(2)}) collective-permute-start(bf16[16,512]{1,0:T(8,128)(2,1)S(1)} %constant_dynamic-update-slice_fusion.ride), channel_id=1, source_target_pairs={{0,192},{8,200},{16,208},{24,216},{32,224},{40,232},{48,240},{56,2... | collective-permute-start | bytes 49160 | tf_op jit(solution)/shard_map/ppermute | solution.py:402

commit v6 on v5

--- a/solution.py
+++ b/solution.py
@@ -31,22 +31,8 @@
     return by_real + jnp.where(iota(turned.shape, 1) < HALF, -turned, turned)
 
 
-def child_columns():
-    row = iota((128, 1024), 0)
-    col = iota((128, 1024), 1)
-    octant, lane = col >> 7, col & 127
-    box = (lane & 63) * 8 + octant
-    wanted = jnp.where(box < HALF, (lane & HALF) + box, -1)
-    return (row == wanted).astype(BF16)
-
-
-def parent_columns():
-    row = iota((128, 1024), 0)
-    col = iota((128, 1024), 1)
-    octant, lane = col >> 7, col & 127
-    box = lane & 63
-    wanted = jnp.where((box & 7) == octant, (lane & HALF) + (box >> 3), -1)
-    return (row == wanted).astype(BF16)
+def box_order(lane):
+    return (lane & 7) * 8 + ((lane & 63) >> 3)
 
 
 def regroup(first, second):
@@ -105,8 +91,7 @@
     copies.append(pltpu.make_async_copy(ops_hbm.at[3, lax.axis_index("col")], own_op, sems.at[3]))
     for copy in first + copies:
         copy.start()
-    fill_places(by_octant, lambda col: (col & 63) * 8 + (col >> 6))
-    pick = child_columns()
+    fill_places(by_octant, lambda col: box_order(col) * 8 + (col >> 6))
     for copy in first:
         copy.wait()
     field = jnp.concatenate([check[0], check[1]], axis=1)
@@ -122,13 +107,21 @@
     for pair in range(OCTANTS // 2):
         children += regroup(tile(ordered[:SIZE], pair), tile(ordered[SIZE:], pair))
     children = [child.astype(BF16) for child in children]
-    packed = []
-    for level in range(3):
+    copies[0].wait()
+    packed = [apply_each(ops.at[0], lambda c: children[c], OCTANTS).astype(BF16)]
+    lane = iota((SIZE, 128), 1) & 63
+    for level, octant, steps in ((1, lane >> 3, (32, 16, 8)), (2, lane, (4, 2, 1))):
         copies[level].wait()
-        packed.append(apply_each(ops.at[level], lambda c: children[c], OCTANTS).astype(BF16))
-        if level < 2:
-            spread = mm(packed[level], pick).astype(BF16)
-            children = [tile(spread, c) for c in range(OCTANTS)]
+        below = packed[level - 1]
+        by_real = mm(ops[level, 0, 0], below)
+        by_imag = mm(ops[level, 0, 1], below)
+        for c in range(1, OCTANTS):
+            by_real = jnp.where(octant == c, mm(ops[level, c, 0], below), by_real)
+            by_imag = jnp.where(octant == c, mm(ops[level, c, 1], below), by_imag)
+        dense = combine(by_real, by_imag)
+        for step in steps:
+            dense = dense + pltpu.roll(dense, 128 - step, 1)
+        packed.append(jnp.where(lane < steps[-1], dense, 0.0).astype(BF16))
     both = jnp.concatenate([packed[0].astype(F32), packed[1].astype(F32)], axis=0).astype(BF16)
     to_left[:, REACH:] = both
     to_right[:, REACH:] = both
@@ -185,8 +178,10 @@
     codes = jnp.where(lane < 24, (row >> 6) * 1024 + place, -(1 << 20)).astype(F32)
     index = (low_list[...] - device_position() * 8).astype(F32)
     listed = jnp.transpose(jnp.concatenate([index, jnp.zeros((8, 112), F32)], axis=1))[:ENTRIES]
-    pad = jnp.full((ENTRIES, HALF - 8), -(1 << 19), F32)
-    targets = jnp.concatenate([listed, pad, listed + 1024, pad], axis=1)
+    listed = jnp.concatenate([listed, jnp.zeros((ENTRIES, 120), F32)], axis=1).astype(BF16)
+    lane = iota((128, 128), 1)
+    targets = mm(listed, (iota((128, 128), 0) == (lane & 63) >> 3).astype(BF16))
+    targets = targets + jnp.where(iota(targets.shape, 1) < HALF, 0.0, 1024.0)
     out[...] = translate_packed(around, codes, targets, ops, copies)
 
 
@@ -196,7 +191,7 @@
     mids = [ref[:, REACH:].astype(F32)[:SIZE] for ref in (from_left, own, from_right)]
     around = jnp.concatenate(mids, axis=1).astype(BF16)
     row = iota((384, 128), 0)
-    codes = ((row >> 6) & 1) * 1024 + (row & 63) + ((row >> 7) - 1) * HALF
+    codes = ((row >> 6) & 1) * 1024 + box_order(row) + ((row >> 7) - 1) * HALF
     index = mid_t[...] - device_position() * HALF
     targets = jnp.concatenate([index, index + 1024], axis=1)
     out[...] = translate_packed(around, codes, targets, ops, copies)
@@ -260,23 +255,21 @@
     place = place ^ ((place >> 1) & 0b01010)
     mine = iota(place.shape, 1) == own_row
     listed = jnp.sum(jnp.where(mine, place.astype(F32), 0.0), axis=1, keepdims=True)
-    pad = jnp.full((HALF - ENTRIES, 1), -1.0, F32)
-    wanted = jnp.concatenate([listed, pad, listed + HALF, pad], axis=0)
-    select = (iota((128, 128), 1).astype(F32) == wanted).astype(BF16)
-    picked = lax.dot_general(dense, select, (((1,), (1,)), ((), ())), preferred_element_type=F32)
-    entry = iota((SIZE, 128), 1) & 63
-    local = apply_each(transfer, lambda k: jnp.where(entry == k, picked, 0.0).astype(BF16), ENTRIES)
-    for shift in (8, 4, 2, 1):
-        local = local + pltpu.roll(local, 128 - shift, 1)
-    local = jnp.where(entry == 0, local, 0.0).astype(BF16)
+    codes = (iota((128, 128), 0) - (iota((128, 128), 1) & HALF)).astype(F32)
+    select = jnp.concatenate([(codes == listed[k : k + 1, :]).astype(BF16) for k in range(ENTRIES)], axis=1)
+    picked = mm(dense, select).astype(BF16)
+    local = apply_each(transfer, lambda k: tile(picked, k), ENTRIES).astype(BF16)
     copies[3].wait()
     local = combine(mm(own_op[0], local), mm(own_op[1], local)).astype(BF16)
-    place = parent_columns()
-    for level, at_level in ((2, low_near), (1, mid_near)):
-        parents = mm(local, place).astype(BF16)
+    lane = iota((SIZE, 128), 1) & 63
+    for level, at_level, octant in ((2, low_near, lane >> 3), (1, mid_near, lane & 7)):
         copies[level].wait()
-        local = apply_each(down.at[level], lambda c: tile(parents, c), OCTANTS) + at_level[...]
-        local = local.astype(BF16)
+        by_real = mm(down[level, 0, 0], local)
+        by_imag = mm(down[level, 0, 1], local)
+        for c in range(1, OCTANTS):
+            by_real = jnp.where(octant == c, mm(down[level, c, 0], local), by_real)
+            by_imag = jnp.where(octant == c, mm(down[level, c, 1], local), by_imag)
+        local = (combine(by_real, by_imag) + at_level[...]).astype(BF16)
     copies[0].wait()
     real, imag = [], []
     for pair in range(OCTANTS // 2):
@@ -294,11 +287,15 @@
         term = jnp.concatenate(terms, axis=1)
         high = term.astype(BF16)
         low = (term - high.astype(F32)).astype(BF16)
-        far = mm(high, places[...]) + mm(low, places[...])
-        out[part, :, :REACH] = near[0, part] + far[:, :REACH]
-        out[part, :, REACH:] = near[1, part] + far[:, REACH:]
-        out_copies.append(pltpu.make_async_copy(out.at[part], out_hbm.at[part], sems.at[6 + part]))
-        out_copies[part].start()
+        for half in range(2):
+            columns = pl.ds(half * REACH, REACH)
+            place = places[:, columns]
+            out[part, :, columns] = near[half, part] + mm(high, place) + mm(low, place)
+            copy = pltpu.make_async_copy(
+                out.at[part, :, columns], out_hbm.at[part, :, columns], sems.at[6 + 2 * part + half]
+            )
+            copy.start()
+            out_copies.append(copy)
     for copy in out_copies:
         copy.wait()
 
@@ -402,21 +399,20 @@
         return lax.ppermute(x, axis, [(i, i ^ mask) for i in range(lax.axis_size(axis))])
 
     work = {
-        1: load,
-        2: lambda ride: fine(0, 0, [], ride),
-        3: lambda ride: fine(0, 1, done[2], ride),
-        4: lambda ride: fine(1, 0, [], ride),
-        5: lambda ride: fine(1, 1, done[4], ride),
-        6: functools.partial(small, mid_kernel, list_mid.T),
-        7: functools.partial(small, low_kernel, list_low),
+        1: {"top": load, "a": lambda ride: fine(0, 0, [], ride)},
+        2: {"a": lambda ride: fine(0, 1, done["a"], ride)},
+        4: {"b": lambda ride: fine(1, 0, [], ride)},
+        5: {"b": lambda ride: fine(1, 1, done["b"], ride)},
+        6: {"mid": functools.partial(small, mid_kernel, list_mid.T)},
+        7: {"low": functools.partial(small, low_kernel, list_low)},
     }
     done = {}
     total = top
     for step, mask in enumerate((1, 2, 6, 1, 2, 6, 8, 24)):
         axis = "col" if step < 3 else "row"
         other = swap(total, axis, mask) if axis == "col" or mask < rows else None
-        if step in work:
-            total, *done[step] = work[step](total)
+        for name, kernel in work.get(step, {}).items():
+            total, *done[name] = kernel(total)
         if axis == "col":
             total = total + other
         elif step < 7:
@@ -434,12 +430,13 @@
             pltpu.VMEM((3, OCTANTS) + octant_ops, BF16),
             pltpu.VMEM(octant_ops, BF16),
             pltpu.VMEM((FINE, FINE), BF16),
-            pltpu.SemaphoreType.DMA((8,)),
+            pltpu.SemaphoreType.DMA((10,)),
         ],
         8 << 30,
         place=HBM,
     )(
-        total, other, list_top.T, in_hbm(done[3][0]), in_hbm(done[5][0]), *done[6], *done[7], *done[1],
+        total, other, list_top.T, in_hbm(done["a"][0]), in_hbm(done["b"][0]), *done["mid"], *done["low"],
+        *done["top"],
         downward_ops,
     )
     return far

time: 50.3 us -> 50.4 us (level)
  Pallas kernels: 26.1 us -> 25.3 us
  starting transfers between devices: 16.1 us -> 16.7 us
    ppermute x1, waiting for transfers between devices: 0.01 us -> 2.04 us  [body(): lax.ppermute(to_right, axes, [(i, (i + 1) % count) for i in range(count)])]
    ppermute x8, waiting for transfers between devices: 6.75 us -> 4.96 us  [swap(): lax.ppermute(x, axis, [(i, i ^ mask) for i in range(lax.axis_size(axis))])]
    pallas_call x1, Pallas kernels: 5.44 us -> 4.64 us  [body(): call(down_kernel, [VMEM] * 3 + [HBM] * 2 + [VMEM] * 3 + [HBM], [shape((2,...]
    ppermute x8, starting transfers between devices: 12 us -> 12.7 us  [swap(): lax.ppermute(x, axis, [(i, i ^ mask) for i in range(lax.axis_size(axis))])]
where the time goes in v6:
time: 50.4 us; the launch traced here: 49.4 us
  Pallas kernels  25.3 us (50%)
  starting transfers between devices  16.7 us (33%)
  waiting for transfers between devices  7 us (14%)
    ppermute x8, starting transfers between devices, swap(): lax.ppermute(x, axis, [(i, i ^ mask) for i in range(lax.axis_size(axis))])  12.7 us
    pallas_call x4, Pallas kernels, fine(): call(functools.partial(fine_kernel, (half, group)), [VMEM] * 5 + [HBM] +...  9.98 us
    ppermute x8, waiting for transfers between devices, swap(): lax.ppermute(x, axis, [(i, i ^ mask) for i in range(lax.axis_size(axis))])  4.96 us
    pallas_call x2, Pallas kernels, small(): call(kernel, [VMEM] * 5 + [HBM], [shape(ride.shape, ride.dtype), shape((S...  4.7 us
    pallas_call x1, Pallas kernels, body(): call(down_kernel, [VMEM] * 3 + [HBM] * 2 + [VMEM] * 3 + [HBM], [shape((2,...  4.64 us
    pallas_call x1, Pallas kernels, body(): call(up_kernel, [HBM, HBM, HBM], [shape((2 * SIZE, 384), BF16), shape((2...  4.27 us
    ppermute x1, starting transfers between devices, body(): lax.ppermute(to_left, axes, [(i, (i - 1) % count) for i in range(count)])  3.97 us
    ppermute x1, waiting for transfers between devices, body(): lax.ppermute(to_right, axes, [(i, (i + 1) % count) for i in range(count)])  2.04 us
  transfers between devices with their start and end apart: 10, of which 5 were waited for; matrix products, arithmetic and copies ran while one was open for 0% of the time, Pallas kernels for 33%

profile of v6, /device:TPU:2, one launch (start us, length us, event | category | flops | bytes accessed | tf_op | source)
XLA Modules:
  0.0 49.4 jit_solution(476794301368410005)
XLA Ops:
  0.0 4.3 %shard_map.91 = (bf16[304,384]{1,0:T(8,128)(2,1)S(1)}, bf16[304,384]{1,0:T(8,128)(2,1)S(1)}, f32[1,512]{1,0:T(1,128)S(1)}) custom-call(bf16[2,152,512]{2,1,0:T(8,128)(2,1)} %check_hbm.1, bf16[2,152,152]{2,1,0:T(8,128)(2,1)} %equiv_hbm.1, bf16[4,8,2,152,152]{4,3,2,1,0:T(8,128)(2,1)} %ops_hbm.7), custom_call_target="tpu_custom_call" | custom-call | flops 4294967296 | bytes 8388608 | tf_op jit(solution)/shard_map/pallas_call | solution.py:348
  4.3 2.0 %collective-permute-start = (f32[1,512]{1,0:T(1,128)S(1)}, f32[1,512]{1,0:T(1,128)S(1)}, u32[]{:S(2)}, u32[]{:S(2)}) collective-permute-start(f32[1,512]{1,0:T(1,128)S(1)} %get-tuple-element.22), channel_id=1, source_target_pairs={{0,1},{1,0},{2,3},{3,2},{4,5},{5,4},{6,7},{7,6},{8,9},{9,8},{10,11... | collective-permute-start | bytes 6152 | tf_op jit(solution)/shard_map/ppermute | solution.py:399
  6.3 0.1 collective-permute-start.1
  6.4 4.0 %collective-permute-start.5 = (bf16[304,384]{1,0:T(8,128)(2,1)S(1)}, bf16[304,384]{1,0:T(8,128)(2,1)S(1)}, u32[]{:S(2)}, u32[]{:S(2)}) collective-permute-start(bf16[304,384]{1,0:T(8,128)(2,1)S(1)} %get-tuple-element.25.first.before.own), channel_id=1, source_target_pairs={{0,255},{1,0},{2,1},{3,2},{4,3},{5,4},{6,5},{7,6},{8,7},{9,8},{10,... | collective-permute-start | bytes 700424 | tf_op jit(solution)/shard_map/ppermute | solution.py:363
  10.4 0.0 collective-permute-done
  10.4 0.0 copy-start
  10.4 1.3 %collective-permute-start.2 = (f32[1,512]{1,0:T(1,128)S(1)}, f32[1,512]{1,0:T(1,128)S(1)}, u32[]{:S(2)}, u32[]{:S(2)}) collective-permute-start(f32[1,512]{1,0:T(1,128)S(1)} %add.9.ride), channel_id=1, source_target_pairs={{0,2},{1,3},{2,0},{3,1},{4,6},{5,7},{6,4},{7,5},{8,10},{9,11},{10,... | collective-permute-start | bytes 6152 | tf_op jit(solution)/shard_map/ppermute | solution.py:399
  11.7 1.7 %shard_map.92 = (f32[1,512]{1,0:T(1,128)S(1)}, bf16[16,2,152,152]{3,2,1,0:T(8,128)(2,1)S(1)}) custom-call(f32[1,512]{1,0:T(1,128)S(1)} %add.9.ride, bf16[4,16,2,152,152]{4,3,2,1,0:T(8,128)(2,1)} %ops_hbm.13), custom_call_target="tpu_custom_call" | custom-call | flops 8589934592 | bytes 8388608 | tf_op jit(solution)/shard_map/pallas_call | solution.py:366
  13.4 2.0 %collective-permute-done.1.before.from_left = bf16[304,384]{1,0:T(8,128)(2,1)S(1)} collective-permute-done((bf16[304,384]{1,0:T(8,128)(2,1)S(1)}, bf16[304,384]{1,0:T(8,128)(2,1)S(1)}, u32[]{:S(2)}, u32[]{:S(2)}) %collective-permute-start.1) | collective-permute-done | bytes 233504 | tf_op jit(solution)/shard_map/ppermute | solution.py:362
  15.4 0.0 copy-done
  15.4 2.1 %shard_map.93 = (f32[1,512]{1,0:T(1,128)S(1)}, f32[2,152,256]{2,1,0:T(8,128)S(1)}) custom-call(f32[1,512]{1,0:T(1,128)S(1)} %get-tuple-element.23.ride, bf16[304,384]{1,0:T(8,128)(2,1)S(1)} %collective-permute-done.1.before.from_left, bf16[304,384]{1,0:T(8,128)(2,1)S(1)} %get-tuple-element.25.first.before.own, ...), custom_call_target="tpu_custom_call" | custom-call | flops 4294967296 | bytes 8388608 | tf_op jit(solution)/shard_map/pallas_call | solution.py:385
  17.6 0.0 collective-permute-done.2
  17.6 3.5 %collective-permute-start.3 = (f32[1,512]{1,0:T(1,128)S(1)}, f32[1,512]{1,0:T(1,128)S(1)}, u32[]{:S(2)}, u32[]{:S(2)}) collective-permute-start(f32[1,512]{1,0:T(1,128)S(1)} %add.10.ride), channel_id=1, source_target_pairs={{0,6},{1,7},{2,4},{3,5},{4,2},{5,3},{6,0},{7,1},{8,14},{9,15},{10,... | collective-permute-start | bytes 6152 | tf_op jit(solution)/shard_map/ppermute | solution.py:399
  21.1 2.9 %shard_map.94 = (f32[1,512]{1,0:T(1,128)S(1)}, f32[2,152,256]{2,1,0:T(8,128)}) custom-call(f32[1,512]{1,0:T(1,128)S(1)} %add.10.ride, bf16[304,384]{1,0:T(8,128)(2,1)S(1)} %collective-permute-done.1.before.from_left, bf16[304,384]{1,0:T(8,128)(2,1)S(1)} %get-tuple-element.25.first.before.own, bf16[304,384]{1,0:T(8,128)(2,1)S(1)} %get-tuple-element.24.second.first, ...), custom_call_target="tpu_custom_call" | custom-call | flops 4294967296 | bytes 8388608 | tf_op jit(solution)/shard_map/pallas_call | solution.py:385
  24.0 0.0 collective-permute-done.3
  24.0 0.1 collective-permute-start.4
  24.1 1.1 %collective-permute-done.4 = bf16[1,512]{1,0:T(2,128)(2,1)S(1)} collective-permute-done((bf16[1,512]{1,0:T(2,128)(2,1)S(1)}, bf16[1,512]{1,0:T(2,128)(2,1)S(1)}, u32[]{:S(2)}, u32[]{:S(2)}) %collective-permute-start.4) | collective-permute-done | bytes 1056 | tf_op jit(solution)/shard_map/ppermute | solution.py:399
  25.3 4.6 %collective-permute-start.6 = (bf16[2,512]{1,0:T(2,128)(2,1)S(1)}, bf16[2,512]{1,0:T(2,128)(2,1)S(1)}, u32[]{:S(2)}, u32[]{:S(2)}) collective-permute-start(bf16[2,512]{1,0:T(2,128)(2,1)S(1)} %pad_maximum_fusion.2.ride), channel_id=1, source_target_pairs={{0,16},{8,24},{16,0},{24,8},{32,48},{40,56},{48,32},{56,40},{64,80... | collective-permute-start | bytes 6152 | tf_op jit(solution)/shard_map/ppermute | solution.py:399
  29.9 0.0 collective-permute-done.5.second.from_right
  29.9 2.1 %shard_map.95 = (bf16[2,512]{1,0:T(2,128)(2,1)S(1)}, f32[2,152,256]{2,1,0:T(8,128)S(1)}) custom-call(bf16[2,512]{1,0:T(2,128)(2,1)S(1)} %pad_maximum_fusion.2.ride, bf16[304,384]{1,0:T(8,128)(2,1)S(1)} %get-tuple-element.25.first.before.own, bf16[304,384]{1,0:T(8,128)(2,1)S(1)} %get-tuple-element.24.second.first, ...), custom_call_target="tpu_custom_call" | custom-call | flops 4294967296 | bytes 8388608 | tf_op jit(solution)/shard_map/pallas_call | solution.py:385
  32.0 0.0 collective-permute-done.6
  32.1 0.3 collective-permute-start.7
  32.3 0.0 copy-start.1
  32.3 2.9 %shard_map.96 = (bf16[4,512]{1,0:T(4,128)(2,1)S(1)}, f32[2,152,256]{2,1,0:T(8,128)}) custom-call(bf16[4,512]{1,0:T(4,128)(2,1)S(1)} %pad_maximum_fusion.1.ride, bf16[304,384]{1,0:T(8,128)(2,1)S(1)} %get-tuple-element.25.first.before.own, bf16[304,384]{1,0:T(8,128)(2,1)S(1)} %get-tuple-element.24.second.first, ...), custom_call_target="tpu_custom_call" | custom-call | flops 4294967296 | bytes 8388608 | tf_op jit(solution)/shard_map/pallas_call | solution.py:385
  35.2 0.7 %collective-permute-done.7 = bf16[4,512]{1,0:T(4,128)(2,1)S(1)} collective-permute-done((bf16[4,512]{1,0:T(4,128)(2,1)S(1)}, bf16[4,512]{1,0:T(4,128)(2,1)S(1)}, u32[]{:S(2)}, u32[]{:S(2)}) %collective-permute-start.7) | collective-permute-done | bytes 4128 | tf_op jit(solution)/shard_map/ppermute | solution.py:399
  35.9 0.1 collective-permute-start.8
  36.0 0.0 copy-done.1
  36.0 0.0 copy-start.3
  36.1 2.3 %shard_map.97 = (bf16[8,512]{1,0:T(8,128)(2,1)S(1)}, f32[152,128]{1,0:T(8,128)S(1)}) custom-call(bf16[8,512]{1,0:T(8,128)(2,1)S(1)} %pad_maximum_fusion.ride, bf16[304,384]{1,0:T(8,128)(2,1)S(1)} %collective-permute-done.1.before.from_left, bf16[304,384]{1,0:T(8,128)(2,1)S(1)} %collective-permute-done.5.second.from_right, ...), custom_call_target="tpu_custom_call" | custom-call | flops 3221225472 | bytes 8388608 | tf_op jit(solution)/shard_map/pallas_call | solution.py:375
  38.4 1.3 %collective-permute-done.8 = bf16[8,512]{1,0:T(8,128)(2,1)S(1)} collective-permute-done((bf16[8,512]{1,0:T(8,128)(2,1)S(1)}, bf16[8,512]{1,0:T(8,128)(2,1)S(1)}, u32[]{:S(2)}, u32[]{:S(2)}) %collective-permute-start.8) | collective-permute-done | bytes 8224 | tf_op jit(solution)/shard_map/ppermute | solution.py:399
  39.7 0.0 copy-start.2
  39.7 0.7 %collective-permute-start.9 = (bf16[16,512]{1,0:T(8,128)(2,1)S(1)}, bf16[16,512]{1,0:T(8,128)(2,1)S(1)}, u32[]{:S(2)}, u32[]{:S(2)}) collective-permute-start(bf16[16,512]{1,0:T(8,128)(2,1)S(1)} %constant_dynamic-update-slice_fusion.ride), channel_id=1, source_target_pairs={{0,192},{8,200},{16,208},{24,216},{32,224},{40,232},{48,240},{56,2... | collective-permute-start | bytes 49160 | tf_op jit(solution)/shard_map/ppermute | solution.py:399
  40.4 0.0 copy-done.3
  40.4 2.4 %shard_map.98 = (bf16[16,512]{1,0:T(8,128)(2,1)S(1)}, f32[152,128]{1,0:T(8,128)S(1)}) custom-call(bf16[16,512]{1,0:T(8,128)(2,1)S(1)} %constant_dynamic-update-slice_fusion.ride, bf16[304,384]{1,0:T(8,128)(2,1)S(1)} %collective-permute-done.1.before.from_left, bf16[304,384]{1,0:T(8,128)(2,1)S(1)} %collective-permute-done.5.second.from_right, ...), custom_call_target="tpu_custom_call" | custom-call | flops 3221225472 | bytes 8388608 | tf_op jit(solution)/shard_map/pallas_call | solution.py:375
  42.8 1.8 %collective-permute-done.9.others = bf16[16,512]{1,0:T(8,128)(2,1)S(1)} collective-permute-done((bf16[16,512]{1,0:T(8,128)(2,1)S(1)}, bf16[16,512]{1,0:T(8,128)(2,1)S(1)}, u32[]{:S(2)}, u32[]{:S(2)}) %collective-permute-start.9) | collective-permute-done | bytes 16416 | tf_op jit(solution)/shard_map/ppermute | solution.py:399
  44.6 0.0 copy-done.2
  44.6 4.6 %shard_map.99 = f32[2,152,512]{2,1,0:T(8,128)} custom-call(bf16[16,512]{1,0:T(8,128)(2,1)S(1)} %get-tuple-element.33.tops, bf16[16,512]{1,0:T(8,128)(2,1)S(1)} %collective-permute-done.9.others, s32[16,32]{1,0:T(8,128)S(1)} %bitcast.8, f32[2,152,256]{2,1,0:T(8,128)} %get-tuple-element.34.fine_a_hbm, f32[2,152,256]{2,1,0:T(8,128)} %get-tuple-element.35.fine_b_hbm, ...), custom_call_target="tpu_custom_call" | custom-call | flops 8589934592 | bytes 8388608 | tf_op jit(solution)/shard_map/pallas_call | solution.py:423
  (8 shorter events, 0.1 us)
Async XLA Ops:
  4.3 6.1 %collective-permute-start = (f32[1,512]{1,0:T(1,128)S(1)}, f32[1,512]{1,0:T(1,128)S(1)}, u32[]{:S(2)}, u32[]{:S(2)}) collective-permute-start(f32[1,512]{1,0:T(1,128)S(1)} %get-tuple-element.22), channel_id=1, source_target_pairs={{0,1},{1,0},{2,3},{3,2},{4,5},{5,4},{6,7},{7,6},{8,9},{9,8},{10,11... | collective-permute-start | bytes 6152 | tf_op jit(solution)/shard_map/ppermute | solution.py:399
  6.3 9.1 %collective-permute-start.1 = (bf16[304,384]{1,0:T(8,128)(2,1)S(1)}, bf16[304,384]{1,0:T(8,128)(2,1)S(1)}, u32[]{:S(2)}, u32[]{:S(2)}) collective-permute-start(bf16[304,384]{1,0:T(8,128)(2,1)S(1)} %get-tuple-element.24.second.first), channel_id=1, source_target_pairs={{0,1},{1,2},{2,3},{3,4},{4,5},{5,6},{6,7},{7,8},{8,9},{9,10},{10,1... | collective-permute-start | bytes 700424 | tf_op jit(solution)/shard_map/ppermute | solution.py:362
  6.4 23.5 %collective-permute-start.5 = (bf16[304,384]{1,0:T(8,128)(2,1)S(1)}, bf16[304,384]{1,0:T(8,128)(2,1)S(1)}, u32[]{:S(2)}, u32[]{:S(2)}) collective-permute-start(bf16[304,384]{1,0:T(8,128)(2,1)S(1)} %get-tuple-element.25.first.before.own), channel_id=1, source_target_pairs={{0,255},{1,0},{2,1},{3,2},{4,3},{5,4},{6,5},{7,6},{8,7},{9,8},{10,... | collective-permute-start | bytes 700424 | tf_op jit(solution)/shard_map/ppermute | solution.py:363
  10.4 5.1 %copy-start = (s32[512,16]{0,1:T(8,128)S(1)}, s32[512,16]{0,1:T(8,128)}, u32[]{:S(2)}) copy-start(s32[512,16]{0,1:T(8,128)} %param.14) | copy-start | bytes 98308
  10.4 7.2 %collective-permute-start.2 = (f32[1,512]{1,0:T(1,128)S(1)}, f32[1,512]{1,0:T(1,128)S(1)}, u32[]{:S(2)}, u32[]{:S(2)}) collective-permute-start(f32[1,512]{1,0:T(1,128)S(1)} %add.9.ride), channel_id=1, source_target_pairs={{0,2},{1,3},{2,0},{3,1},{4,6},{5,7},{6,4},{7,5},{8,10},{9,11},{10,... | collective-permute-start | bytes 6152 | tf_op jit(solution)/shard_map/ppermute | solution.py:399
  17.6 6.4 %collective-permute-start.3 = (f32[1,512]{1,0:T(1,128)S(1)}, f32[1,512]{1,0:T(1,128)S(1)}, u32[]{:S(2)}, u32[]{:S(2)}) collective-permute-start(f32[1,512]{1,0:T(1,128)S(1)} %add.10.ride), channel_id=1, source_target_pairs={{0,6},{1,7},{2,4},{3,5},{4,2},{5,3},{6,0},{7,1},{8,14},{9,15},{10,... | collective-permute-start | bytes 6152 | tf_op jit(solution)/shard_map/ppermute | solution.py:399
  24.0 1.2 %collective-permute-start.4 = (bf16[1,512]{1,0:T(2,128)(2,1)S(1)}, bf16[1,512]{1,0:T(2,128)(2,1)S(1)}, u32[]{:S(2)}, u32[]{:S(2)}) collective-permute-start(bf16[1,512]{1,0:T(2,128)(2,1)S(1)} %add_convert_fusion), channel_id=1, source_target_pairs={{0,8},{8,0},{16,24},{24,16},{32,40},{40,32},{48,56},{56,48},{64,72... | collective-permute-start | bytes 3080 | tf_op jit(solution)/shard_map/ppermute | solution.py:399
  25.3 6.7 %collective-permute-start.6 = (bf16[2,512]{1,0:T(2,128)(2,1)S(1)}, bf16[2,512]{1,0:T(2,128)(2,1)S(1)}, u32[]{:S(2)}, u32[]{:S(2)}) collective-permute-start(bf16[2,512]{1,0:T(2,128)(2,1)S(1)} %pad_maximum_fusion.2.ride), channel_id=1, source_target_pairs={{0,16},{8,24},{16,0},{24,8},{32,48},{40,56},{48,32},{56,40},{64,80... | collective-permute-start | bytes 6152 | tf_op jit(solution)/shard_map/ppermute | solution.py:399
  32.1 3.9 %collective-permute-start.7 = (bf16[4,512]{1,0:T(4,128)(2,1)S(1)}, bf16[4,512]{1,0:T(4,128)(2,1)S(1)}, u32[]{:S(2)}, u32[]{:S(2)}) collective-permute-start(bf16[4,512]{1,0:T(4,128)(2,1)S(1)} %pad_maximum_fusion.1.ride), channel_id=1, source_target_pairs={{0,48},{8,56},{16,32},{24,40},{32,16},{40,24},{48,0},{56,8},{64,11... | collective-permute-start | bytes 12296 | tf_op jit(solution)/shard_map/ppermute | solution.py:399
  32.3 3.7 %copy-start.1 = (s32[64,16]{0,1:T(8,128)S(1)}, s32[64,16]{0,1:T(8,128)}, u32[]{:S(2)}) copy-start(s32[64,16]{0,1:T(8,128)} %param.15) | copy-start | bytes 12292
  35.9 3.7 %collective-permute-start.8 = (bf16[8,512]{1,0:T(8,128)(2,1)S(1)}, bf16[8,512]{1,0:T(8,128)(2,1)S(1)}, u32[]{:S(2)}, u32[]{:S(2)}) collective-permute-start(bf16[8,512]{1,0:T(8,128)(2,1)S(1)} %pad_maximum_fusion.ride), channel_id=1, source_target_pairs={{0,64},{8,72},{16,80},{24,88},{32,96},{40,104},{48,112},{56,120},{... | collective-permute-start | bytes 24584 | tf_op jit(solution)/shard_map/ppermute | solution.py:399
  36.0 4.4 %copy-start.3 = (s32[8,16]{1,0:T(8,128)S(1)}, s32[8,16]{1,0:T(8,128)}, u32[]{:S(2)}) copy-start(s32[8,16]{1,0:T(8,128)} %low_list.1) | copy-start | bytes 1540
  39.7 5.0 %copy-start.2 = (s32[32,16]{0,1:T(8,128)S(1)}, s32[32,16]{0,1:T(8,128)}, u32[]{:S(2)}) copy-start(s32[32,16]{0,1:T(8,128)} %param.17) | copy-start | bytes 6148
  39.7 4.9 %collective-permute-start.9 = (bf16[16,512]{1,0:T(8,128)(2,1)S(1)}, bf16[16,512]{1,0:T(8,128)(2,1)S(1)}, u32[]{:S(2)}, u32[]{:S(2)}) collective-permute-start(bf16[16,512]{1,0:T(8,128)(2,1)S(1)} %constant_dynamic-update-slice_fusion.ride), channel_id=1, source_target_pairs={{0,192},{8,200},{16,208},{24,216},{32,224},{40,232},{48,240},{56,2... | collective-permute-start | bytes 49160 | tf_op jit(solution)/shard_map/ppermute | solution.py:399

commit v7 on v6

--- a/solution.py
+++ b/solution.py
@@ -231,25 +231,28 @@
 
 
 def down_kernel(
-    tops, others, top_list, fine_a_hbm, fine_b_hbm, mid_near, low_near, transfer, down_hbm,
-    out_hbm, out, near, down, own_op, places, sems,
+    tops, others, top_list, fine_a_hbm, fine_b, mid_near, low_near, transfer, down_hbm,
+    out_hbm, out, fine_a, down, own_op, rows, sems,
 ):
     copies = [
         pltpu.make_async_copy(down_hbm.at[level], down.at[level], sems.at[level])
         for level in range(3)
     ]
     copies.append(pltpu.make_async_copy(down_hbm.at[3, lax.axis_index("col")], own_op, sems.at[3]))
-    near_copies = [
-        pltpu.make_async_copy(hbm, near.at[half], sems.at[4 + half])
-        for half, hbm in enumerate((fine_a_hbm, fine_b_hbm))
-    ]
-    for copy in [copies[3], copies[2], copies[1], copies[0]] + near_copies:
-        copy.start()
-    fill_places(places, lambda col: (col & 7) * HALF + (col >> 3))
-    wide = jnp.concatenate([tops[...].astype(F32), others[...].astype(F32)], axis=0)
-    gap = jnp.zeros((HALF - wide.shape[0], 256), F32)
-    rows = jnp.concatenate([wide[:, :256], gap, wide[:, 256:], gap], axis=0)
-    dense = jnp.transpose(rows)[:SIZE].astype(BF16)
+    copies.append(pltpu.make_async_copy(fine_a_hbm, fine_a, sems.at[4]))
+    for level in (3, 2, 1, 0, 4):
+        copies[level].start()
+
+    def fill(part, carry):
+        begin = pl.multiple_of(part * HALF, HALF)
+        lanes = pl.ds(pl.multiple_of(part * 256, 256), 256)
+        held = [tops[:, lanes].astype(F32), others[:, lanes].astype(F32)]
+        gap = jnp.zeros((HALF - 2 * tops.shape[0], 256), F32)
+        rows[pl.ds(begin, HALF), :] = jnp.concatenate(held + [gap], axis=0)
+        return carry
+
+    lax.fori_loop(0, 2, fill, 0)
+    dense = jnp.transpose(rows[...])[:SIZE].astype(BF16)
     own_row = lax.axis_index("row")
     place = top_list[...] ^ own_row
     place = place ^ ((place >> 1) & 0b01010)
@@ -280,8 +283,10 @@
         one_real, one_imag = regroup(*terms)
         real.append(one_real)
         imag.append(one_imag)
-    for copy in near_copies:
-        copy.wait()
+    copies[4].wait()
+    row = iota((FINE, FINE), 0)
+    col = iota((FINE, FINE), 1)
+    places = (row == (col & 7) * HALF + (col >> 3)).astype(BF16)
     out_copies = []
     for part, terms in enumerate((real, imag)):
         term = jnp.concatenate(terms, axis=1)
@@ -289,8 +294,9 @@
         low = (term - high.astype(F32)).astype(BF16)
         for half in range(2):
             columns = pl.ds(half * REACH, REACH)
-            place = places[:, columns]
-            out[part, :, columns] = near[half, part] + mm(high, place) + mm(low, place)
+            place = places[:, half * REACH : (half + 1) * REACH]
+            near = fine_b if half else fine_a
+            out[part, :, columns] = near[part] + mm(high, place) + mm(low, place)
             copy = pltpu.make_async_copy(
                 out.at[part, :, columns], out_hbm.at[part, :, columns], sems.at[6 + 2 * part + half]
             )
@@ -385,7 +391,7 @@
         return call(
             functools.partial(fine_kernel, (half, group)),
             [VMEM] * 5 + [HBM] + [VMEM] * len(earlier),
-            [shape(ride.shape, ride.dtype), (off_chip if group else shape)((2, SIZE, REACH), F32)],
+            [shape(ride.shape, ride.dtype), (off_chip, on_chip)[half]((2, SIZE, REACH), F32) if group else shape((2, SIZE, REACH), F32)],
             [
                 pltpu.VMEM((2 * SIZE, 3 * REACH), BF16),
                 pltpu.VMEM((GROUP, SIZE, FINE), BF16),
@@ -401,10 +407,10 @@
     work = {
         1: {"top": load, "a": lambda ride: fine(0, 0, [], ride)},
         2: {"a": lambda ride: fine(0, 1, done["a"], ride)},
-        4: {"b": lambda ride: fine(1, 0, [], ride)},
-        5: {"b": lambda ride: fine(1, 1, done["b"], ride)},
-        6: {"mid": functools.partial(small, mid_kernel, list_mid.T)},
-        7: {"low": functools.partial(small, low_kernel, list_low)},
+        4: {"mid": functools.partial(small, mid_kernel, list_mid.T)},
+        5: {"low": functools.partial(small, low_kernel, list_low)},
+        6: {"b": lambda ride: fine(1, 0, [], ride)},
+        7: {"b": lambda ride: fine(1, 1, done["b"], ride)},
     }
     done = {}
     total = top
@@ -422,20 +428,20 @@
     other = total if other is None else other
     (far,) = call(
         down_kernel,
-        [VMEM] * 3 + [HBM] * 2 + [VMEM] * 3 + [HBM],
+        [VMEM] * 3 + [HBM] + [VMEM] * 4 + [HBM],
         [shape((2, SIZE, FINE), F32)],
         [
             pltpu.VMEM((2, SIZE, FINE), F32),
-            pltpu.VMEM((2, 2, SIZE, REACH), F32),
+            pltpu.VMEM((2, SIZE, REACH), F32),
             pltpu.VMEM((3, OCTANTS) + octant_ops, BF16),
             pltpu.VMEM(octant_ops, BF16),
-            pltpu.VMEM((FINE, FINE), BF16),
+            pltpu.VMEM((128, 256), F32),
             pltpu.SemaphoreType.DMA((10,)),
         ],
         8 << 30,
         place=HBM,
     )(
-        total, other, list_top.T, in_hbm(done["a"][0]), in_hbm(done["b"][0]), *done["mid"], *done["low"],
+        total, other, list_top.T, in_hbm(done["a"][0]), *done["b"], *done["mid"], *done["low"],
         *done["top"],
         downward_ops,
     )

time: 50.4 us -> 50 us (level); the launches traced: 49.4 us -> 49.6 us
  waiting for transfers between devices: 7 us -> 7.95 us
  Pallas kernels: 25.3 us -> 24.5 us
    ppermute x8, waiting for transfers between devices: 4.96 us -> 5.91 us  [swap(): lax.ppermute(x, axis, [(i, i ^ mask) for i in range(lax.axis_size(axis))])]
    pallas_call x4, Pallas kernels: 9.98 us -> 9.28 us  [fine(): call(functools.partial(fine_kernel, (half, group)), [VMEM] * 5 + [HBM] +...]
  transfers between devices with their start and end apart: 10 -> 10, of which waited for: 5 -> 5; matrix products, arithmetic and copies ran while one was open for 0% -> 0% of each run, Pallas kernels for 33% -> 32%
where the time goes in v7:
time: 50 us; the launch traced here: 49.6 us
  Pallas kernels  24.5 us (49%)
  starting transfers between devices  16.7 us (33%)
  waiting for transfers between devices  7.95 us (16%)
    ppermute x8, starting transfers between devices, swap(): lax.ppermute(x, axis, [(i, i ^ mask) for i in range(lax.axis_size(axis))])  12.6 us
    pallas_call x4, Pallas kernels, fine(): call(functools.partial(fine_kernel, (half, group)), [VMEM] * 5 + [HBM] +...  9.28 us
    ppermute x8, waiting for transfers between devices, swap(): lax.ppermute(x, axis, [(i, i ^ mask) for i in range(lax.axis_size(axis))])  5.91 us
    pallas_call x2, Pallas kernels, small(): call(kernel, [VMEM] * 5 + [HBM], [shape(ride.shape, ride.dtype), shape((S...  4.72 us
    pallas_call x1, Pallas kernels, body(): call(down_kernel, [VMEM] * 3 + [HBM] + [VMEM] * 4 + [HBM], [shape((2, SIZ...  4.57 us
    pallas_call x1, Pallas kernels, body(): call(up_kernel, [HBM, HBM, HBM], [shape((2 * SIZE, 384), BF16), shape((2...  4.27 us
    ppermute x1, starting transfers between devices, body(): lax.ppermute(to_left, axes, [(i, (i - 1) % count) for i in range(count)])  3.97 us
    ppermute x1, waiting for transfers between devices, body(): lax.ppermute(to_right, axes, [(i, (i + 1) % count) for i in range(count)])  2.04 us
  transfers between devices with their start and end apart: 10, of which 5 were waited for; matrix products, arithmetic and copies ran while one was open for 0% of the time, Pallas kernels for 32%

profile of v7, /device:TPU:2, one launch (start us, length us, event | category | flops | bytes accessed | tf_op | source)
XLA Modules:
  0.0 49.6 jit_solution(13161629098322794303)
XLA Ops:
  0.0 4.3 %shard_map.91 = (bf16[304,384]{1,0:T(8,128)(2,1)S(1)}, bf16[304,384]{1,0:T(8,128)(2,1)S(1)}, f32[1,512]{1,0:T(1,128)S(1)}) custom-call(bf16[2,152,512]{2,1,0:T(8,128)(2,1)} %check_hbm.1, bf16[2,152,152]{2,1,0:T(8,128)(2,1)} %equiv_hbm.1, bf16[4,8,2,152,152]{4,3,2,1,0:T(8,128)(2,1)} %ops_hbm.7), custom_call_target="tpu_custom_call" | custom-call | flops 4294967296 | bytes 8388608 | tf_op jit(solution)/shard_map/pallas_call | solution.py:354
  4.3 2.0 %collective-permute-start = (f32[1,512]{1,0:T(1,128)S(1)}, f32[1,512]{1,0:T(1,128)S(1)}, u32[]{:S(2)}, u32[]{:S(2)}) collective-permute-start(f32[1,512]{1,0:T(1,128)S(1)} %get-tuple-element.22), channel_id=1, source_target_pairs={{0,1},{1,0},{2,3},{3,2},{4,5},{5,4},{6,7},{7,6},{8,9},{9,8},{10,11... | collective-permute-start | bytes 6152 | tf_op jit(solution)/shard_map/ppermute | solution.py:405
  6.3 0.1 collective-permute-start.1
  6.4 4.0 %collective-permute-start.5 = (bf16[304,384]{1,0:T(8,128)(2,1)S(1)}, bf16[304,384]{1,0:T(8,128)(2,1)S(1)}, u32[]{:S(2)}, u32[]{:S(2)}) collective-permute-start(bf16[304,384]{1,0:T(8,128)(2,1)S(1)} %get-tuple-element.25.first.own.before), channel_id=1, source_target_pairs={{0,255},{1,0},{2,1},{3,2},{4,3},{5,4},{6,5},{7,6},{8,7},{9,8},{10,... | collective-permute-start | bytes 700424 | tf_op jit(solution)/shard_map/ppermute | solution.py:369
  10.4 0.0 collective-permute-done
  10.4 0.0 copy-start
  10.4 1.3 %collective-permute-start.2 = (f32[1,512]{1,0:T(1,128)S(1)}, f32[1,512]{1,0:T(1,128)S(1)}, u32[]{:S(2)}, u32[]{:S(2)}) collective-permute-start(f32[1,512]{1,0:T(1,128)S(1)} %add.9.ride), channel_id=1, source_target_pairs={{0,2},{1,3},{2,0},{3,1},{4,6},{5,7},{6,4},{7,5},{8,10},{9,11},{10,... | collective-permute-start | bytes 6152 | tf_op jit(solution)/shard_map/ppermute | solution.py:405
  11.7 1.7 %shard_map.92 = (f32[1,512]{1,0:T(1,128)S(1)}, bf16[16,2,152,152]{3,2,1,0:T(8,128)(2,1)S(1)}) custom-call(f32[1,512]{1,0:T(1,128)S(1)} %add.9.ride, bf16[4,16,2,152,152]{4,3,2,1,0:T(8,128)(2,1)} %ops_hbm.13), custom_call_target="tpu_custom_call" | custom-call | flops 8589934592 | bytes 8388608 | tf_op jit(solution)/shard_map/pallas_call | solution.py:372
  13.4 2.0 %collective-permute-done.1.before.from_left = bf16[304,384]{1,0:T(8,128)(2,1)S(1)} collective-permute-done((bf16[304,384]{1,0:T(8,128)(2,1)S(1)}, bf16[304,384]{1,0:T(8,128)(2,1)S(1)}, u32[]{:S(2)}, u32[]{:S(2)}) %collective-permute-start.1) | collective-permute-done | bytes 233504 | tf_op jit(solution)/shard_map/ppermute | solution.py:368
  15.4 0.0 copy-done
  15.4 2.1 %shard_map.93 = (f32[1,512]{1,0:T(1,128)S(1)}, f32[2,152,256]{2,1,0:T(8,128)S(1)}) custom-call(f32[1,512]{1,0:T(1,128)S(1)} %get-tuple-element.23.ride, bf16[304,384]{1,0:T(8,128)(2,1)S(1)} %collective-permute-done.1.before.from_left, bf16[304,384]{1,0:T(8,128)(2,1)S(1)} %get-tuple-element.25.first.own.before, ...), custom_call_target="tpu_custom_call" | custom-call | flops 4294967296 | bytes 8388608 | tf_op jit(solution)/shard_map/pallas_call | solution.py:391
  17.6 0.0 collective-permute-done.2
  17.6 3.5 %collective-permute-start.3 = (f32[1,512]{1,0:T(1,128)S(1)}, f32[1,512]{1,0:T(1,128)S(1)}, u32[]{:S(2)}, u32[]{:S(2)}) collective-permute-start(f32[1,512]{1,0:T(1,128)S(1)} %add.10.ride), channel_id=1, source_target_pairs={{0,6},{1,7},{2,4},{3,5},{4,2},{5,3},{6,0},{7,1},{8,14},{9,15},{10,... | collective-permute-start | bytes 6152 | tf_op jit(solution)/shard_map/ppermute | solution.py:405
  21.1 0.0 copy-start.1
  21.1 2.9 %shard_map.94 = (f32[1,512]{1,0:T(1,128)S(1)}, f32[2,152,256]{2,1,0:T(8,128)}) custom-call(f32[1,512]{1,0:T(1,128)S(1)} %add.10.ride, bf16[304,384]{1,0:T(8,128)(2,1)S(1)} %collective-permute-done.1.before.from_left, bf16[304,384]{1,0:T(8,128)(2,1)S(1)} %get-tuple-element.25.first.own.before, bf16[304,384]{1,0:T(8,128)(2,1)S(1)} %get-tuple-element.24.second.first, ...), custom_call_target="tpu_custom_call" | custom-call | flops 4294967296 | bytes 8388608 | tf_op jit(solution)/shard_map/pallas_call | solution.py:391
  24.0 0.0 collective-permute-done.3
  24.0 0.1 collective-permute-start.4
  24.1 1.1 %collective-permute-done.4 = bf16[1,512]{1,0:T(2,128)(2,1)S(1)} collective-permute-done((bf16[1,512]{1,0:T(2,128)(2,1)S(1)}, bf16[1,512]{1,0:T(2,128)(2,1)S(1)}, u32[]{:S(2)}, u32[]{:S(2)}) %collective-permute-start.4) | collective-permute-done | bytes 1056 | tf_op jit(solution)/shard_map/ppermute | solution.py:405
  25.3 4.6 %collective-permute-start.6 = (bf16[2,512]{1,0:T(2,128)(2,1)S(1)}, bf16[2,512]{1,0:T(2,128)(2,1)S(1)}, u32[]{:S(2)}, u32[]{:S(2)}) collective-permute-start(bf16[2,512]{1,0:T(2,128)(2,1)S(1)} %pad_maximum_fusion.2.ride), channel_id=1, source_target_pairs={{0,16},{8,24},{16,0},{24,8},{32,48},{40,56},{48,32},{56,40},{64,80... | collective-permute-start | bytes 6152 | tf_op jit(solution)/shard_map/ppermute | solution.py:405
  29.9 0.0 collective-permute-done.5.from_right.second
  29.9 0.0 copy-done.1
  29.9 0.0 copy-start.3
  29.9 2.3 %shard_map.95 = (bf16[2,512]{1,0:T(2,128)(2,1)S(1)}, f32[152,128]{1,0:T(8,128)S(1)}) custom-call(bf16[2,512]{1,0:T(2,128)(2,1)S(1)} %pad_maximum_fusion.2.ride, bf16[304,384]{1,0:T(8,128)(2,1)S(1)} %collective-permute-done.1.before.from_left, bf16[304,384]{1,0:T(8,128)(2,1)S(1)} %collective-permute-done.5.from_right.second, ...), custom_call_target="tpu_custom_call" | custom-call | flops 3221225472 | bytes 8388608 | tf_op jit(solution)/shard_map/pallas_call | solution.py:381
  32.3 0.0 collective-permute-done.6
  32.3 0.3 collective-permute-start.7
  32.6 0.0 copy-done.3
  32.6 2.4 %shard_map.96 = (bf16[4,512]{1,0:T(4,128)(2,1)S(1)}, f32[152,128]{1,0:T(8,128)S(1)}) custom-call(bf16[4,512]{1,0:T(4,128)(2,1)S(1)} %pad_maximum_fusion.1.ride, bf16[304,384]{1,0:T(8,128)(2,1)S(1)} %collective-permute-done.1.before.from_left, bf16[304,384]{1,0:T(8,128)(2,1)S(1)} %collective-permute-done.5.from_right.second, ...), custom_call_target="tpu_custom_call" | custom-call | flops 3221225472 | bytes 8388608 | tf_op jit(solution)/shard_map/pallas_call | solution.py:381
  34.9 1.2 %collective-permute-done.7 = bf16[4,512]{1,0:T(4,128)(2,1)S(1)} collective-permute-done((bf16[4,512]{1,0:T(4,128)(2,1)S(1)}, bf16[4,512]{1,0:T(4,128)(2,1)S(1)}, u32[]{:S(2)}, u32[]{:S(2)}) %collective-permute-start.7) | collective-permute-done | bytes 4128 | tf_op jit(solution)/shard_map/ppermute | solution.py:405
  36.2 0.1 collective-permute-start.8
  36.3 2.1 %shard_map.97 = (bf16[8,512]{1,0:T(8,128)(2,1)S(1)}, f32[2,152,256]{2,1,0:T(8,128)S(1)}) custom-call(bf16[8,512]{1,0:T(8,128)(2,1)S(1)} %pad_maximum_fusion.ride, bf16[304,384]{1,0:T(8,128)(2,1)S(1)} %get-tuple-element.25.first.own.before, bf16[304,384]{1,0:T(8,128)(2,1)S(1)} %get-tuple-element.24.second.first, ...), custom_call_target="tpu_custom_call" | custom-call | flops 4294967296 | bytes 8388608 | tf_op jit(solution)/shard_map/pallas_call | solution.py:391
  38.4 1.5 %collective-permute-done.8 = bf16[8,512]{1,0:T(8,128)(2,1)S(1)} collective-permute-done((bf16[8,512]{1,0:T(8,128)(2,1)S(1)}, bf16[8,512]{1,0:T(8,128)(2,1)S(1)}, u32[]{:S(2)}, u32[]{:S(2)}) %collective-permute-start.8) | collective-permute-done | bytes 8224 | tf_op jit(solution)/shard_map/ppermute | solution.py:405
  39.9 0.7 %collective-permute-start.9 = (bf16[16,512]{1,0:T(8,128)(2,1)S(1)}, bf16[16,512]{1,0:T(8,128)(2,1)S(1)}, u32[]{:S(2)}, u32[]{:S(2)}) collective-permute-start(bf16[16,512]{1,0:T(8,128)(2,1)S(1)} %constant_dynamic-update-slice_fusion.ride), channel_id=1, source_target_pairs={{0,192},{8,200},{16,208},{24,216},{32,224},{40,232},{48,240},{56,2... | collective-permute-start | bytes 49160 | tf_op jit(solution)/shard_map/ppermute | solution.py:405
  40.6 0.0 copy-start.2
  40.6 2.1 %shard_map.98 = (bf16[16,512]{1,0:T(8,128)(2,1)S(1)}, f32[2,152,256]{2,1,0:T(8,128)S(1)}) custom-call(bf16[16,512]{1,0:T(8,128)(2,1)S(1)} %constant_dynamic-update-slice_fusion.ride, bf16[304,384]{1,0:T(8,128)(2,1)S(1)} %get-tuple-element.25.first.own.before, bf16[304,384]{1,0:T(8,128)(2,1)S(1)} %get-tuple-element.24.second.first, ...), custom_call_target="tpu_custom_call" | custom-call | flops 4294967296 | bytes 8388608 | tf_op jit(solution)/shard_map/pallas_call | solution.py:391
  42.8 2.1 %collective-permute-done.9.others = bf16[16,512]{1,0:T(8,128)(2,1)S(1)} collective-permute-done((bf16[16,512]{1,0:T(8,128)(2,1)S(1)}, bf16[16,512]{1,0:T(8,128)(2,1)S(1)}, u32[]{:S(2)}, u32[]{:S(2)}) %collective-permute-start.9) | collective-permute-done | bytes 16416 | tf_op jit(solution)/shard_map/ppermute | solution.py:405
  44.9 0.0 copy-done.2
  44.9 4.6 %shard_map.99 = f32[2,152,512]{2,1,0:T(8,128)} custom-call(bf16[16,512]{1,0:T(8,128)(2,1)S(1)} %get-tuple-element.33.tops, bf16[16,512]{1,0:T(8,128)(2,1)S(1)} %collective-permute-done.9.others, s32[16,32]{1,0:T(8,128)S(1)} %bitcast.8, f32[2,152,256]{2,1,0:T(8,128)} %get-tuple-element.34.fine_a_hbm, f32[2,152,256]{2,1,0:T(8,128)S(1)} %get-tuple-element.35.fine_b, ...), custom_call_target="tpu_custom_call" | custom-call | flops 8589934592 | bytes 8388608 | tf_op jit(solution)/shard_map/pallas_call | solution.py:429
  (8 shorter events, 0.1 us)
Async XLA Ops:
  4.3 6.1 %collective-permute-start = (f32[1,512]{1,0:T(1,128)S(1)}, f32[1,512]{1,0:T(1,128)S(1)}, u32[]{:S(2)}, u32[]{:S(2)}) collective-permute-start(f32[1,512]{1,0:T(1,128)S(1)} %get-tuple-element.22), channel_id=1, source_target_pairs={{0,1},{1,0},{2,3},{3,2},{4,5},{5,4},{6,7},{7,6},{8,9},{9,8},{10,11... | collective-permute-start | bytes 6152 | tf_op jit(solution)/shard_map/ppermute | solution.py:405
  6.3 9.1 %collective-permute-start.1 = (bf16[304,384]{1,0:T(8,128)(2,1)S(1)}, bf16[304,384]{1,0:T(8,128)(2,1)S(1)}, u32[]{:S(2)}, u32[]{:S(2)}) collective-permute-start(bf16[304,384]{1,0:T(8,128)(2,1)S(1)} %get-tuple-element.24.second.first), channel_id=1, source_target_pairs={{0,1},{1,2},{2,3},{3,4},{4,5},{5,6},{6,7},{7,8},{8,9},{9,10},{10,1... | collective-permute-start | bytes 700424 | tf_op jit(solution)/shard_map/ppermute | solution.py:368
  6.4 23.5 %collective-permute-start.5 = (bf16[304,384]{1,0:T(8,128)(2,1)S(1)}, bf16[304,384]{1,0:T(8,128)(2,1)S(1)}, u32[]{:S(2)}, u32[]{:S(2)}) collective-permute-start(bf16[304,384]{1,0:T(8,128)(2,1)S(1)} %get-tuple-element.25.first.own.before), channel_id=1, source_target_pairs={{0,255},{1,0},{2,1},{3,2},{4,3},{5,4},{6,5},{7,6},{8,7},{9,8},{10,... | collective-permute-start | bytes 700424 | tf_op jit(solution)/shard_map/ppermute | solution.py:369
  10.4 5.1 %copy-start = (s32[512,16]{0,1:T(8,128)S(1)}, s32[512,16]{0,1:T(8,128)}, u32[]{:S(2)}) copy-start(s32[512,16]{0,1:T(8,128)} %param.14) | copy-start | bytes 98308
  10.4 7.2 %collective-permute-start.2 = (f32[1,512]{1,0:T(1,128)S(1)}, f32[1,512]{1,0:T(1,128)S(1)}, u32[]{:S(2)}, u32[]{:S(2)}) collective-permute-start(f32[1,512]{1,0:T(1,128)S(1)} %add.9.ride), channel_id=1, source_target_pairs={{0,2},{1,3},{2,0},{3,1},{4,6},{5,7},{6,4},{7,5},{8,10},{9,11},{10,... | collective-permute-start | bytes 6152 | tf_op jit(solution)/shard_map/ppermute | solution.py:405
  17.6 6.4 %collective-permute-start.3 = (f32[1,512]{1,0:T(1,128)S(1)}, f32[1,512]{1,0:T(1,128)S(1)}, u32[]{:S(2)}, u32[]{:S(2)}) collective-permute-start(f32[1,512]{1,0:T(1,128)S(1)} %add.10.ride), channel_id=1, source_target_pairs={{0,6},{1,7},{2,4},{3,5},{4,2},{5,3},{6,0},{7,1},{8,14},{9,15},{10,... | collective-permute-start | bytes 6152 | tf_op jit(solution)/shard_map/ppermute | solution.py:405
  21.1 8.8 %copy-start.1 = (s32[64,16]{0,1:T(8,128)S(1)}, s32[64,16]{0,1:T(8,128)}, u32[]{:S(2)}) copy-start(s32[64,16]{0,1:T(8,128)} %param.15) | copy-start | bytes 12292
  24.0 1.2 %collective-permute-start.4 = (bf16[1,512]{1,0:T(2,128)(2,1)S(1)}, bf16[1,512]{1,0:T(2,128)(2,1)S(1)}, u32[]{:S(2)}, u32[]{:S(2)}) collective-permute-start(bf16[1,512]{1,0:T(2,128)(2,1)S(1)} %add_convert_fusion), channel_id=1, source_target_pairs={{0,8},{8,0},{16,24},{24,16},{32,40},{40,32},{48,56},{56,48},{64,72... | collective-permute-start | bytes 3080 | tf_op jit(solution)/shard_map/ppermute | solution.py:405
  25.3 7.0 %collective-permute-start.6 = (bf16[2,512]{1,0:T(2,128)(2,1)S(1)}, bf16[2,512]{1,0:T(2,128)(2,1)S(1)}, u32[]{:S(2)}, u32[]{:S(2)}) collective-permute-start(bf16[2,512]{1,0:T(2,128)(2,1)S(1)} %pad_maximum_fusion.2.ride), channel_id=1, source_target_pairs={{0,16},{8,24},{16,0},{24,8},{32,48},{40,56},{48,32},{56,40},{64,80... | collective-permute-start | bytes 6152 | tf_op jit(solution)/shard_map/ppermute | solution.py:405
  29.9 2.7 %copy-start.3 = (s32[8,16]{1,0:T(8,128)S(1)}, s32[8,16]{1,0:T(8,128)}, u32[]{:S(2)}) copy-start(s32[8,16]{1,0:T(8,128)} %low_list.1) | copy-start | bytes 1540
  32.3 3.9 %collective-permute-start.7 = (bf16[4,512]{1,0:T(4,128)(2,1)S(1)}, bf16[4,512]{1,0:T(4,128)(2,1)S(1)}, u32[]{:S(2)}, u32[]{:S(2)}) collective-permute-start(bf16[4,512]{1,0:T(4,128)(2,1)S(1)} %pad_maximum_fusion.1.ride), channel_id=1, source_target_pairs={{0,48},{8,56},{16,32},{24,40},{32,16},{40,24},{48,0},{56,8},{64,11... | collective-permute-start | bytes 12296 | tf_op jit(solution)/shard_map/ppermute | solution.py:405
  36.2 3.7 %collective-permute-start.8 = (bf16[8,512]{1,0:T(8,128)(2,1)S(1)}, bf16[8,512]{1,0:T(8,128)(2,1)S(1)}, u32[]{:S(2)}, u32[]{:S(2)}) collective-permute-start(bf16[8,512]{1,0:T(8,128)(2,1)S(1)} %pad_maximum_fusion.ride), channel_id=1, source_target_pairs={{0,64},{8,72},{16,80},{24,88},{32,96},{40,104},{48,112},{56,120},{... | collective-permute-start | bytes 24584 | tf_op jit(solution)/shard_map/ppermute | solution.py:405
  39.9 4.9 %collective-permute-start.9 = (bf16[16,512]{1,0:T(8,128)(2,1)S(1)}, bf16[16,512]{1,0:T(8,128)(2,1)S(1)}, u32[]{:S(2)}, u32[]{:S(2)}) collective-permute-start(bf16[16,512]{1,0:T(8,128)(2,1)S(1)} %constant_dynamic-update-slice_fusion.ride), channel_id=1, source_target_pairs={{0,192},{8,200},{16,208},{24,216},{32,224},{40,232},{48,240},{56,2... | collective-permute-start | bytes 49160 | tf_op jit(solution)/shard_map/ppermute | solution.py:405
  40.6 4.2 %copy-start.2 = (s32[32,16]{0,1:T(8,128)S(1)}, s32[32,16]{0,1:T(8,128)}, u32[]{:S(2)}) copy-start(s32[32,16]{0,1:T(8,128)} %param.17) | copy-start | bytes 6148

commit v8 on v7

--- a/solution.py
+++ b/solution.py
@@ -32,7 +32,12 @@
 
 
 def box_order(lane):
-    return (lane & 7) * 8 + ((lane & 63) >> 3)
+    return ((lane & 3) + ((lane & 32) >> 3)) * 8 + ((lane >> 2) & 7)
+
+
+def unpack(halo):
+    rows = halo[2 * SIZE :, :].astype(F32)
+    return jnp.concatenate([rows[:, :128], rows[8:, 128:]], axis=0)
 
 
 def regroup(first, second):
@@ -78,7 +83,7 @@
 
 
 def up_kernel(
-    check_hbm, equiv_hbm, ops_hbm, to_left, to_right, top, check, equiv, ops, own_op, by_octant, sems
+    check_hbm, equiv_hbm, ops_hbm, to_left, to_right, small_out, top, check, equiv, ops, own_op, by_octant, sems
 ):
     first = [
         pltpu.make_async_copy(equiv_hbm, equiv, sems.at[4]),
@@ -100,8 +105,8 @@
     real = by_real[:, :FINE] - by_imag[:, FINE:]
     imag = by_real[:, FINE:] + by_imag[:, :FINE]
     dense = jnp.concatenate([real, imag], axis=0).astype(BF16)
-    to_left[:, :REACH] = dense[:, :REACH]
-    to_right[:, :REACH] = dense[:, REACH:]
+    to_left[: 2 * SIZE, :] = dense[:, :REACH]
+    to_right[: 2 * SIZE, :] = dense[:, REACH:]
     ordered = mm(dense, by_octant[...])
     children = []
     for pair in range(OCTANTS // 2):
@@ -110,7 +115,8 @@
     copies[0].wait()
     packed = [apply_each(ops.at[0], lambda c: children[c], OCTANTS).astype(BF16)]
     lane = iota((SIZE, 128), 1) & 63
-    for level, octant, steps in ((1, lane >> 3, (32, 16, 8)), (2, lane, (4, 2, 1))):
+    places = ((lane >> 2) & 7, (16, 8, 4), (lane & 31) < 4), ((lane & 3) + (lane >> 5) * 4, (32, 2, 1), lane == 0)
+    for level, (octant, steps, held) in enumerate(places, 1):
         copies[level].wait()
         below = packed[level - 1]
         by_real = mm(ops[level, 0, 0], below)
@@ -121,10 +127,15 @@
         dense = combine(by_real, by_imag)
         for step in steps:
             dense = dense + pltpu.roll(dense, 128 - step, 1)
-        packed.append(jnp.where(lane < steps[-1], dense, 0.0).astype(BF16))
-    both = jnp.concatenate([packed[0].astype(F32), packed[1].astype(F32)], axis=0).astype(BF16)
-    to_left[:, REACH:] = both
-    to_right[:, REACH:] = both
+        packed.append(jnp.where(held, dense, 0.0).astype(BF16))
+    mid, low = packed[0].astype(F32), packed[1].astype(F32)
+    small_out[...] = jnp.concatenate([mid, low], axis=0).astype(BF16)
+    to_neighbour = (
+        (to_left, jnp.where(lane < 32, mid, pltpu.roll(low, 32, 1))),
+        (to_right, jnp.where(lane < 32, pltpu.roll(low, 96, 1), mid)),
+    )
+    for halo, columns in to_neighbour:
+        halo[2 * SIZE :, :] = jnp.concatenate([columns[:80], columns[72:]], axis=1).astype(BF16)
     copies[3].wait()
     part = combine(mm(own_op[0], packed[2]), mm(own_op[1], packed[2]))
     flat = jnp.transpose(jnp.concatenate([part, jnp.zeros((104, 128), F32)], axis=0))
@@ -170,12 +181,15 @@
 def low_kernel(ride, from_left, from_right, own, low_list, ops_hbm, ride_out, out, ops, sems):
     copies = start_copies(ops_hbm, 2, ops, sems)
     pass_on(ride, ride_out)
-    lows = [ref[:, REACH:].astype(F32)[SIZE:] for ref in (own, from_left, from_right)]
-    around = (lows[0] + pltpu.roll(lows[1], 8, 1) + pltpu.roll(lows[2], 16, 1)).astype(BF16)
+    lane = iota((SIZE, 128), 1) & 63
+    left = jnp.where(lane < 4, unpack(from_left), 0.0)
+    right = jnp.where((lane >= 32) & (lane < 36), unpack(from_right), 0.0)
+    around = (own[...].astype(F32)[SIZE:] + pltpu.roll(left, 8, 1) + pltpu.roll(right, 8, 1)).astype(BF16)
     row = iota((128, 128), 0)
-    lane = row & 63
-    place = jnp.where(lane < 8, lane, jnp.where(lane < 16, lane - 16, lane - 8))
-    codes = jnp.where(lane < 24, (row >> 6) * 1024 + place, -(1 << 20)).astype(F32)
+    first = (row & 31) < 4
+    place = (row & 3) + jnp.where((row & 32) == 0, jnp.where(first, 0, -4), jnp.where(first, 4, 8))
+    held = first | ((row & 31) >> 2 == 2)
+    codes = jnp.where(held, (row >> 6) * 1024 + place, -(1 << 20)).astype(F32)
     index = (low_list[...] - device_position() * 8).astype(F32)
     listed = jnp.transpose(jnp.concatenate([index, jnp.zeros((8, 112), F32)], axis=1))[:ENTRIES]
     listed = jnp.concatenate([listed, jnp.zeros((ENTRIES, 120), F32)], axis=1).astype(BF16)
@@ -188,10 +202,12 @@
 def mid_kernel(ride, from_left, from_right, own, mid_t, ops_hbm, ride_out, out, ops, sems):
     copies = start_copies(ops_hbm, 1, ops, sems)
     pass_on(ride, ride_out)
-    mids = [ref[:, REACH:].astype(F32)[:SIZE] for ref in (from_left, own, from_right)]
+    mids = [unpack(from_left), own[...].astype(F32)[:SIZE], unpack(from_right)]
     around = jnp.concatenate(mids, axis=1).astype(BF16)
     row = iota((384, 128), 0)
-    codes = ((row >> 6) & 1) * 1024 + box_order(row) + ((row >> 7) - 1) * HALF
+    device = (row >> 7) - 1
+    held = (device == 0) | ((row & 32 == 32) & (device < 0)) | ((row & 32 == 0) & (device > 0))
+    codes = jnp.where(held, ((row >> 6) & 1) * 1024 + box_order(row) + device * HALF, -(1 << 20))
     index = mid_t[...] - device_position() * HALF
     targets = jnp.concatenate([index, index + 1024], axis=1)
     out[...] = translate_packed(around, codes, targets, ops, copies)
@@ -204,9 +220,8 @@
     copy = pltpu.make_async_copy(ops_hbm.at[0, pl.ds(begin, GROUP)], ops, sem)
     copy.start()
     pass_on(ride, ride_out)
-    window[:, :REACH] = before[:, :REACH]
-    window[:, REACH : 2 * REACH] = first[:, :REACH]
-    window[:, 2 * REACH :] = second[:, :REACH]
+    for j, halo in enumerate((before, first, second)):
+        window[:, REACH * j : REACH * (j + 1)] = halo[: 2 * SIZE, :]
     index = fine_t[begin : begin + GROUP, half * REACH : (half + 1) * REACH]
     index = index - (device_position() * FINE + (half - 1) * REACH)
     row = iota((3 * REACH, REACH), 0)
@@ -351,10 +366,15 @@
         in_hbm(x) for x in (check_field, to_equiv, upward_ops, downward_ops, transfer_ops)
     ]
     octant_ops = (2, SIZE, SIZE)
-    to_left, to_right, top = call(
+    to_left, to_right, own_small, top = call(
         up_kernel,
         [HBM, HBM, HBM],
-        [shape((2 * SIZE, 384), BF16), shape((2 * SIZE, 384), BF16), shape((1, 512), F32)],
+        [
+            shape((2 * SIZE + 80, REACH), BF16),
+            shape((2 * SIZE + 80, REACH), BF16),
+            shape((2 * SIZE, 128), BF16),
+            shape((1, 512), F32),
+        ],
         [
             pltpu.VMEM((2, SIZE, FINE), BF16),
             pltpu.VMEM(octant_ops, BF16),
@@ -384,7 +404,7 @@
             [shape(ride.shape, ride.dtype), shape((SIZE, 128), F32)],
             [pltpu.VMEM((ENTRIES,) + octant_ops, BF16), pltpu.SemaphoreType.DMA((2,))],
             3 << 30,
-        )(ride, from_left, from_right, to_left, listed, transfer_ops)
+        )(ride, from_left, from_right, own_small, listed, transfer_ops)
 
     def fine(half, group, earlier, ride):
         around = (from_left, to_left, to_right) if half == 0 else (to_left, to_right, from_right)

time: 50 us -> 49.2 us (0.984)
  waiting for transfers between devices: 7.95 us -> 7.18 us
    ppermute x1, waiting for transfers between devices: 2.04 us -> 1.28 us  [body(): lax.ppermute(to_right, axes, [(i, (i + 1) % count) for i in range(count)])]
where the time goes in v8:
time: 49.2 us; the launch traced here: 48.8 us
  Pallas kernels  24.5 us (50%)
  starting transfers between devices  16.7 us (34%)
  waiting for transfers between devices  7.18 us (15%)
    ppermute x8, starting transfers between devices, swap(): lax.ppermute(x, axis, [(i, i ^ mask) for i in range(lax.axis_size(axis))])  12.6 us
    pallas_call x4, Pallas kernels, fine(): call(functools.partial(fine_kernel, (half, group)), [VMEM] * 5 + [HBM] +...  9.29 us
    ppermute x8, waiting for transfers between devices, swap(): lax.ppermute(x, axis, [(i, i ^ mask) for i in range(lax.axis_size(axis))])  5.9 us
    pallas_call x2, Pallas kernels, small(): call(kernel, [VMEM] * 5 + [HBM], [shape(ride.shape, ride.dtype), shape((S...  4.68 us
    pallas_call x1, Pallas kernels, body(): call(down_kernel, [VMEM] * 3 + [HBM] + [VMEM] * 4 + [HBM], [shape((2, SIZ...  4.55 us
    pallas_call x1, Pallas kernels, body(): call(up_kernel, [HBM, HBM, HBM], [shape((2 * SIZE + 80, REACH), BF16), sh...  4.28 us
    ppermute x1, starting transfers between devices, body(): lax.ppermute(to_left, axes, [(i, (i - 1) % count) for i in range(count)])  3.98 us
    pallas_call x1, Pallas kernels, load(): call(load_kernel, [VMEM, HBM], [shape(ride.shape, ride.dtype), on_chip((E...  1.71 us
  transfers between devices with their start and end apart: 10, of which 5 were waited for; matrix products, arithmetic and copies ran while one was open for 0% of the time, Pallas kernels for 32%

profile of v8, /device:TPU:2, one launch (start us, length us, event | category | flops | bytes accessed | tf_op | source)
XLA Modules:
  0.0 48.8 jit_solution(13469943505782958673)
XLA Ops:
  0.0 4.3 %shard_map.91 = (bf16[384,256]{1,0:T(8,128)(2,1)S(1)}, bf16[384,256]{1,0:T(8,128)(2,1)S(1)}, bf16[304,128]{1,0:T(8,128)(2,1)S(1)}, f32[1,512]{1,0:T(1,128)S(1)}) custom-call(bf16[2,152,512]{2,1,0:T(8,128)(2,1)} %check_hbm.1, bf16[2,152,152]{2,1,0:T(8,128)(2,1)} %equiv_hbm.1, bf16[4,8,2,152,152]{4,3,2,1,0:T(8,128)(2,1)} %ops_hbm.7), custom_call_target="tpu_custom_call" | custom-call | flops 4294967296 | bytes 8388608 | tf_op jit(solution)/shard_map/pallas_call | solution.py:369
  4.3 2.0 %collective-permute-start = (f32[1,512]{1,0:T(1,128)S(1)}, f32[1,512]{1,0:T(1,128)S(1)}, u32[]{:S(2)}, u32[]{:S(2)}) collective-permute-start(f32[1,512]{1,0:T(1,128)S(1)} %get-tuple-element.23), channel_id=1, source_target_pairs={{0,1},{1,0},{2,3},{3,2},{4,5},{5,4},{6,7},{7,6},{8,9},{9,8},{10,11... | collective-permute-start | bytes 6152 | tf_op jit(solution)/shard_map/ppermute | solution.py:425
  6.3 0.1 collective-permute-start.1
  6.4 4.0 %collective-permute-start.5 = (bf16[384,256]{1,0:T(8,128)(2,1)S(1)}, bf16[384,256]{1,0:T(8,128)(2,1)S(1)}, u32[]{:S(2)}, u32[]{:S(2)}) collective-permute-start(bf16[384,256]{1,0:T(8,128)(2,1)S(1)} %get-tuple-element.26.first.before), channel_id=1, source_target_pairs={{0,255},{1,0},{2,1},{3,2},{4,3},{5,4},{6,5},{7,6},{8,7},{9,8},{10,... | collective-permute-start | bytes 589832 | tf_op jit(solution)/shard_map/ppermute | solution.py:389
  10.4 0.0 collective-permute-done
  10.4 0.0 copy-start
  10.4 1.3 %collective-permute-start.2 = (f32[1,512]{1,0:T(1,128)S(1)}, f32[1,512]{1,0:T(1,128)S(1)}, u32[]{:S(2)}, u32[]{:S(2)}) collective-permute-start(f32[1,512]{1,0:T(1,128)S(1)} %add.9.ride), channel_id=1, source_target_pairs={{0,2},{1,3},{2,0},{3,1},{4,6},{5,7},{6,4},{7,5},{8,10},{9,11},{10,... | collective-permute-start | bytes 6152 | tf_op jit(solution)/shard_map/ppermute | solution.py:425
  11.7 1.7 %shard_map.92 = (f32[1,512]{1,0:T(1,128)S(1)}, bf16[16,2,152,152]{3,2,1,0:T(8,128)(2,1)S(1)}) custom-call(f32[1,512]{1,0:T(1,128)S(1)} %add.9.ride, bf16[4,16,2,152,152]{4,3,2,1,0:T(8,128)(2,1)} %ops_hbm.13), custom_call_target="tpu_custom_call" | custom-call | flops 8589934592 | bytes 8388608 | tf_op jit(solution)/shard_map/pallas_call | solution.py:392
  13.4 1.3 %collective-permute-done.1.before.from_left = bf16[384,256]{1,0:T(8,128)(2,1)S(1)} collective-permute-done((bf16[384,256]{1,0:T(8,128)(2,1)S(1)}, bf16[384,256]{1,0:T(8,128)(2,1)S(1)}, u32[]{:S(2)}, u32[]{:S(2)}) %collective-permute-start.1) | collective-permute-done | bytes 196640 | tf_op jit(solution)/shard_map/ppermute | solution.py:388
  14.7 0.0 copy-done
  14.7 2.1 %shard_map.93 = (f32[1,512]{1,0:T(1,128)S(1)}, f32[2,152,256]{2,1,0:T(8,128)S(1)}) custom-call(f32[1,512]{1,0:T(1,128)S(1)} %get-tuple-element.24.ride, bf16[384,256]{1,0:T(8,128)(2,1)S(1)} %collective-permute-done.1.before.from_left, bf16[384,256]{1,0:T(8,128)(2,1)S(1)} %get-tuple-element.26.first.before, ...), custom_call_target="tpu_custom_call" | custom-call | flops 4294967296 | bytes 8388608 | tf_op jit(solution)/shard_map/pallas_call | solution.py:411
  16.8 0.0 collective-permute-done.2
  16.8 3.6 %collective-permute-start.3 = (f32[1,512]{1,0:T(1,128)S(1)}, f32[1,512]{1,0:T(1,128)S(1)}, u32[]{:S(2)}, u32[]{:S(2)}) collective-permute-start(f32[1,512]{1,0:T(1,128)S(1)} %add.10.ride), channel_id=1, source_target_pairs={{0,6},{1,7},{2,4},{3,5},{4,2},{5,3},{6,0},{7,1},{8,14},{9,15},{10,... | collective-permute-start | bytes 6152 | tf_op jit(solution)/shard_map/ppermute | solution.py:425
  20.5 0.0 copy-start.1
  20.5 2.9 %shard_map.94 = (f32[1,512]{1,0:T(1,128)S(1)}, f32[2,152,256]{2,1,0:T(8,128)}) custom-call(f32[1,512]{1,0:T(1,128)S(1)} %add.10.ride, bf16[384,256]{1,0:T(8,128)(2,1)S(1)} %collective-permute-done.1.before.from_left, bf16[384,256]{1,0:T(8,128)(2,1)S(1)} %get-tuple-element.26.first.before, bf16[384,256]{1,0:T(8,128)(2,1)S(1)} %get-tuple-element.25.second.first, ...), custom_call_target="tpu_custom_call" | custom-call | flops 4294967296 | bytes 8388608 | tf_op jit(solution)/shard_map/pallas_call | solution.py:411
  23.4 0.0 collective-permute-done.3
  23.4 0.1 collective-permute-start.4
  23.5 1.1 %collective-permute-done.4 = bf16[1,512]{1,0:T(2,128)(2,1)S(1)} collective-permute-done((bf16[1,512]{1,0:T(2,128)(2,1)S(1)}, bf16[1,512]{1,0:T(2,128)(2,1)S(1)}, u32[]{:S(2)}, u32[]{:S(2)}) %collective-permute-start.4) | collective-permute-done | bytes 1056 | tf_op jit(solution)/shard_map/ppermute | solution.py:425
  24.6 4.5 %collective-permute-start.6 = (bf16[2,512]{1,0:T(2,128)(2,1)S(1)}, bf16[2,512]{1,0:T(2,128)(2,1)S(1)}, u32[]{:S(2)}, u32[]{:S(2)}) collective-permute-start(bf16[2,512]{1,0:T(2,128)(2,1)S(1)} %pad_maximum_fusion.2.ride), channel_id=1, source_target_pairs={{0,16},{8,24},{16,0},{24,8},{32,48},{40,56},{48,32},{56,40},{64,80... | collective-permute-start | bytes 6152 | tf_op jit(solution)/shard_map/ppermute | solution.py:425
  29.1 0.0 collective-permute-done.5.from_right.second
  29.1 0.0 copy-done.1
  29.1 0.0 copy-start.3
  29.1 2.3 %shard_map.95 = (bf16[2,512]{1,0:T(2,128)(2,1)S(1)}, f32[152,128]{1,0:T(8,128)S(1)}) custom-call(bf16[2,512]{1,0:T(2,128)(2,1)S(1)} %pad_maximum_fusion.2.ride, bf16[384,256]{1,0:T(8,128)(2,1)S(1)} %collective-permute-done.1.before.from_left, bf16[384,256]{1,0:T(8,128)(2,1)S(1)} %collective-permute-done.5.from_right.second, ...), custom_call_target="tpu_custom_call" | custom-call | flops 3221225472 | bytes 8388608 | tf_op jit(solution)/shard_map/pallas_call | solution.py:401
  31.4 0.0 collective-permute-done.6
  31.5 0.3 collective-permute-start.7
  31.8 0.0 copy-done.3
  31.8 2.4 %shard_map.96 = (bf16[4,512]{1,0:T(4,128)(2,1)S(1)}, f32[152,128]{1,0:T(8,128)S(1)}) custom-call(bf16[4,512]{1,0:T(4,128)(2,1)S(1)} %pad_maximum_fusion.1.ride, bf16[384,256]{1,0:T(8,128)(2,1)S(1)} %collective-permute-done.1.before.from_left, bf16[384,256]{1,0:T(8,128)(2,1)S(1)} %collective-permute-done.5.from_right.second, ...), custom_call_target="tpu_custom_call" | custom-call | flops 3221225472 | bytes 8388608 | tf_op jit(solution)/shard_map/pallas_call | solution.py:401
  34.1 1.2 %collective-permute-done.7 = bf16[4,512]{1,0:T(4,128)(2,1)S(1)} collective-permute-done((bf16[4,512]{1,0:T(4,128)(2,1)S(1)}, bf16[4,512]{1,0:T(4,128)(2,1)S(1)}, u32[]{:S(2)}, u32[]{:S(2)}) %collective-permute-start.7) | collective-permute-done | bytes 4128 | tf_op jit(solution)/shard_map/ppermute | solution.py:425
  35.4 0.1 collective-permute-start.8
  35.5 2.1 %shard_map.97 = (bf16[8,512]{1,0:T(8,128)(2,1)S(1)}, f32[2,152,256]{2,1,0:T(8,128)S(1)}) custom-call(bf16[8,512]{1,0:T(8,128)(2,1)S(1)} %pad_maximum_fusion.ride, bf16[384,256]{1,0:T(8,128)(2,1)S(1)} %get-tuple-element.26.first.before, bf16[384,256]{1,0:T(8,128)(2,1)S(1)} %get-tuple-element.25.second.first, ...), custom_call_target="tpu_custom_call" | custom-call | flops 4294967296 | bytes 8388608 | tf_op jit(solution)/shard_map/pallas_call | solution.py:411
  37.6 1.5 %collective-permute-done.8 = bf16[8,512]{1,0:T(8,128)(2,1)S(1)} collective-permute-done((bf16[8,512]{1,0:T(8,128)(2,1)S(1)}, bf16[8,512]{1,0:T(8,128)(2,1)S(1)}, u32[]{:S(2)}, u32[]{:S(2)}) %collective-permute-start.8) | collective-permute-done | bytes 8224 | tf_op jit(solution)/shard_map/ppermute | solution.py:425
  39.1 0.7 %collective-permute-start.9 = (bf16[16,512]{1,0:T(8,128)(2,1)S(1)}, bf16[16,512]{1,0:T(8,128)(2,1)S(1)}, u32[]{:S(2)}, u32[]{:S(2)}) collective-permute-start(bf16[16,512]{1,0:T(8,128)(2,1)S(1)} %constant_dynamic-update-slice_fusion.ride), channel_id=1, source_target_pairs={{0,192},{8,200},{16,208},{24,216},{32,224},{40,232},{48,240},{56,2... | collective-permute-start | bytes 49160 | tf_op jit(solution)/shard_map/ppermute | solution.py:425
  39.8 0.0 copy-start.2
  39.8 2.1 %shard_map.98 = (bf16[16,512]{1,0:T(8,128)(2,1)S(1)}, f32[2,152,256]{2,1,0:T(8,128)S(1)}) custom-call(bf16[16,512]{1,0:T(8,128)(2,1)S(1)} %constant_dynamic-update-slice_fusion.ride, bf16[384,256]{1,0:T(8,128)(2,1)S(1)} %get-tuple-element.26.first.before, bf16[384,256]{1,0:T(8,128)(2,1)S(1)} %get-tuple-element.25.second.first, ...), custom_call_target="tpu_custom_call" | custom-call | flops 4294967296 | bytes 8388608 | tf_op jit(solution)/shard_map/pallas_call | solution.py:411
  42.0 2.0 %collective-permute-done.9.others = bf16[16,512]{1,0:T(8,128)(2,1)S(1)} collective-permute-done((bf16[16,512]{1,0:T(8,128)(2,1)S(1)}, bf16[16,512]{1,0:T(8,128)(2,1)S(1)}, u32[]{:S(2)}, u32[]{:S(2)}) %collective-permute-start.9) | collective-permute-done | bytes 16416 | tf_op jit(solution)/shard_map/ppermute | solution.py:425
  44.1 0.0 copy-done.2
  44.1 4.5 %shard_map.99 = f32[2,152,512]{2,1,0:T(8,128)} custom-call(bf16[16,512]{1,0:T(8,128)(2,1)S(1)} %get-tuple-element.35.tops, bf16[16,512]{1,0:T(8,128)(2,1)S(1)} %collective-permute-done.9.others, s32[16,32]{1,0:T(8,128)S(1)} %bitcast.8, f32[2,152,256]{2,1,0:T(8,128)} %get-tuple-element.36.fine_a_hbm, f32[2,152,256]{2,1,0:T(8,128)S(1)} %get-tuple-element.37.fine_b, ...), custom_call_target="tpu_custom_call" | custom-call | flops 8589934592 | bytes 8388608 | tf_op jit(solution)/shard_map/pallas_call | solution.py:449
  (8 shorter events, 0.1 us)
Async XLA Ops:
  4.3 6.1 %collective-permute-start = (f32[1,512]{1,0:T(1,128)S(1)}, f32[1,512]{1,0:T(1,128)S(1)}, u32[]{:S(2)}, u32[]{:S(2)}) collective-permute-start(f32[1,512]{1,0:T(1,128)S(1)} %get-tuple-element.23), channel_id=1, source_target_pairs={{0,1},{1,0},{2,3},{3,2},{4,5},{5,4},{6,7},{7,6},{8,9},{9,8},{10,11... | collective-permute-start | bytes 6152 | tf_op jit(solution)/shard_map/ppermute | solution.py:425
  6.3 8.4 %collective-permute-start.1 = (bf16[384,256]{1,0:T(8,128)(2,1)S(1)}, bf16[384,256]{1,0:T(8,128)(2,1)S(1)}, u32[]{:S(2)}, u32[]{:S(2)}) collective-permute-start(bf16[384,256]{1,0:T(8,128)(2,1)S(1)} %get-tuple-element.25.second.first), channel_id=1, source_target_pairs={{0,1},{1,2},{2,3},{3,4},{4,5},{5,6},{6,7},{7,8},{8,9},{9,10},{10,1... | collective-permute-start | bytes 589832 | tf_op jit(solution)/shard_map/ppermute | solution.py:388
  6.4 22.7 %collective-permute-start.5 = (bf16[384,256]{1,0:T(8,128)(2,1)S(1)}, bf16[384,256]{1,0:T(8,128)(2,1)S(1)}, u32[]{:S(2)}, u32[]{:S(2)}) collective-permute-start(bf16[384,256]{1,0:T(8,128)(2,1)S(1)} %get-tuple-element.26.first.before), channel_id=1, source_target_pairs={{0,255},{1,0},{2,1},{3,2},{4,3},{5,4},{6,5},{7,6},{8,7},{9,8},{10,... | collective-permute-start | bytes 589832 | tf_op jit(solution)/shard_map/ppermute | solution.py:389
  10.4 4.3 %copy-start = (s32[512,16]{0,1:T(8,128)S(1)}, s32[512,16]{0,1:T(8,128)}, u32[]{:S(2)}) copy-start(s32[512,16]{0,1:T(8,128)} %param.14) | copy-start | bytes 98308
  10.4 6.4 %collective-permute-start.2 = (f32[1,512]{1,0:T(1,128)S(1)}, f32[1,512]{1,0:T(1,128)S(1)}, u32[]{:S(2)}, u32[]{:S(2)}) collective-permute-start(f32[1,512]{1,0:T(1,128)S(1)} %add.9.ride), channel_id=1, source_target_pairs={{0,2},{1,3},{2,0},{3,1},{4,6},{5,7},{6,4},{7,5},{8,10},{9,11},{10,... | collective-permute-start | bytes 6152 | tf_op jit(solution)/shard_map/ppermute | solution.py:425
  16.8 6.5 %collective-permute-start.3 = (f32[1,512]{1,0:T(1,128)S(1)}, f32[1,512]{1,0:T(1,128)S(1)}, u32[]{:S(2)}, u32[]{:S(2)}) collective-permute-start(f32[1,512]{1,0:T(1,128)S(1)} %add.10.ride), channel_id=1, source_target_pairs={{0,6},{1,7},{2,4},{3,5},{4,2},{5,3},{6,0},{7,1},{8,14},{9,15},{10,... | collective-permute-start | bytes 6152 | tf_op jit(solution)/shard_map/ppermute | solution.py:425
  20.5 8.6 %copy-start.1 = (s32[64,16]{0,1:T(8,128)S(1)}, s32[64,16]{0,1:T(8,128)}, u32[]{:S(2)}) copy-start(s32[64,16]{0,1:T(8,128)} %param.15) | copy-start | bytes 12292
  23.4 1.2 %collective-permute-start.4 = (bf16[1,512]{1,0:T(2,128)(2,1)S(1)}, bf16[1,512]{1,0:T(2,128)(2,1)S(1)}, u32[]{:S(2)}, u32[]{:S(2)}) collective-permute-start(bf16[1,512]{1,0:T(2,128)(2,1)S(1)} %add_convert_fusion), channel_id=1, source_target_pairs={{0,8},{8,0},{16,24},{24,16},{32,40},{40,32},{48,56},{56,48},{64,72... | collective-permute-start | bytes 3080 | tf_op jit(solution)/shard_map/ppermute | solution.py:425
  24.6 6.8 %collective-permute-start.6 = (bf16[2,512]{1,0:T(2,128)(2,1)S(1)}, bf16[2,512]{1,0:T(2,128)(2,1)S(1)}, u32[]{:S(2)}, u32[]{:S(2)}) collective-permute-start(bf16[2,512]{1,0:T(2,128)(2,1)S(1)} %pad_maximum_fusion.2.ride), channel_id=1, source_target_pairs={{0,16},{8,24},{16,0},{24,8},{32,48},{40,56},{48,32},{56,40},{64,80... | collective-permute-start | bytes 6152 | tf_op jit(solution)/shard_map/ppermute | solution.py:425
  29.1 2.6 %copy-start.3 = (s32[8,16]{1,0:T(8,128)S(1)}, s32[8,16]{1,0:T(8,128)}, u32[]{:S(2)}) copy-start(s32[8,16]{1,0:T(8,128)} %low_list.1) | copy-start | bytes 1540
  31.5 3.9 %collective-permute-start.7 = (bf16[4,512]{1,0:T(4,128)(2,1)S(1)}, bf16[4,512]{1,0:T(4,128)(2,1)S(1)}, u32[]{:S(2)}, u32[]{:S(2)}) collective-permute-start(bf16[4,512]{1,0:T(4,128)(2,1)S(1)} %pad_maximum_fusion.1.ride), channel_id=1, source_target_pairs={{0,48},{8,56},{16,32},{24,40},{32,16},{40,24},{48,0},{56,8},{64,11... | collective-permute-start | bytes 12296 | tf_op jit(solution)/shard_map/ppermute | solution.py:425
  35.4 3.7 %collective-permute-start.8 = (bf16[8,512]{1,0:T(8,128)(2,1)S(1)}, bf16[8,512]{1,0:T(8,128)(2,1)S(1)}, u32[]{:S(2)}, u32[]{:S(2)}) collective-permute-start(bf16[8,512]{1,0:T(8,128)(2,1)S(1)} %pad_maximum_fusion.ride), channel_id=1, source_target_pairs={{0,64},{8,72},{16,80},{24,88},{32,96},{40,104},{48,112},{56,120},{... | collective-permute-start | bytes 24584 | tf_op jit(solution)/shard_map/ppermute | solution.py:425
  39.1 4.9 %collective-permute-start.9 = (bf16[16,512]{1,0:T(8,128)(2,1)S(1)}, bf16[16,512]{1,0:T(8,128)(2,1)S(1)}, u32[]{:S(2)}, u32[]{:S(2)}) collective-permute-start(bf16[16,512]{1,0:T(8,128)(2,1)S(1)} %constant_dynamic-update-slice_fusion.ride), channel_id=1, source_target_pairs={{0,192},{8,200},{16,208},{24,216},{32,224},{40,232},{48,240},{56,2... | collective-permute-start | bytes 49160 | tf_op jit(solution)/shard_map/ppermute | solution.py:425
  39.8 4.2 %copy-start.2 = (s32[32,16]{0,1:T(8,128)S(1)}, s32[32,16]{0,1:T(8,128)}, u32[]{:S(2)}) copy-start(s32[32,16]{0,1:T(8,128)} %param.17) | copy-start | bytes 6148

commit v9 on v8

--- a/solution.py
+++ b/solution.py
@@ -214,18 +214,17 @@
 
 
 def fine_kernel(part, ride, before, first, second, fine_t, ops_hbm, *refs):
-    half, group = part
+    half, begin, size = part
     earlier, (ride_out, out, window, picked, ops, sem) = refs[:-6], refs[-6:]
-    begin = group * GROUP
-    copy = pltpu.make_async_copy(ops_hbm.at[0, pl.ds(begin, GROUP)], ops, sem)
+    copy = pltpu.make_async_copy(ops_hbm.at[0, pl.ds(begin, size)], ops, sem)
     copy.start()
     pass_on(ride, ride_out)
     for j, halo in enumerate((before, first, second)):
         window[:, REACH * j : REACH * (j + 1)] = halo[: 2 * SIZE, :]
-    index = fine_t[begin : begin + GROUP, half * REACH : (half + 1) * REACH]
+    index = fine_t[begin : begin + size, half * REACH : (half + 1) * REACH]
     index = index - (device_position() * FINE + (half - 1) * REACH)
     row = iota((3 * REACH, REACH), 0)
-    for k in range(GROUP):
+    for k in range(size):
         select = (row == index[k : k + 1, :]).astype(BF16)
         both = mm(window[...], select)
         picked[k, :, :REACH] = both[:SIZE].astype(BF16)
@@ -233,7 +232,7 @@
     copy.wait()
     by_real = jnp.zeros((SIZE, FINE), F32)
     by_imag = jnp.zeros((SIZE, FINE), F32)
-    for k in range(GROUP):
+    for k in range(size):
         by_real += mm(ops[k, 0], picked[k])
         by_imag += mm(ops[k, 1], picked[k])
     real = by_real[:, :REACH] - by_imag[:, REACH:]
@@ -406,31 +405,32 @@
             3 << 30,
         )(ride, from_left, from_right, own_small, listed, transfer_ops)
 
-    def fine(half, group, earlier, ride):
+    def fine(half, begin, size, earlier, ride):
         around = (from_left, to_left, to_right) if half == 0 else (to_left, to_right, from_right)
+        place = off_chip if half == 0 else on_chip if earlier else shape
         return call(
-            functools.partial(fine_kernel, (half, group)),
+            functools.partial(fine_kernel, (half, begin, size)),
             [VMEM] * 5 + [HBM] + [VMEM] * len(earlier),
-            [shape(ride.shape, ride.dtype), (off_chip, on_chip)[half]((2, SIZE, REACH), F32) if group else shape((2, SIZE, REACH), F32)],
+            [shape(ride.shape, ride.dtype), place((2, SIZE, REACH), F32)],
             [
                 pltpu.VMEM((2 * SIZE, 3 * REACH), BF16),
-                pltpu.VMEM((GROUP, SIZE, FINE), BF16),
-                pltpu.VMEM((GROUP,) + octant_ops, BF16),
+                pltpu.VMEM((size, SIZE, FINE), BF16),
+                pltpu.VMEM((size,) + octant_ops, BF16),
                 pltpu.SemaphoreType.DMA(()),
             ],
-            4 << 30,
+            size << 29,
         )(ride, *around, list_fine.T, transfer_ops, *earlier)
 
     def swap(x, axis, mask):
         return lax.ppermute(x, axis, [(i, i ^ mask) for i in range(lax.axis_size(axis))])
 
     work = {
-        1: {"top": load, "a": lambda ride: fine(0, 0, [], ride)},
-        2: {"a": lambda ride: fine(0, 1, done["a"], ride)},
+        1: {"top": load},
+        2: {"a": lambda ride: fine(0, 0, ENTRIES, [], ride)},
         4: {"mid": functools.partial(small, mid_kernel, list_mid.T)},
         5: {"low": functools.partial(small, low_kernel, list_low)},
-        6: {"b": lambda ride: fine(1, 0, [], ride)},
-        7: {"b": lambda ride: fine(1, 1, done["b"], ride)},
+        6: {"b": lambda ride: fine(1, 0, GROUP, [], ride)},
+        7: {"b": lambda ride: fine(1, GROUP, ENTRIES - GROUP, done["b"], ride)},
     }
     done = {}
     total = top

time: 49.2 us -> 47.2 us (0.959)
  waiting for transfers between devices: 7.18 us -> 6.52 us
  Pallas kernels: 24.5 us -> 23.9 us
  starting transfers between devices: 16.7 us -> 16.1 us
    ppermute x1, waiting for transfers between devices: 1.28 us -> 0.01 us  [body(): lax.ppermute(to_right, axes, [(i, (i + 1) % count) for i in range(count)])]
    pallas_call x4 -> x3, Pallas kernels: 9.29 us -> 8.65 us  [fine(): call(functools.partial(fine_kernel, (half, begin, size)), [VMEM] * 5 + [H...]
    ppermute x8, waiting for transfers between devices: 5.9 us -> 6.51 us  [swap(): lax.ppermute(x, axis, [(i, i ^ mask) for i in range(lax.axis_size(axis))])]
    ppermute x8, starting transfers between devices: 12.6 us -> 12 us  [swap(): lax.ppermute(x, axis, [(i, i ^ mask) for i in range(lax.axis_size(axis))])]
where the time goes in v9:
time: 47.2 us; the launch traced here: 46.8 us
  Pallas kernels  23.9 us (51%)
  starting transfers between devices  16.1 us (34%)
  waiting for transfers between devices  6.52 us (14%)
    ppermute x8, starting transfers between devices, swap(): lax.ppermute(x, axis, [(i, i ^ mask) for i in range(lax.axis_size(axis))])  12 us
    pallas_call x3, Pallas kernels, fine(): call(functools.partial(fine_kernel, (half, begin, size)), [VMEM] * 5 + [H...  8.65 us
    ppermute x8, waiting for transfers between devices, swap(): lax.ppermute(x, axis, [(i, i ^ mask) for i in range(lax.axis_size(axis))])  6.51 us
    pallas_call x2, Pallas kernels, small(): call(kernel, [VMEM] * 5 + [HBM], [shape(ride.shape, ride.dtype), shape((S...  4.68 us
    pallas_call x1, Pallas kernels, body(): call(down_kernel, [VMEM] * 3 + [HBM] + [VMEM] * 4 + [HBM], [shape((2, SIZ...  4.55 us
    pallas_call x1, Pallas kernels, body(): call(up_kernel, [HBM, HBM, HBM], [shape((2 * SIZE + 80, REACH), BF16), sh...  4.28 us
    ppermute x1, starting transfers between devices, body(): lax.ppermute(to_left, axes, [(i, (i - 1) % count) for i in range(count)])  3.98 us
    pallas_call x1, Pallas kernels, load(): call(load_kernel, [VMEM, HBM], [shape(ride.shape, ride.dtype), on_chip((E...  1.71 us
  transfers between devices with their start and end apart: 10, of which 5 were waited for; matrix products, arithmetic and copies ran while one was open for 0% of the time, Pallas kernels for 32%

profile of v9, /device:TPU:2, one launch (start us, length us, event | category | flops | bytes accessed | tf_op | source)
XLA Modules:
  0.0 46.8 jit_solution(4063444373307855749)
XLA Ops:
  0.0 4.3 %shard_map.91 = (bf16[384,256]{1,0:T(8,128)(2,1)S(1)}, bf16[384,256]{1,0:T(8,128)(2,1)S(1)}, bf16[304,128]{1,0:T(8,128)(2,1)S(1)}, f32[1,512]{1,0:T(1,128)S(1)}) custom-call(bf16[2,152,512]{2,1,0:T(8,128)(2,1)} %check_hbm.1, bf16[2,152,152]{2,1,0:T(8,128)(2,1)} %equiv_hbm.1, bf16[4,8,2,152,152]{4,3,2,1,0:T(8,128)(2,1)} %ops_hbm.6), custom_call_target="tpu_custom_call" | custom-call | flops 4294967296 | bytes 8388608 | tf_op jit(solution)/shard_map/pallas_call | solution.py:368
  4.3 2.0 %collective-permute-start = (f32[1,512]{1,0:T(1,128)S(1)}, f32[1,512]{1,0:T(1,128)S(1)}, u32[]{:S(2)}, u32[]{:S(2)}) collective-permute-start(f32[1,512]{1,0:T(1,128)S(1)} %get-tuple-element.21), channel_id=1, source_target_pairs={{0,1},{1,0},{2,3},{3,2},{4,5},{5,4},{6,7},{7,6},{8,9},{9,8},{10,11... | collective-permute-start | bytes 6152 | tf_op jit(solution)/shard_map/ppermute | solution.py:425
  6.3 0.1 collective-permute-start.2
  6.4 4.0 %collective-permute-start.5 = (bf16[384,256]{1,0:T(8,128)(2,1)S(1)}, bf16[384,256]{1,0:T(8,128)(2,1)S(1)}, u32[]{:S(2)}, u32[]{:S(2)}) collective-permute-start(bf16[384,256]{1,0:T(8,128)(2,1)S(1)} %get-tuple-element.24.first.before), channel_id=1, source_target_pairs={{0,255},{1,0},{2,1},{3,2},{4,3},{5,4},{6,5},{7,6},{8,7},{9,8},{10,... | collective-permute-start | bytes 589832 | tf_op jit(solution)/shard_map/ppermute | solution.py:388
  10.4 0.0 collective-permute-done
  10.4 0.0 copy-start
  10.4 1.3 %collective-permute-start.1 = (f32[1,512]{1,0:T(1,128)S(1)}, f32[1,512]{1,0:T(1,128)S(1)}, u32[]{:S(2)}, u32[]{:S(2)}) collective-permute-start(f32[1,512]{1,0:T(1,128)S(1)} %add.9.ride), channel_id=1, source_target_pairs={{0,2},{1,3},{2,0},{3,1},{4,6},{5,7},{6,4},{7,5},{8,10},{9,11},{10,... | collective-permute-start | bytes 6152 | tf_op jit(solution)/shard_map/ppermute | solution.py:425
  11.7 1.7 %shard_map.92 = (f32[1,512]{1,0:T(1,128)S(1)}, bf16[16,2,152,152]{3,2,1,0:T(8,128)(2,1)S(1)}) custom-call(f32[1,512]{1,0:T(1,128)S(1)} %add.9.ride, bf16[4,16,2,152,152]{4,3,2,1,0:T(8,128)(2,1)} %ops_hbm.11), custom_call_target="tpu_custom_call" | custom-call | flops 8589934592 | bytes 8388608 | tf_op jit(solution)/shard_map/pallas_call | solution.py:391
  13.4 2.3 %collective-permute-done.1 = f32[1,512]{1,0:T(1,128)S(1)} collective-permute-done((f32[1,512]{1,0:T(1,128)S(1)}, f32[1,512]{1,0:T(1,128)S(1)}, u32[]{:S(2)}, u32[]{:S(2)}) %collective-permute-start.1) | collective-permute-done | bytes 2080 | tf_op jit(solution)/shard_map/ppermute | solution.py:425
  15.7 3.1 %collective-permute-start.3 = (f32[1,512]{1,0:T(1,128)S(1)}, f32[1,512]{1,0:T(1,128)S(1)}, u32[]{:S(2)}, u32[]{:S(2)}) collective-permute-start(f32[1,512]{1,0:T(1,128)S(1)} %add.10.ride), channel_id=1, source_target_pairs={{0,6},{1,7},{2,4},{3,5},{4,2},{5,3},{6,0},{7,1},{8,14},{9,15},{10,... | collective-permute-start | bytes 6152 | tf_op jit(solution)/shard_map/ppermute | solution.py:425
  18.8 0.0 collective-permute-done.2.before.from_left
  18.8 0.0 copy-done
  18.8 0.0 copy-start.1
  18.8 4.4 %shard_map.93 = (f32[1,512]{1,0:T(1,128)S(1)}, f32[2,152,256]{2,1,0:T(8,128)}) custom-call(f32[1,512]{1,0:T(1,128)S(1)} %add.10.ride, bf16[384,256]{1,0:T(8,128)(2,1)S(1)} %collective-permute-done.2.before.from_left, bf16[384,256]{1,0:T(8,128)(2,1)S(1)} %get-tuple-element.24.first.before, bf16[384,256]{1,0:T(8,128)(2,1)S(1)} %get-tuple-element.23.second.first, ...), custom_call_target="tpu_custom_call" | custom-call | flops 8589934592 | bytes 8388608 | tf_op jit(solution)/shard_map/pallas_call | solution.py:411
  23.2 0.0 collective-permute-done.3
  23.2 0.1 collective-permute-start.4
  23.3 1.1 %collective-permute-done.4 = bf16[1,512]{1,0:T(2,128)(2,1)S(1)} collective-permute-done((bf16[1,512]{1,0:T(2,128)(2,1)S(1)}, bf16[1,512]{1,0:T(2,128)(2,1)S(1)}, u32[]{:S(2)}, u32[]{:S(2)}) %collective-permute-start.4) | collective-permute-done | bytes 1056 | tf_op jit(solution)/shard_map/ppermute | solution.py:425
  24.4 2.7 %collective-permute-start.6 = (bf16[2,512]{1,0:T(2,128)(2,1)S(1)}, bf16[2,512]{1,0:T(2,128)(2,1)S(1)}, u32[]{:S(2)}, u32[]{:S(2)}) collective-permute-start(bf16[2,512]{1,0:T(2,128)(2,1)S(1)} %pad_maximum_fusion.2.ride), channel_id=1, source_target_pairs={{0,16},{8,24},{16,0},{24,8},{32,48},{40,56},{48,32},{56,40},{64,80... | collective-permute-start | bytes 6152 | tf_op jit(solution)/shard_map/ppermute | solution.py:425
  27.1 0.0 collective-permute-done.5.from_right.second
  27.1 0.0 copy-done.1
  27.1 0.0 copy-start.3
  27.1 2.3 %shard_map.94 = (bf16[2,512]{1,0:T(2,128)(2,1)S(1)}, f32[152,128]{1,0:T(8,128)S(1)}) custom-call(bf16[2,512]{1,0:T(2,128)(2,1)S(1)} %pad_maximum_fusion.2.ride, bf16[384,256]{1,0:T(8,128)(2,1)S(1)} %collective-permute-done.2.before.from_left, bf16[384,256]{1,0:T(8,128)(2,1)S(1)} %collective-permute-done.5.from_right.second, ...), custom_call_target="tpu_custom_call" | custom-call | flops 3221225472 | bytes 8388608 | tf_op jit(solution)/shard_map/pallas_call | solution.py:400
  29.5 0.0 collective-permute-done.6
  29.5 0.4 collective-permute-start.7
  29.9 0.0 copy-done.3
  29.9 2.3 %shard_map.95 = (bf16[4,512]{1,0:T(4,128)(2,1)S(1)}, f32[152,128]{1,0:T(8,128)S(1)}) custom-call(bf16[4,512]{1,0:T(4,128)(2,1)S(1)} %pad_maximum_fusion.1.ride, bf16[384,256]{1,0:T(8,128)(2,1)S(1)} %collective-permute-done.2.before.from_left, bf16[384,256]{1,0:T(8,128)(2,1)S(1)} %collective-permute-done.5.from_right.second, ...), custom_call_target="tpu_custom_call" | custom-call | flops 3221225472 | bytes 8388608 | tf_op jit(solution)/shard_map/pallas_call | solution.py:400
  32.3 1.1 %collective-permute-done.7 = bf16[4,512]{1,0:T(4,128)(2,1)S(1)} collective-permute-done((bf16[4,512]{1,0:T(4,128)(2,1)S(1)}, bf16[4,512]{1,0:T(4,128)(2,1)S(1)}, u32[]{:S(2)}, u32[]{:S(2)}) %collective-permute-start.7) | collective-permute-done | bytes 4128 | tf_op jit(solution)/shard_map/ppermute | solution.py:425
  33.4 0.5 %collective-permute-start.8 = (bf16[8,512]{1,0:T(8,128)(2,1)S(1)}, bf16[8,512]{1,0:T(8,128)(2,1)S(1)}, u32[]{:S(2)}, u32[]{:S(2)}) collective-permute-start(bf16[8,512]{1,0:T(8,128)(2,1)S(1)} %pad_maximum_fusion.ride), channel_id=1, source_target_pairs={{0,64},{8,72},{16,80},{24,88},{32,96},{40,104},{48,112},{56,120},{... | collective-permute-start | bytes 24584 | tf_op jit(solution)/shard_map/ppermute | solution.py:425
  33.9 2.1 %shard_map.96 = (bf16[8,512]{1,0:T(8,128)(2,1)S(1)}, f32[2,152,256]{2,1,0:T(8,128)S(1)}) custom-call(bf16[8,512]{1,0:T(8,128)(2,1)S(1)} %pad_maximum_fusion.ride, bf16[384,256]{1,0:T(8,128)(2,1)S(1)} %get-tuple-element.24.first.before, bf16[384,256]{1,0:T(8,128)(2,1)S(1)} %get-tuple-element.23.second.first, ...), custom_call_target="tpu_custom_call" | custom-call | flops 4294967296 | bytes 8388608 | tf_op jit(solution)/shard_map/pallas_call | solution.py:411
  36.1 1.1 %collective-permute-done.8 = bf16[8,512]{1,0:T(8,128)(2,1)S(1)} collective-permute-done((bf16[8,512]{1,0:T(8,128)(2,1)S(1)}, bf16[8,512]{1,0:T(8,128)(2,1)S(1)}, u32[]{:S(2)}, u32[]{:S(2)}) %collective-permute-start.8) | collective-permute-done | bytes 8224 | tf_op jit(solution)/shard_map/ppermute | solution.py:425
  37.1 1.9 %collective-permute-start.9 = (bf16[16,512]{1,0:T(8,128)(2,1)S(1)}, bf16[16,512]{1,0:T(8,128)(2,1)S(1)}, u32[]{:S(2)}, u32[]{:S(2)}) collective-permute-start(bf16[16,512]{1,0:T(8,128)(2,1)S(1)} %constant_dynamic-update-slice_fusion.ride), channel_id=1, source_target_pairs={{0,192},{8,200},{16,208},{24,216},{32,224},{40,232},{48,240},{56,2... | collective-permute-start | bytes 49160 | tf_op jit(solution)/shard_map/ppermute | solution.py:425
  39.0 0.0 copy-start.2
  39.0 2.2 %shard_map.97 = (bf16[16,512]{1,0:T(8,128)(2,1)S(1)}, f32[2,152,256]{2,1,0:T(8,128)S(1)}) custom-call(bf16[16,512]{1,0:T(8,128)(2,1)S(1)} %constant_dynamic-update-slice_fusion.ride, bf16[384,256]{1,0:T(8,128)(2,1)S(1)} %get-tuple-element.24.first.before, bf16[384,256]{1,0:T(8,128)(2,1)S(1)} %get-tuple-element.23.second.first, ...), custom_call_target="tpu_custom_call" | custom-call | flops 4294967296 | bytes 8388608 | tf_op jit(solution)/shard_map/pallas_call | solution.py:411
  41.2 0.9 %collective-permute-done.9.others = bf16[16,512]{1,0:T(8,128)(2,1)S(1)} collective-permute-done((bf16[16,512]{1,0:T(8,128)(2,1)S(1)}, bf16[16,512]{1,0:T(8,128)(2,1)S(1)}, u32[]{:S(2)}, u32[]{:S(2)}) %collective-permute-start.9) | collective-permute-done | bytes 16416 | tf_op jit(solution)/shard_map/ppermute | solution.py:425
  42.1 0.0 copy-done.2
  42.1 4.5 %shard_map.98 = f32[2,152,512]{2,1,0:T(8,128)} custom-call(bf16[16,512]{1,0:T(8,128)(2,1)S(1)} %get-tuple-element.31.tops, bf16[16,512]{1,0:T(8,128)(2,1)S(1)} %collective-permute-done.9.others, s32[16,32]{1,0:T(8,128)S(1)} %bitcast.7, f32[2,152,256]{2,1,0:T(8,128)} %get-tuple-element.32.fine_a_hbm, f32[2,152,256]{2,1,0:T(8,128)S(1)} %get-tuple-element.33.fine_b, ...), custom_call_target="tpu_custom_call" | custom-call | flops 8589934592 | bytes 8388608 | tf_op jit(solution)/shard_map/pallas_call | solution.py:449
  (8 shorter events, 0.0 us)
Async XLA Ops:
  4.3 6.1 %collective-permute-start = (f32[1,512]{1,0:T(1,128)S(1)}, f32[1,512]{1,0:T(1,128)S(1)}, u32[]{:S(2)}, u32[]{:S(2)}) collective-permute-start(f32[1,512]{1,0:T(1,128)S(1)} %get-tuple-element.21), channel_id=1, source_target_pairs={{0,1},{1,0},{2,3},{3,2},{4,5},{5,4},{6,7},{7,6},{8,9},{9,8},{10,11... | collective-permute-start | bytes 6152 | tf_op jit(solution)/shard_map/ppermute | solution.py:425
  6.3 12.4 %collective-permute-start.2 = (bf16[384,256]{1,0:T(8,128)(2,1)S(1)}, bf16[384,256]{1,0:T(8,128)(2,1)S(1)}, u32[]{:S(2)}, u32[]{:S(2)}) collective-permute-start(bf16[384,256]{1,0:T(8,128)(2,1)S(1)} %get-tuple-element.23.second.first), channel_id=1, source_target_pairs={{0,1},{1,2},{2,3},{3,4},{4,5},{5,6},{6,7},{7,8},{8,9},{9,10},{10,1... | collective-permute-start | bytes 589832 | tf_op jit(solution)/shard_map/ppermute | solution.py:387
  6.4 20.7 %collective-permute-start.5 = (bf16[384,256]{1,0:T(8,128)(2,1)S(1)}, bf16[384,256]{1,0:T(8,128)(2,1)S(1)}, u32[]{:S(2)}, u32[]{:S(2)}) collective-permute-start(bf16[384,256]{1,0:T(8,128)(2,1)S(1)} %get-tuple-element.24.first.before), channel_id=1, source_target_pairs={{0,255},{1,0},{2,1},{3,2},{4,3},{5,4},{6,5},{7,6},{8,7},{9,8},{10,... | collective-permute-start | bytes 589832 | tf_op jit(solution)/shard_map/ppermute | solution.py:388
  10.4 8.4 %copy-start = (s32[512,16]{0,1:T(8,128)S(1)}, s32[512,16]{0,1:T(8,128)}, u32[]{:S(2)}) copy-start(s32[512,16]{0,1:T(8,128)} %param.14) | copy-start | bytes 98308
  10.4 5.3 %collective-permute-start.1 = (f32[1,512]{1,0:T(1,128)S(1)}, f32[1,512]{1,0:T(1,128)S(1)}, u32[]{:S(2)}, u32[]{:S(2)}) collective-permute-start(f32[1,512]{1,0:T(1,128)S(1)} %add.9.ride), channel_id=1, source_target_pairs={{0,2},{1,3},{2,0},{3,1},{4,6},{5,7},{6,4},{7,5},{8,10},{9,11},{10,... | collective-permute-start | bytes 6152 | tf_op jit(solution)/shard_map/ppermute | solution.py:425
  15.7 7.5 %collective-permute-start.3 = (f32[1,512]{1,0:T(1,128)S(1)}, f32[1,512]{1,0:T(1,128)S(1)}, u32[]{:S(2)}, u32[]{:S(2)}) collective-permute-start(f32[1,512]{1,0:T(1,128)S(1)} %add.10.ride), channel_id=1, source_target_pairs={{0,6},{1,7},{2,4},{3,5},{4,2},{5,3},{6,0},{7,1},{8,14},{9,15},{10,... | collective-permute-start | bytes 6152 | tf_op jit(solution)/shard_map/ppermute | solution.py:425
  18.8 8.4 %copy-start.1 = (s32[64,16]{0,1:T(8,128)S(1)}, s32[64,16]{0,1:T(8,128)}, u32[]{:S(2)}) copy-start(s32[64,16]{0,1:T(8,128)} %param.15) | copy-start | bytes 12292
  23.2 1.2 %collective-permute-start.4 = (bf16[1,512]{1,0:T(2,128)(2,1)S(1)}, bf16[1,512]{1,0:T(2,128)(2,1)S(1)}, u32[]{:S(2)}, u32[]{:S(2)}) collective-permute-start(bf16[1,512]{1,0:T(2,128)(2,1)S(1)} %add_convert_fusion), channel_id=1, source_target_pairs={{0,8},{8,0},{16,24},{24,16},{32,40},{40,32},{48,56},{56,48},{64,72... | collective-permute-start | bytes 3080 | tf_op jit(solution)/shard_map/ppermute | solution.py:425
  24.4 5.0 %collective-permute-start.6 = (bf16[2,512]{1,0:T(2,128)(2,1)S(1)}, bf16[2,512]{1,0:T(2,128)(2,1)S(1)}, u32[]{:S(2)}, u32[]{:S(2)}) collective-permute-start(bf16[2,512]{1,0:T(2,128)(2,1)S(1)} %pad_maximum_fusion.2.ride), channel_id=1, source_target_pairs={{0,16},{8,24},{16,0},{24,8},{32,48},{40,56},{48,32},{56,40},{64,80... | collective-permute-start | bytes 6152 | tf_op jit(solution)/shard_map/ppermute | solution.py:425
  27.1 2.7 %copy-start.3 = (s32[8,16]{1,0:T(8,128)S(1)}, s32[8,16]{1,0:T(8,128)}, u32[]{:S(2)}) copy-start(s32[8,16]{1,0:T(8,128)} %low_list.1) | copy-start | bytes 1540
  29.5 3.9 %collective-permute-start.7 = (bf16[4,512]{1,0:T(4,128)(2,1)S(1)}, bf16[4,512]{1,0:T(4,128)(2,1)S(1)}, u32[]{:S(2)}, u32[]{:S(2)}) collective-permute-start(bf16[4,512]{1,0:T(4,128)(2,1)S(1)} %pad_maximum_fusion.1.ride), channel_id=1, source_target_pairs={{0,48},{8,56},{16,32},{24,40},{32,16},{40,24},{48,0},{56,8},{64,11... | collective-permute-start | bytes 12296 | tf_op jit(solution)/shard_map/ppermute | solution.py:425
  33.4 3.7 %collective-permute-start.8 = (bf16[8,512]{1,0:T(8,128)(2,1)S(1)}, bf16[8,512]{1,0:T(8,128)(2,1)S(1)}, u32[]{:S(2)}, u32[]{:S(2)}) collective-permute-start(bf16[8,512]{1,0:T(8,128)(2,1)S(1)} %pad_maximum_fusion.ride), channel_id=1, source_target_pairs={{0,64},{8,72},{16,80},{24,88},{32,96},{40,104},{48,112},{56,120},{... | collective-permute-start | bytes 24584 | tf_op jit(solution)/shard_map/ppermute | solution.py:425
  37.1 4.9 %collective-permute-start.9 = (bf16[16,512]{1,0:T(8,128)(2,1)S(1)}, bf16[16,512]{1,0:T(8,128)(2,1)S(1)}, u32[]{:S(2)}, u32[]{:S(2)}) collective-permute-start(bf16[16,512]{1,0:T(8,128)(2,1)S(1)} %constant_dynamic-update-slice_fusion.ride), channel_id=1, source_target_pairs={{0,192},{8,200},{16,208},{24,216},{32,224},{40,232},{48,240},{56,2... | collective-permute-start | bytes 49160 | tf_op jit(solution)/shard_map/ppermute | solution.py:425
  39.0 3.1 %copy-start.2 = (s32[32,16]{0,1:T(8,128)S(1)}, s32[32,16]{0,1:T(8,128)}, u32[]{:S(2)}) copy-start(s32[32,16]{0,1:T(8,128)} %param.17) | copy-start | bytes 6148
